TPU v7x, 32 devices: a whole 2x2x4 slice. The times are simulated.
32 devices in a mesh: grp: 1, tm: 16 (over z, y, x), chan: 2 (over core).
Axes of the slice: x: 2, y: 2, z: 4, core: 2. Of those that a mesh axis runs over, the one named last changes fastest.
Arguments:
- signal: float32 [131072, 256], P(('grp', 'tm'), 'chan'), may hold values from -6 to 6
- kernel: float32 [131072, 256], P('tm', 'chan'), may hold values from -0.015625 to 0.015625
- skip_gain: float32 [256], replicated, may hold values from -4 to 4
- gate_input: float32 [131072, 256], P(('grp', 'tm', 'chan')), may hold values from -6 to 6
- tap_weight: float32 [256, 254], replicated, may hold values from -0.03125 to 0.03125
- norm_gain: float32 [256], replicated, may hold values from 0.5 to 2
- up_weight: float32 [256, 1024], replicated, may hold values from -0.375 to 0.375
- up_bias: float32 [1024], replicated, may hold values from -4 to 4
- down_weight: float32 [1024, 256], replicated, may hold values from -0.1875 to 0.1875
Outputs:
- block_output: float32 [131072, 256], P(('grp', 'tm', 'chan'))
All inputs are finite; a program needn't handle non-finite values.
Results may differ from a plain program's by a relative error of at most 0.0003.
Values sent between devices are 32-bit elements; how exact they have to be, the bound alone decides.
No kernel may reach another device: no remote copies, remote signals or barrier semaphores. Data moves between devices by JAX's collectives and lax.ppermute only.
A program may use at most 256 MiB of HBM per device.

v0:
```python
import math

import jax
import jax.numpy as jnp
from jax import lax
from jax.sharding import PartitionSpec as P

WIDTH = 256
N1 = 512
N2 = 512
HEADS = 2
TAPS = 127


HIGHEST = lax.Precision.HIGHEST
EPSILON = 1e-06


def from_behind(value, axis, by):
    length = lax.axis_size(axis)
    pairs = [(i, i + by) for i in range(length) if 0 <= i + by < length]
    return lax.ppermute(value, axis, pairs)


def phase_table(left_ids, right_ids, modulus):
    products = left_ids[:, None] * right_ids[None, :] % modulus
    return products.astype(jnp.float32) * (2.0 * math.pi / modulus)


def slot_frequencies(groups):
    slot_ids = jnp.arange(N1, dtype=jnp.int32)
    half_slots = N1 // (2 * groups)
    owner = slot_ids // (2 * half_slots)
    within = slot_ids % (2 * half_slots)
    lower = owner * half_slots + within % half_slots
    mirrored = jnp.where(lower == 0, N1 // 2, N1 - lower)
    return jnp.where(within < half_slots, lower, mirrored)


def apply_matrix(pattern, matrix, operand):
    return jnp.einsum(pattern, matrix, operand, precision=HIGHEST)


def complex_apply(pattern, cos_table, sin_table, real_in, imag_in):
    first_term = apply_matrix(pattern, cos_table, real_in)
    second_term = apply_matrix(pattern, sin_table, imag_in)
    joint_term = apply_matrix(pattern, cos_table + sin_table, real_in + imag_in)
    return (first_term - second_term, joint_term - first_term - second_term)


def long_filter(signal_rows, kernel_rows, device, groups, enter_rows, cross_slots, back_slots):
    width_here = signal_rows.shape[1]
    half_slots = N1 // (2 * groups)
    frequencies = slot_frequencies(groups)
    columns_here = N2 // groups
    column_ids = device * columns_here + jnp.arange(columns_here, dtype=jnp.int32)
    twiddle = phase_table(frequencies, column_ids, N1 * N2)
    twiddle_cos = jnp.cos(twiddle)[:, :, None]
    twiddle_sin = jnp.sin(twiddle)[:, :, None]
    first_phases = phase_table(frequencies, jnp.arange(N1 // 2, dtype=jnp.int32), N1)
    first_cos = jnp.cos(first_phases)
    first_sin = jnp.sin(first_phases)
    second_phases = phase_table(
        jnp.arange(N2, dtype=jnp.int32), jnp.arange(N2, dtype=jnp.int32), N2
    )
    second_cos = jnp.cos(second_phases)
    second_sin = jnp.sin(second_phases)
    last_phases = phase_table(jnp.arange(N1 // 2, dtype=jnp.int32), frequencies, N1)
    last_cos = jnp.cos(last_phases)
    last_sin = jnp.sin(last_phases)

    def forward_rows(arrays):
        signal_part, kernel_part = arrays
        real_part, imag_part = complex_apply(
            "sn,nqc->sqc", first_cos, -first_sin, signal_part, kernel_part
        )
        turned_real = real_part * twiddle_cos + imag_part * twiddle_sin
        turned_imag = imag_part * twiddle_cos - real_part * twiddle_sin
        return (turned_real, turned_imag)

    def mirror_of(values):
        flipped = values[:, ::-1]
        swapped = jnp.concatenate([flipped[half_slots:], flipped[:half_slots]], axis=0)
        rolled = jnp.roll(flipped, 1, axis=1)
        row_ids = jnp.arange(2 * half_slots, dtype=jnp.int32)[:, None, None]
        leading = device == 0
        return jnp.where(
            leading & (row_ids == 0),
            rolled,
            jnp.where(leading & (row_ids == half_slots), flipped, swapped),
        )

    def finish_rows(arrays):
        real_in, imag_in = arrays
        turned_real = real_in * twiddle_cos - imag_in * twiddle_sin
        turned_imag = real_in * twiddle_sin + imag_in * twiddle_cos
        result = apply_matrix("ns,sqc->nqc", last_cos, turned_real) - apply_matrix(
            "ns,sqc->nqc", last_sin, turned_imag
        )
        return result * (1.0 / (N1 * N2))

    def spectral(arrays):
        real_in, imag_in = arrays
        real_z, imag_z = complex_apply("kn,snc->skc", second_cos, -second_sin, real_in, imag_in)
        partner_real = mirror_of(real_z)
        partner_imag = mirror_of(imag_z)
        signal_real = 0.5 * (real_z + partner_real)
        signal_imag = 0.5 * (imag_z - partner_imag)
        kernel_real = 0.5 * (imag_z + partner_imag)
        kernel_imag = 0.5 * (partner_real - real_z)
        product_real = signal_real * kernel_real - signal_imag * kernel_imag
        product_imag = signal_real * kernel_imag + signal_imag * kernel_real
        inverse_real, inverse_imag = complex_apply(
            "kn,skc->snc", second_cos, second_sin, product_real, product_imag
        )
        return back_slots((inverse_real, inverse_imag), finish_rows)

    shaped_signal = signal_rows.reshape(-1, N2, width_here)
    shaped_kernel = kernel_rows.reshape(-1, N2, width_here)
    halves = enter_rows((shaped_signal, shaped_kernel), forward_rows)
    return cross_slots(halves, spectral)


def on_device(
    signal, kernel, skip_gain, gate_input, tap_weight, norm_gain, up_weight, up_bias, down_weight
):
    device = lax.axis_index("tm")
    groups = lax.axis_size("tm")
    channels_here = signal.shape[1]
    skip_here = lax.dynamic_slice_in_dim(
        skip_gain, lax.axis_index("chan") * channels_here, channels_here
    )
    kernel_rows = kernel.at[0].add(jnp.where(device == 0, skip_here, 0.0))

    def enter_rows(arrays, handler):
        return handler(
            (
                lax.all_to_all(arrays[0], "tm", split_axis=1, concat_axis=0, tiled=True),
                lax.all_to_all(arrays[1], "tm", split_axis=1, concat_axis=0, tiled=True),
            )
        )

    def cross_slots(arrays, handler):
        return handler(
            (
                lax.all_to_all(arrays[0], "tm", split_axis=0, concat_axis=1, tiled=True),
                lax.all_to_all(arrays[1], "tm", split_axis=0, concat_axis=1, tiled=True),
            )
        )

    def back_slots(arrays, handler):
        return handler(
            (
                lax.all_to_all(arrays[0], "tm", split_axis=1, concat_axis=0, tiled=True),
                lax.all_to_all(arrays[1], "tm", split_axis=1, concat_axis=0, tiled=True),
            )
        )

    spectral_out = long_filter(
        signal, kernel_rows, device, groups, enter_rows, cross_slots, back_slots
    )
    convolved = lax.all_to_all(
        lax.all_to_all(spectral_out, "tm", split_axis=0, concat_axis=1, tiled=True),
        "chan",
        split_axis=0,
        concat_axis=2,
        tiled=True,
    )
    gated_rows = gate_input * convolved.reshape(-1, WIDTH)
    row_count = gated_rows.shape[0]
    earlier = from_behind(gated_rows[row_count - (TAPS - 1) :], ("tm", "chan"), 1)
    extended = jnp.concatenate([earlier, gated_rows, jnp.zeros((2, WIDTH), jnp.float32)], axis=0)
    tap_values = jnp.dot(gated_rows, tap_weight, precision=HIGHEST)
    block_rows = min(512, row_count)
    block_count = row_count // block_rows
    band_width = block_rows + TAPS + 1

    def conv_block(offset):
        block_taps = lax.dynamic_slice_in_dim(tap_values, offset, block_rows, 0)
        block_taps = block_taps.reshape(block_rows, HEADS, TAPS)[:, :, ::-1]
        padded = jnp.concatenate(
            [block_taps, jnp.zeros((block_rows, HEADS, block_rows + 2), jnp.float32)], axis=2
        )
        flattened = padded.transpose(1, 0, 2).reshape(HEADS, block_rows * (band_width + 1))
        band_matrix = flattened[:, : block_rows * band_width].reshape(HEADS, block_rows, band_width)
        window = lax.dynamic_slice_in_dim(extended, offset, band_width, 0)
        window = window.reshape(band_width, HEADS, WIDTH // HEADS)
        mixed_rows = jnp.einsum("hts,shc->thc", band_matrix, window, precision=HIGHEST)
        return mixed_rows.reshape(block_rows, WIDTH)

    offsets = jnp.arange(block_count, dtype=jnp.int32) * block_rows
    local_mix = lax.map(conv_block, offsets).reshape(row_count, WIDTH)
    mean_square = jnp.mean(local_mix * local_mix, axis=1, keepdims=True)
    normed = local_mix * lax.rsqrt(mean_square + EPSILON) * norm_gain
    hidden_units = jax.nn.gelu(jnp.dot(normed, up_weight, precision=HIGHEST) + up_bias)
    return local_mix + jnp.dot(hidden_units, down_weight, precision=HIGHEST)


def solution(mesh):
    placed = (
        P(("grp", "tm"), "chan"),
        P("tm", "chan"),
        P(),
        P(("grp", "tm", "chan"), None),
        P(),
        P(),
        P(),
        P(),
        P(),
    )
    return jax.shard_map(
        on_device,
        mesh=mesh,
        in_specs=placed,
        out_specs=P(("grp", "tm", "chan"), None),
        check_vma=False,
    )
```

profile of v0, /device:TPU:11, one launch (start us, length us, event | category | flops | bytes accessed | tf_op | source)
XLA Modules:
  0.0 2154.0 jit_solution(2523852586578889871)
XLA Ops:
  26.5 84.4 %all-to-all-done.1 = f32[16,512,128]{2,0,1:T(8,128)} async-done(((f32[16,512,128]{2,0,1:T(8,128)}), f32[16,512,128]{2,0,1:T(8,128)}, u32[]{:S(2)}, u32[]{:S(2)}) %all-to-all-start.1) | async-done | bytes 4194336 | tf_op jit(solution)/shard_map/all_to_all | solution.py:139
  124.4 12.4 fusion.65
  136.8 70.9 %all-to-all-done = f32[16,512,128]{2,0,1:T(8,128)} async-done(((f32[16,512,128]{2,0,1:T(8,128)}), f32[16,512,128]{2,0,1:T(8,128)}, u32[]{:S(2)}, u32[]{:S(2)}) %all-to-all-start) | async-done | bytes 4194336 | tf_op jit(solution)/shard_map/all_to_all | solution.py:138
  220.5 22.1 %multiply_add_fusion.1 = (f32[512,32,128]{2,0,1:T(8,128)}, f32[512,32,128]{2,0,1:T(8,128)}) fusion(f32[512,32]{0,1:T(8,128)S(1)} %get-tuple-element.87, f32[512,32]{0,1:T(8,128)S(1)} %get-tuple-element.86, f32[512,32,128]{2,0,1:T(8,128)S(1)} %fusion.67, f32[512,32,128]{2,0,1:T(8,128)S(1)} %bitcast.171, f32[256,32,128]{2,0,1:T(8,128)} %bitcast.175, ...), kind=kOutput, calls=%fused_computation.48 | convolution fusion | flops 6464471040 | bytes 42076160 | tf_op jit(solution)/shard_map/sn,nqc->sqc/dot_general | solution.py:41
  242.6 11.5 copy.77
  263.1 11.5 copy.80
  274.7 174.3 %all-to-all-done.2 = f32[512,32,128]{2,1,0:T(8,128)} async-done(((f32[512,32,128]{2,1,0:T(8,128)}), f32[512,32,128]{2,1,0:T(8,128)}, u32[]{:S(2)}, u32[]{:S(2)}) %all-to-all-start.2) | async-done | bytes 8388640 | tf_op jit(solution)/shard_map/all_to_all | solution.py:146
  464.0 37.7 %fusion.48 = f32[32,128,512]{2,1,0:T(8,128)} fusion(f32[32,512,128]{2,1,0:T(8,128)S(1)} %bitcast.165), kind=kOutput, calls=%fused_computation.71 | convolution fusion | flops 12888571904 | bytes 16777216 | tf_op jit(solution)/shard_map/kn,snc->skc/dot_general | solution.py:41
  501.7 135.3 %all-to-all-done.3 = f32[512,32,128]{2,1,0:T(8,128)} async-done(((f32[512,32,128]{2,1,0:T(8,128)}), f32[512,32,128]{2,1,0:T(8,128)}, u32[]{:S(2)}, u32[]{:S(2)}) %all-to-all-start.3) | async-done | bytes 8388640 | tf_op jit(solution)/shard_map/all_to_all | solution.py:147
  643.1 37.8 %bitcast_subtract_fusion.3 = (f32[32,512,128]{1,2,0:T(8,128)}, f32[32,128,512]{2,1,0:T(8,128)}) fusion(f32[32,128,512]{2,1,0:T(8,128)S(1)} %copy-done.4, f32[32,512,128]{2,1,0:T(8,128)S(1)} %bitcast.167), kind=kOutput, calls=%fused_computation.31 | convolution fusion | flops 12890931200 | bytes 33554432 | tf_op jit(solution)/shard_map/kn,snc->skc/dot_general | solution.py:41
  680.9 41.5 %fusion.15 = f32[32,512,128]{1,2,0:T(8,128)} fusion(f32[32,128,512]{2,1,0:T(8,128)} %get-tuple-element.89, f32[32,128,512]{2,1,0:T(8,128)} %fusion.48, f32[32,512,128]{2,1,0:T(8,128)} %bitcast.166, f32[32,512,128]{2,1,0:T(8,128)} %bitcast.168), kind=kOutput, calls=%fused_computation.30 | convolution fusion | flops 12895387648 | bytes 41943040 | tf_op jit(solution)/shard_map/kn,snc->skc/dot_general | solution.py:41
  735.8 67.5 %rev.10 = f32[32,512,128]{1,2,0:T(8,128)} reverse(f32[32,512,128]{1,2,0:T(8,128)} %fusion.15), dimensions={1} | reverse | bytes 16777216 | tf_op jit(solution)/shard_map/rev | solution.py:82
  817.3 67.5 %rev.9 = f32[32,512,128]{1,2,0:T(8,128)} reverse(f32[32,512,128]{1,2,0:T(8,128)} %get-tuple-element.88), dimensions={1} | reverse | bytes 16777216 | tf_op jit(solution)/shard_map/rev | solution.py:82
  888.0 67.7 %reverse.9 = f32[32,512,128]{1,2,0:T(8,128)} reverse(f32[32,512,128]{1,2,0:T(8,128)} %bitcast.178), dimensions={1} | reverse | bytes 16777216
  964.6 34.3 %slice.81 = f32[16,512,128]{1,2,0:T(8,128)} reverse(f32[16,512,128]{1,2,0:T(8,128)} %get-tuple-element.84), dimensions={1} | reverse | bytes 8388608 | tf_op jit(solution)/shard_map/slice | solution.py:83
  998.8 34.2 %slice.83 = f32[16,512,128]{1,2,0:T(8,128)} reverse(f32[16,512,128]{1,2,0:T(8,128)} %get-tuple-element.85), dimensions={1} | reverse | bytes 8388608 | tf_op jit(solution)/shard_map/slice | solution.py:83
  1033.0 34.3 %slice.74 = f32[16,512,128]{1,2,0:T(8,128)} reverse(f32[16,512,128]{1,2,0:T(8,128)} %get-tuple-element.82), dimensions={1} | reverse | bytes 8388608 | tf_op jit(solution)/shard_map/slice | solution.py:83
  1067.4 34.3 %slice.76 = f32[16,512,128]{1,2,0:T(8,128)} reverse(f32[16,512,128]{1,2,0:T(8,128)} %get-tuple-element.83), dimensions={1} | reverse | bytes 8388608 | tf_op jit(solution)/shard_map/slice | solution.py:83
  1101.7 67.6 %reverse.8 = f32[32,512,128]{1,2,0:T(8,128)} reverse(f32[32,512,128]{1,2,0:T(8,128)} %bitcast.177), dimensions={1} | reverse | bytes 16777216
  1178.4 32.9 %multiply_subtract_fusion = (f32[32,512,128]{1,2,0:T(8,128)}, f32[32,512,128]{1,2,0:T(8,128)}, f32[32,512,128]{1,2,0:T(8,128)}) fusion(f32[32,512,128]{1,2,0:T(8,128)} %get-tuple-element.88, f32[32,512,128]{1,2,0:T(8,128)} %fusion.15, f32[32,512,128]{1,2,0:T(8,128)} %rev.10, f32[16,512,128]{1,2,0:T(8,128)} %slice.83, f32[16,512,128]{1,2,0:T(8,128)} %slice.81, ...), kind=kLoop, calls=%fused_computation.40 | loop fusion | flops 39845888 | bytes 92274752 | tf_op jit(solution)/shard_map/sub | solution.py:111
  1211.2 25.4 %fusion.46 = f32[32,128,512]{2,1,0:T(8,128)} fusion(f32[32,512,128]{1,2,0:T(8,128)} %get-tuple-element.75), kind=kOutput, calls=%fused_computation.69 | convolution fusion | flops 12888571904 | bytes 16777216 | tf_op jit(solution)/shard_map/kn,skc->snc/dot_general | solution.py:41
  1236.6 13.3 multiply_add_fusion
  1250.0 26.8 %bitcast_subtract_fusion.1 = (f32[32,512,128]{1,2,0:T(8,128)}, f32[32,128,512]{2,1,0:T(8,128)}) fusion(f32[32,128,512]{2,1,0:T(8,128)} %fusion.46, f32[32,512,128]{1,2,0:T(8,128)S(1)} %multiply_add_fusion), kind=kOutput, calls=%fused_computation.28 | convolution fusion | flops 12890669056 | bytes 33554432 | tf_op jit(solution)/shard_map/kn,skc->snc/dot_general | solution.py:41
  1276.8 28.7 %fusion.14 = f32[32,512,128]{1,2,0:T(8,128)} fusion(f32[32,128,512]{2,1,0:T(8,128)} %get-tuple-element.91, f32[32,128,512]{2,1,0:T(8,128)} %fusion.46, f32[32,512,128]{1,2,0:T(8,128)} %get-tuple-element.75, f32[32,512,128]{1,2,0:T(8,128)} %copy-done.3), kind=kOutput, calls=%fused_computation.25 | convolution fusion | flops 12895125504 | bytes 41943040 | tf_op jit(solution)/shard_map/kn,skc->snc/dot_general | solution.py:41
  1305.4 10.3 copy.87
  1335.4 174.0 %all-to-all-done.5 = f32[32,512,128]{2,0,1:T(8,128)} async-done(((f32[32,512,128]{2,0,1:T(8,128)}), f32[32,512,128]{2,0,1:T(8,128)}, u32[]{:S(2)}, u32[]{:S(2)}) %all-to-all-start.5) | async-done | bytes 8388640 | tf_op jit(solution)/shard_map/all_to_all | solution.py:155
  1524.9 171.2 %all-to-all-done.4 = f32[32,512,128]{2,0,1:T(8,128)} async-done(((f32[32,512,128]{2,0,1:T(8,128)}), f32[32,512,128]{2,0,1:T(8,128)}, u32[]{:S(2)}, u32[]{:S(2)}) %all-to-all-start.4) | async-done | bytes 8388640 | tf_op jit(solution)/shard_map/all_to_all | solution.py:154
  1751.0 82.4 %all-to-all-done.6 = f32[256,32,128]{2,1,0:T(8,128)} async-done(((f32[256,32,128]{2,1,0:T(8,128)}), f32[256,32,128]{2,1,0:T(8,128)}, u32[]{:S(2)}, u32[]{:S(2)}) %all-to-all-start.6) | async-done | bytes 4194336 | tf_op jit(solution)/shard_map/all_to_all | solution.py:163
  1836.3 10.8 all_to_all.141
  1878.6 229.4 %while.11 = (s32[]{:T(128)}, f32[8,512,256]{1,2,0:T(8,128)}, s32[8]{0:T(128)S(1)}, f32[4224,256]{0,1:T(8,128)}, f32[4096,254]{0,1:T(8,128)}, /*index=5*/s32[]{:T(128)}, s32[]{:T(128)}, s32[]{:T(128)}, s32[]{:T(128)}) while((s32[]{:T(128)}, f32[8,512,256]{1,2,0:T(8,128)}, s32[8]{0:T(128)S(1)}, f32[4224,256]{0,1:T(8,128)}, ...), condition=%wide.region_1.2_spmd, body=%wide.region_0.1_spmd.sunk | while | flops 1006632960 | bytes 28172972 | solution.py:192
  2119.0 15.0 fusion.165
  2134.0 19.7 fusion.25
  (201 shorter events, 470.6 us)
Async XLA Ops:
  0.0 2119.0 %copy-start = (f32[256,1024]{1,0:T(8,128)S(1)}, f32[256,1024]{1,0:T(8,128)}, u32[]{:S(2)}) copy-start(f32[256,1024]{1,0:T(8,128)} %param.19) | copy-start | bytes 3145732
  13.3 97.7 %all-to-all-start.1 = ((f32[16,512,128]{2,0,1:T(8,128)}), f32[16,512,128]{2,0,1:T(8,128)}, u32[]{:S(2)}, u32[]{:S(2)}) async-start(f32[16,512,128]{2,0,1:T(8,128)} %copy.74), calls=%async_computation.1 | async-start | bytes 8388608 | tf_op jit(solution)/shard_map/all_to_all | solution.py:139
  110.9 96.8 %all-to-all-start = ((f32[16,512,128]{2,0,1:T(8,128)}), f32[16,512,128]{2,0,1:T(8,128)}, u32[]{:S(2)}, u32[]{:S(2)}) async-start(f32[16,512,128]{2,0,1:T(8,128)} %copy.71), calls=%async_computation | async-start | bytes 8388608 | tf_op jit(solution)/shard_map/all_to_all | solution.py:138
  119.3 101.1 %copy-start.18 = (s32[512]{0:T(512)}, s32[512]{0:T(512)S(1)}, u32[]{:S(2)}) copy-start(s32[512]{0:T(512)S(1)} %select_select_fusion) | copy-start | bytes 6148
  119.6 100.8 %copy-start.13 = (f32[512,32]{0,1:T(8,128)}, f32[512,32]{0,1:T(8,128)S(1)}, u32[]{:S(2)}) copy-start(f32[512,32]{0,1:T(8,128)S(1)} %get-tuple-element.86) | copy-start | bytes 196612
  119.7 100.8 %copy-start.15 = (f32[512,32]{0,1:T(8,128)}, f32[512,32]{0,1:T(8,128)S(1)}, u32[]{:S(2)}) copy-start(f32[512,32]{0,1:T(8,128)S(1)} %get-tuple-element.87) | copy-start | bytes 196612
  207.7 12.7 slice-start.3
  210.6 9.7 copy-start.8
  210.6 9.8 slice-start.4
  210.7 9.8 copy-start.7
  254.1 194.9 %all-to-all-start.2 = ((f32[512,32,128]{2,1,0:T(8,128)}), f32[512,32,128]{2,1,0:T(8,128)}, u32[]{:S(2)}, u32[]{:S(2)}) async-start(f32[512,32,128]{2,1,0:T(8,128)} %copy.77), calls=%async_computation.2 | async-start | bytes 16777216 | tf_op jit(solution)/shard_map/all_to_all | solution.py:146
  449.0 188.0 %all-to-all-start.3 = ((f32[512,32,128]{2,1,0:T(8,128)}), f32[512,32,128]{2,1,0:T(8,128)}, u32[]{:S(2)}, u32[]{:S(2)}) async-start(f32[512,32,128]{2,1,0:T(8,128)} %copy.80), calls=%async_computation.3 | async-start | bytes 16777216 | tf_op jit(solution)/shard_map/all_to_all | solution.py:147
  641.6 39.3 %copy-start.5 = (f32[32,16,32,128]{3,2,1,0:T(8,128)}, f32[32,16,32,128]{3,2,1,0:T(8,128)S(1)}, u32[]{:S(2)}) copy-start(f32[32,16,32,128]{3,2,1,0:T(8,128)S(1)} %copy.81) | copy-start | bytes 25165828
  722.4 9.1 copy-start.1
  803.4 8.5 slice-start
  803.4 8.5 slice-start.1
  1169.3 9.0 slice-start.2
  1250.0 26.8 %copy-start.3 = (f32[32,512,128]{1,2,0:T(8,128)}, f32[32,512,128]{1,2,0:T(8,128)S(1)}, u32[]{:S(2)}) copy-start(f32[32,512,128]{1,2,0:T(8,128)S(1)} %multiply_add_fusion) | copy-start | bytes 25165828
  1315.8 193.7 %all-to-all-start.5 = ((f32[32,512,128]{2,0,1:T(8,128)}), f32[32,512,128]{2,0,1:T(8,128)}, u32[]{:S(2)}, u32[]{:S(2)}) async-start(f32[32,512,128]{2,0,1:T(8,128)} %copy.87), calls=%async_computation.5 | async-start | bytes 16777216 | tf_op jit(solution)/shard_map/all_to_all | solution.py:155
  1509.4 186.6 %all-to-all-start.4 = ((f32[32,512,128]{2,0,1:T(8,128)}), f32[32,512,128]{2,0,1:T(8,128)}, u32[]{:S(2)}, u32[]{:S(2)}) async-start(f32[32,512,128]{2,0,1:T(8,128)} %copy.84), calls=%async_computation.4 | async-start | bytes 16777216 | tf_op jit(solution)/shard_map/all_to_all | solution.py:154
  1696.1 8.3 copy-start.10
  1696.1 8.3 copy-start.14
  1696.1 8.3 copy-start.16
  1704.4 7.2 copy-start.19
  1735.7 97.8 %all-to-all-start.6 = ((f32[256,32,128]{2,1,0:T(8,128)}), f32[256,32,128]{2,1,0:T(8,128)}, u32[]{:S(2)}, u32[]{:S(2)}) async-start(f32[256,32,128]{2,1,0:T(8,128)} %copy.90), calls=%async_computation.6 | async-start | bytes 8388608 | tf_op jit(solution)/shard_map/all_to_all | solution.py:163
  1858.8 7.6 copy-start.17
  1859.5 6.9 copy-start.9
  1859.6 12.7 collective-permute-start
  2108.1 8.1 copy-start.20
  2119.0 15.0 copy-start.12
  2119.0 15.0 copy-start.22
  2119.0 15.0 copy-start.23
  (5 other events, 22.1 us)
where the time goes:
time: 2190 us; the launch traced here: 2150 us
  waiting for transfers between devices  893 us (41%)
  local copies, waits for them, and re-layouts  761 us (35%)
  matrix products  339 us (15%)
  starting transfers between devices  64.6 us (3%)
  other arithmetic  60.7 us (3%)
  loops' own time  25.2 us (1%)
    dot_general x11, matrix products, apply_matrix(): return jnp.einsum(pattern, matrix, operand, precision=HIGHEST)  262 us
    unnamed x64, local copies, waits for them, and re-layouts  176 us
    all_to_all x1, waiting for transfers between devices, cross_slots(): lax.all_to_all(arrays[0], 'tm', split_axis=0, concat_axis=1, tiled=True)  174 us
    all_to_all x1, waiting for transfers between devices, back_slots(): lax.all_to_all(arrays[1], 'tm', split_axis=1, concat_axis=0, tiled=True)  174 us
    all_to_all x1, waiting for transfers between devices, back_slots(): lax.all_to_all(arrays[0], 'tm', split_axis=1, concat_axis=0, tiled=True)  171 us
    all_to_all x1, waiting for transfers between devices, cross_slots(): lax.all_to_all(arrays[1], 'tm', split_axis=0, concat_axis=1, tiled=True)  135 us
    rev x2, local copies, waits for them, and re-layouts, mirror_of(): flipped = values[:, ::-1]  135 us
    all_to_all x1, waiting for transfers between devices, enter_rows(): lax.all_to_all(arrays[1], 'tm', split_axis=1, concat_axis=0, tiled=True)  84.4 us
  transfers between devices with their start and end apart: 8, of which 7 were waited for; matrix products, arithmetic and copies ran while one was open for 5% of the time, Pallas kernels for 0%

commit v1 on v0

v1 whole, which is shorter than its diff:
```python
import functools
import math

import jax
import jax.numpy as jnp
import numpy as np
from jax import lax
from jax.experimental import pallas as pl
from jax.experimental.pallas import tpu as pltpu
from jax.sharding import PartitionSpec as P
import ml_dtypes

LANES = 512
RADIX = 4
SUB = LANES // RADIX
TAPS = 127
HEADS = 2
EPSILON = 1e-06
BF16 = jnp.bfloat16
F32 = jnp.float32
VMEM_LIMIT = 56 * 1024 * 1024


def table_split(table, axis, order):
    high = table.astype(ml_dtypes.bfloat16)
    low = (table - high.astype(np.float64)).astype(ml_dtypes.bfloat16)
    parts = {"h": high, "l": low}
    return np.concatenate([parts[name] for name in order], axis=axis)


@functools.lru_cache(maxsize=None)
def tables(rows):
    length = rows * LANES
    turn = 2.0 * math.pi
    n1 = np.arange(rows, dtype=np.float64)
    n2 = np.arange(LANES, dtype=np.float64)
    m = np.arange(SUB, dtype=np.float64)
    first = turn * np.outer(n1 + 0.25, n1) / rows
    enter = table_split(np.concatenate([np.cos(first), -np.sin(first)], axis=0), 1, "hhl")
    leave = table_split(
        np.concatenate([np.cos(first.T), -np.sin(first.T)], axis=1) / length, 1, "hhl"
    )
    twiddle = turn * np.outer(n1 + 0.25, n2) / length
    forward, backward = [], []
    for r in range(RADIX):
        phase = turn * np.outer(m, m / SUB + r / LANES)
        c, s = np.cos(phase), np.sin(phase)
        forward.append(table_split(np.block([[c, -s], [s, c]]), 0, "hhl"))
        c, s = c.T, s.T
        backward.append(table_split(np.block([[c, s], [-s, c]]), 0, "hhl"))
    return (
        enter,
        np.cos(twiddle).astype(np.float32),
        np.sin(twiddle).astype(np.float32),
        np.stack(forward),
        np.stack(backward),
        leave,
    )


def halves(value):
    high = value.astype(BF16)
    low = (value - high.astype(F32)).astype(BF16)
    return high, low


def split_cat(value, axis):
    high, low = halves(value)
    return jnp.concatenate([high, low, high], axis=axis)


def dot(left, right):
    return jnp.dot(left, right, preferred_element_type=F32)


def filter_kernel(
    skip_ref, signal_ref, kernel_ref, enter_ref, cos_ref, sin_ref, forward_ref, backward_ref,
    leave_ref, out_ref, spread_ref,
):
    rows = cos_ref.shape[0]
    for index, ref in enumerate((signal_ref, kernel_ref)):
        turned = dot(enter_ref[...], split_cat(ref[...].reshape(rows, LANES), 0))
        real_in, imag_in = turned[:rows], turned[rows:]
        real = real_in * cos_ref[...] + imag_in * sin_ref[...]
        imag = imag_in * cos_ref[...] - real_in * sin_ref[...]
        r0, r1, r2, r3 = (real[:, b * SUB : (b + 1) * SUB] for b in range(RADIX))
        i0, i1, i2, i3 = (imag[:, b * SUB : (b + 1) * SUB] for b in range(RADIX))
        er, ei, fr, fi = r0 + r2, i0 + i2, r0 - r2, i0 - i2
        gr, gi, hr, hi = r1 + r3, i1 + i3, r1 - r3, i1 - i3
        spread = ((er + gr, ei + gi), (fr + hi, fi - hr), (er - gr, ei - gi), (fr - hi, fi + hr))
        for r, pair in enumerate(spread):
            spread_ref[r, index * rows : (index + 1) * rows, :] = split_cat(
                jnp.concatenate(pair, axis=1), 1
            )
    back = []
    for r in range(RADIX):
        both = dot(spread_ref[r], forward_ref[r])
        sr, si = both[:rows, :SUB], both[:rows, SUB:]
        kr, ki = both[rows:, :SUB], both[rows:, SUB:]
        product = jnp.concatenate([sr * kr - si * ki, sr * ki + si * kr], axis=1)
        turned = dot(split_cat(product, 1), backward_ref[r])
        back.append((turned[:, :SUB], turned[:, SUB:]))
    (r0, i0), (r1, i1), (r2, i2), (r3, i3) = back
    er, ei, fr, fi = r0 + r2, i0 + i2, r0 - r2, i0 - i2
    gr, gi, hr, hi = r1 + r3, i1 + i3, r1 - r3, i1 - i3
    real = jnp.concatenate([er + gr, fr - hi, er - gr, fr + hi], axis=1)
    imag = jnp.concatenate([ei + gi, fi + hr, ei - gi, fi - hr], axis=1)
    turned = jnp.concatenate(
        [real * cos_ref[...] - imag * sin_ref[...], imag * cos_ref[...] + real * sin_ref[...]],
        axis=0,
    )
    result = dot(leave_ref[...], split_cat(turned, 0))
    skip = skip_ref[pl.program_id(0)]
    result = result + skip * signal_ref[...].reshape(rows, LANES)
    out_ref[...] = result.reshape(out_ref.shape)


def long_filter(signal, kernel, skip, out_groups):
    groups, channels, group_rows, _ = signal.shape
    rows = groups * group_rows
    straight = group_rows % 8 == 0 and (rows // out_groups) % 8 == 0
    in_block = (groups, 1, group_rows, LANES)
    out_shape = (out_groups, channels, rows // out_groups, LANES)
    if not straight:
        signal = signal.transpose(1, 0, 2, 3).reshape(1, channels, rows, LANES)
        kernel = kernel.transpose(1, 0, 2, 3).reshape(1, channels, rows, LANES)
        in_block = (1, 1, rows, LANES)
        out_shape = (1, channels, rows, LANES)
    out_block = (out_shape[0], 1) + out_shape[2:]

    def along(c):
        return (0, c, 0, 0)

    def whole(array):
        return pl.BlockSpec(array.shape, lambda c: (0,) * array.ndim)

    held = tables(rows)
    result = pl.pallas_call(
        filter_kernel,
        grid=(channels,),
        in_specs=[
            pl.BlockSpec(memory_space=pltpu.SMEM),
            pl.BlockSpec(in_block, along),
            pl.BlockSpec(in_block, along),
        ]
        + [whole(table) for table in held],
        out_specs=pl.BlockSpec(out_block, along),
        out_shape=jax.ShapeDtypeStruct(out_shape, F32),
        scratch_shapes=[pltpu.VMEM((RADIX, 2 * rows, 6 * SUB), BF16)],
        compiler_params=pltpu.CompilerParams(vmem_limit_bytes=VMEM_LIMIT),
        cost_estimate=pl.CostEstimate(
            flops=channels * rows * LANES * 2048 * 3 * 3,
            bytes_accessed=channels * rows * LANES * 12,
            transcendentals=0,
        ),
        name="long_filter",
    )(skip, signal, kernel, *held)
    if not straight:
        result = result.reshape(channels, out_groups, rows // out_groups, LANES)
        result = result.transpose(1, 0, 2, 3)
    return result


def mix_kernel(
    conv_ref, gate_ref, halo_ref, tap_ref, gain_ref, up_ref, bias_ref, down_ref, out_ref,
    window_ref, high_ref, low_ref, mix_ref,
):
    block = gate_ref.shape[0]
    width = gate_ref.shape[1]
    reach = TAPS + 1
    head_width = width // HEADS

    @pl.when(pl.program_id(0) == 0)
    def _():
        window_ref[:reach, :] = halo_ref[...]

    @pl.when(pl.program_id(0) > 0)
    def _():
        window_ref[:reach, :] = window_ref[block : block + reach, :]

    window_ref[reach:, :] = jnp.transpose(conv_ref[0], (1, 0)) * gate_ref[...]
    high, low = halves(window_ref[...])
    high_ref[...] = high
    low_ref[...] = low
    taps = dot(
        jnp.concatenate([high[reach:], low[reach:], high[reach:]], axis=1), tap_ref[...]
    )
    for b in range(block // reach):
        for h in range(HEADS):
            own = taps[b * reach : (b + 1) * reach, h * reach : (h + 1) * reach]
            band = jnp.concatenate([own, jnp.zeros_like(own)], axis=1)
            band = pltpu.roll(band, 1, 1, stride=1, stride_axis=0)
            near_rows = slice(b * reach, (b + 2) * reach)
            columns = slice(h * head_width, (h + 1) * head_width)
            near_high = high_ref[near_rows, columns]
            near_low = low_ref[near_rows, columns]
            mix_ref[b * reach : (b + 1) * reach, columns] = dot(
                split_cat(band, 1), jnp.concatenate([near_high, near_high, near_low], axis=0)
            )
    mixed = mix_ref[...]
    mean_square = jnp.mean(mixed * mixed, axis=1, keepdims=True)
    normed = mixed * lax.rsqrt(mean_square + EPSILON) * gain_ref[...]
    raised = dot(split_cat(normed, 1), up_ref[...]) + bias_ref[...]
    inner = math.sqrt(2.0 / math.pi) * (raised + 0.044715 * (raised * raised * raised))
    hidden = 0.5 * raised * (1.0 + jnp.tanh(inner))
    out_ref[...] = mixed + dot(split_cat(hidden, 1), down_ref[...])


def weight_split(weight):
    high = lax.reduce_precision(weight, 8, 7)
    low = weight - high
    return jnp.concatenate([high, high, low], axis=0).astype(BF16)


def tail(conv_blocks, gate_input, halo, tap_weight, norm_gain, up_weight, up_bias, down_weight):
    count, width, block = conv_blocks.shape
    reach = TAPS + 1
    taps = tap_weight.reshape(width, HEADS, TAPS)[:, :, ::-1]
    taps = jnp.pad(taps, ((0, 0), (0, 0), (1, 0))).reshape(width, HEADS * reach)
    fixed = (
        weight_split(taps),
        norm_gain.reshape(1, -1),
        weight_split(up_weight),
        up_bias.reshape(1, -1),
        weight_split(down_weight),
    )

    def whole(array):
        return pl.BlockSpec(array.shape, lambda r: (0,) * array.ndim)

    return pl.pallas_call(
        mix_kernel,
        grid=(count,),
        in_specs=[
            pl.BlockSpec((1, width, block), lambda r: (r, 0, 0)),
            pl.BlockSpec((block, width), lambda r: (r, 0)),
            whole(halo),
        ]
        + [whole(array) for array in fixed],
        out_specs=pl.BlockSpec((block, width), lambda r: (r, 0)),
        out_shape=jax.ShapeDtypeStruct(gate_input.shape, F32),
        scratch_shapes=[
            pltpu.VMEM((block + reach, width), F32),
            pltpu.VMEM((block + reach, width), BF16),
            pltpu.VMEM((block + reach, width), BF16),
            pltpu.VMEM((block, width), F32),
        ],
        compiler_params=pltpu.CompilerParams(vmem_limit_bytes=VMEM_LIMIT),
        cost_estimate=pl.CostEstimate(
            flops=count * block * 3 * 2 * (2 * width * up_weight.shape[1] + 3 * width * width),
            bytes_accessed=count * block * width * 12,
            transcendentals=count * block * up_weight.shape[1],
        ),
        name="mix_and_mlp",
    )(conv_blocks, gate_input, halo, *fixed)


def on_device(
    signal, kernel, skip_gain, gate_input, tap_weight, norm_gain, up_weight, up_bias, down_weight
):
    groups = lax.axis_size("tm")
    pair = lax.axis_size("chan")
    frames_here, channels_here = signal.shape
    owned = channels_here // groups
    width = gate_input.shape[1]
    first_channel = lax.axis_index("chan") * channels_here + lax.axis_index("tm") * owned
    skip_here = lax.dynamic_slice_in_dim(skip_gain, first_channel, owned)

    def enter(array):
        shaped = array.reshape(frames_here // LANES, LANES, groups, owned).transpose(2, 3, 0, 1)
        return lax.all_to_all(shaped, "tm", split_axis=0, concat_axis=0, tiled=True)

    filtered = long_filter(enter(signal), enter(kernel), skip_here, groups * pair)
    back = lax.all_to_all(filtered, ("tm", "chan"), split_axis=0, concat_axis=0, tiled=True)
    blocks = back.reshape(groups, pair, owned, -1, LANES).transpose(3, 1, 0, 2, 4)
    blocks = blocks.reshape(-1, width, LANES)
    reach = TAPS + 1
    last = blocks[-1, :, LANES - reach :].T * gate_input[-reach:]
    devices = groups * pair
    halo = lax.ppermute(last, ("tm", "chan"), [(i, i + 1) for i in range(devices - 1)])
    return tail(blocks, gate_input, halo, tap_weight, norm_gain, up_weight, up_bias, down_weight)


def solution(mesh):
    placed = (
        P(("grp", "tm"), "chan"),
        P("tm", "chan"),
        P(),
        P(("grp", "tm", "chan"), None),
        P(),
        P(),
        P(),
        P(),
        P(),
    )
    return jax.shard_map(
        on_device,
        mesh=mesh,
        in_specs=placed,
        out_specs=P(("grp", "tm", "chan"), None),
        check_vma=False,
    )
```

time: 2190 us -> 405 us (0.18); the launches traced: 2150 us -> 400 us
  local copies, waits for them, and re-layouts: 761 us -> 35.3 us
  waiting for transfers between devices: 893 us -> 254 us
  matrix products: 339 us -> 0 us
  Pallas kernels: 0 us -> 78.3 us
  other arithmetic: 60.7 us -> 4.71 us
  starting transfers between devices: 64.6 us -> 27.3 us
  loops' own time: 25.2 us -> 0 us
    all_to_all x7 -> x3, waiting for transfers between devices: 893 us -> 254 us  [the longest x2 166 us: enter(): return lax.all_to_all(shaped, 'tm', split_axis=0, concat_axis=0, tiled=True)]
    dot_general x22 -> x0, matrix products: 339 us -> none  [the longest x11 262 us: apply_matrix(): return jnp.einsum(pattern, matrix, operand, precision=HIGHEST)]
    slice x20 -> x1, local copies, waits for them, and re-layouts: 200 us -> 0.02 us  [on_device(): last = blocks[-1, :, LANES - reach:].T * gate_input[-reach:]]
    unnamed x64 -> x17, local copies, waits for them, and re-layouts: 176 us -> 29.3 us
    rev x10 -> x1, local copies, waits for them, and re-layouts: 138 us -> 0.19 us  [tail(): taps = tap_weight.reshape(width, HEADS, TAPS)[:, :, ::-1]]
    pallas_call x0 -> x2, Pallas kernels: none -> 78.3 us  [the longest x1 41.2 us: long_filter(): pl.pallas_call(filter_kernel, grid=(channels,), in_specs=[pl.BlockSpec(me...]
    reshape x18 -> x4, local copies, waits for them, and re-layouts: 70.6 us -> 5.11 us  [the longest x1 4.62 us: on_device(): back.reshape(groups, pair, owned, -1, LANES).transpose(3, 1, 0, 2, 4)]
    transpose x16 -> x0, local copies, waits for them, and re-layouts: 42.1 us -> none  [conv_block(): padded.transpose(1, 0, 2).reshape(HEADS, block_rows * (band_width + 1))]
  transfers between devices with their start and end apart: 8 -> 4, of which waited for: 7 -> 3; matrix products, arithmetic and copies ran while one was open for 5% -> 5% of each run, Pallas kernels for 0% -> 0%
where the time goes in v1:
time: 405 us; the launch traced here: 400 us
  waiting for transfers between devices  254 us (63%)
  Pallas kernels  78.3 us (19%)
  local copies, waits for them, and re-layouts  35.3 us (9%)
  starting transfers between devices  27.3 us (7%)
  other arithmetic  4.71 us (1%)
    all_to_all x2, waiting for transfers between devices, enter(): return lax.all_to_all(shaped, 'tm', split_axis=0, concat_axis=0, tiled=True)  166 us
    all_to_all x1, waiting for transfers between devices, on_device(): lax.all_to_all(filtered, ('tm', 'chan'), split_axis=0, concat_axis=0, til...  88 us
    pallas_call x1, Pallas kernels, long_filter(): pl.pallas_call(filter_kernel, grid=(channels,), in_specs=[pl.BlockSpec(me...  41.2 us
    pallas_call x1, Pallas kernels, tail(): pl.pallas_call(mix_kernel, grid=(count,), in_specs=[pl.BlockSpec((1, widt...  37 us
    unnamed x17, local copies, waits for them, and re-layouts  29.3 us
    all_to_all x2, starting transfers between devices, enter(): return lax.all_to_all(shaped, 'tm', split_axis=0, concat_axis=0, tiled=True)  14.7 us
    all_to_all x1, starting transfers between devices, on_device(): lax.all_to_all(filtered, ('tm', 'chan'), split_axis=0, concat_axis=0, til...  9.64 us
  transfers between devices with their start and end apart: 4, of which 3 were waited for; matrix products, arithmetic and copies ran while one was open for 5% of the time, Pallas kernels for 0%

profile of v1, /device:TPU:11, one launch (start us, length us, event | category | flops | bytes accessed | tf_op | source)
XLA Modules:
  0.0 399.7 jit_solution(13556189744764684147)
XLA Ops:
  0.0 5.6 %copy.20 = f32[8192,128]{0,1:T(8,128)} copy(f32[8192,128]{1,0:T(8,128)} %param.15) | data formatting | bytes 8388608 | tf_op args[0]
  5.6 7.4 %copy.34 = f32[16,8,16,512]{3,2,1,0:T(8,128)} copy(f32[16,8,16,512]{3,1,2,0:T(8,128)} %bitcast.31) | data formatting | bytes 8388608
  13.0 6.6 %all-to-all-start = ((f32[16,8,16,512]{3,2,1,0:T(8,128)}), f32[16,8,16,512]{3,2,1,0:T(8,128)}, u32[]{:S(2)}, u32[]{:S(2)}) async-start(f32[16,8,16,512]{3,2,1,0:T(8,128)} %copy.34), calls=%async_computation | async-start | bytes 8388608 | tf_op jit(solution)/shard_map/all_to_all | solution.py:271
  19.6 5.6 %copy.21 = f32[8192,128]{0,1:T(8,128)} copy(f32[8192,128]{1,0:T(8,128)} %param.16) | data formatting | bytes 8388608 | tf_op args[1]
  25.2 7.4 %copy.33 = f32[16,8,16,512]{3,2,1,0:T(8,128)} copy(f32[16,8,16,512]{3,1,2,0:T(8,128)} %bitcast.32) | data formatting | bytes 8388608
  32.6 78.0 %all-to-all-done.signal_ref = f32[16,8,16,512]{3,2,1,0:T(8,128)} async-done(((f32[16,8,16,512]{3,2,1,0:T(8,128)}), f32[16,8,16,512]{3,2,1,0:T(8,128)}, u32[]{:S(2)}, u32[]{:S(2)}) %all-to-all-start) | async-done | bytes 4194336 | tf_op jit(solution)/shard_map/all_to_all | solution.py:271
  110.7 8.1 %all-to-all-start.1 = ((f32[16,8,16,512]{3,2,1,0:T(8,128)}), f32[16,8,16,512]{3,2,1,0:T(8,128)}, u32[]{:S(2)}, u32[]{:S(2)}) async-start(f32[16,8,16,512]{3,2,1,0:T(8,128)} %copy.33), calls=%async_computation.1 | async-start | bytes 8388608 | tf_op jit(solution)/shard_map/all_to_all | solution.py:271
  118.8 0.7 dynamic_slice.3.skip_ref
  119.5 88.0 %all-to-all-done.1.kernel_ref = f32[16,8,16,512]{3,2,1,0:T(8,128)} async-done(((f32[16,8,16,512]{3,2,1,0:T(8,128)}), f32[16,8,16,512]{3,2,1,0:T(8,128)}, u32[]{:S(2)}, u32[]{:S(2)}) %all-to-all-start.1) | async-done | bytes 4194336 | tf_op jit(solution)/shard_map/all_to_all | solution.py:271
  207.5 41.2 %long_filter.1 = f32[32,8,8,512]{3,2,1,0:T(8,128)} custom-call(f32[8]{0:T(128)} %dynamic_slice.3.skip_ref, f32[16,8,16,512]{3,2,1,0:T(8,128)} %all-to-all-done.signal_ref, f32[16,8,16,512]{3,2,1,0:T(8,128)} %all-to-all-done.1.kernel_ref, bf16[512,768]{1,0:T(8,128)(2,1)} %constant.30.clone.enter_ref, f32[256,512]{1,0:T(8,128)} %constant.31.clone.cos_ref, ...), custom_call_target="tpu_custom_call" | custom-call | flops 19327352832 | bytes 12582912 | tf_op jit(solution)/shard_map/long_filter/pallas_call | solution.py:138
  248.7 9.6 %all-to-all-start.2 = ((f32[32,8,8,512]{3,2,1,0:T(8,128)}), f32[32,8,8,512]{3,2,1,0:T(8,128)}, u32[]{:S(2)}, u32[]{:S(2)}) async-start(f32[32,8,8,512]{3,2,1,0:T(8,128)} %long_filter.1), calls=%async_computation.2 | async-start | bytes 8388608 | tf_op jit(solution)/shard_map/all_to_all | solution.py:274
  258.3 0.0 copy-start.1
  258.3 0.0 copy-start.2
  258.4 0.2 reshape.32
  258.6 0.2 copy.26
  258.7 0.2 rev.3
  258.9 0.1 copy.27
  259.1 0.4 copy-done.1
  259.6 0.2 reduce-precision_convert_fusion.1
  259.8 0.1 copy-done.2
  259.9 0.2 reduce-precision_convert_fusion
  260.0 1.3 pad_maximum_fusion.1.down_ref
  261.3 88.0 %all-to-all-done.2 = f32[32,8,8,512]{3,2,1,0:T(8,128)} async-done(((f32[32,8,8,512]{3,2,1,0:T(8,128)}), f32[32,8,8,512]{3,2,1,0:T(8,128)}, u32[]{:S(2)}, u32[]{:S(2)}) %all-to-all-start.2) | async-done | bytes 4194336 | tf_op jit(solution)/shard_map/all_to_all | solution.py:274
  349.3 4.6 %copy.22 = f32[16,2,8,8,512]{4,2,0,1,3:T(8,128)S(1)} copy(f32[16,2,8,8,512]{4,3,2,1,0:T(8,128)} %bitcast.2) | data formatting | bytes 8388608 | tf_op jit(solution)/shard_map/reshape | solution.py:275
  354.0 1.9 copy-done
  355.9 0.1 copy.28
  356.0 0.9 bitcast_multiply_fusion
  357.0 2.9 collective-permute-start
  359.9 1.4 pad_maximum_fusion.up_ref
  361.3 0.8 pad_maximum_fusion.2.tap_ref
  362.0 0.6 copy-done.4
  362.7 37.0 %mix_and_mlp.1 = f32[4096,256]{1,0:T(8,128)} custom-call(f32[8,256,512]{2,1,0:T(8,128)} %bitcast.34, f32[4096,256]{1,0:T(8,128)} %gate_ref.1, f32[128,256]{1,0:T(8,128)} %copy-done.4, bf16[768,256]{1,0:T(8,128)(2,1)} %pad_maximum_fusion.2.tap_ref, f32[1,256]{1,0:T(1,128)} %bitcast.37, bf16[768,1024]{1,0:T(8,128)(2,1)} %pad_maximum_fusion.up_ref, ...), custom_call_target="tpu_custom_call" | custom-call | flops 17716740096 | bytes 12582912 | tf_op jit(solution)/shard_map/mix_and_mlp/pallas_call | solution.py:231
  (10 shorter events, 0.1 us)
Async XLA Ops:
  13.0 97.7 %all-to-all-start = ((f32[16,8,16,512]{3,2,1,0:T(8,128)}), f32[16,8,16,512]{3,2,1,0:T(8,128)}, u32[]{:S(2)}, u32[]{:S(2)}) async-start(f32[16,8,16,512]{3,2,1,0:T(8,128)} %copy.34), calls=%async_computation | async-start | bytes 8388608 | tf_op jit(solution)/shard_map/all_to_all | solution.py:271
  110.7 8.1 %copy-start.5 = (f32[256]{0:T(256)S(1)}, f32[256]{0:T(256)}, u32[]{:S(2)}) copy-start(f32[256]{0:T(256)} %param.17) | copy-start | bytes 3076
  110.7 96.8 %all-to-all-start.1 = ((f32[16,8,16,512]{3,2,1,0:T(8,128)}), f32[16,8,16,512]{3,2,1,0:T(8,128)}, u32[]{:S(2)}, u32[]{:S(2)}) async-start(f32[16,8,16,512]{3,2,1,0:T(8,128)} %copy.33), calls=%async_computation.1 | async-start | bytes 8388608 | tf_op jit(solution)/shard_map/all_to_all | solution.py:271
  248.7 9.7 %copy-start.3 = (f32[256,254]{1,0:T(8,128)S(1)}, f32[256,254]{1,0:T(8,128)}, u32[]{:S(2)}) copy-start(f32[256,254]{1,0:T(8,128)} %param.19) | copy-start | bytes 780292
  248.7 100.7 %all-to-all-start.2 = ((f32[32,8,8,512]{3,2,1,0:T(8,128)}), f32[32,8,8,512]{3,2,1,0:T(8,128)}, u32[]{:S(2)}, u32[]{:S(2)}) async-start(f32[32,8,8,512]{3,2,1,0:T(8,128)} %long_filter.1), calls=%async_computation.2 | async-start | bytes 8388608 | tf_op jit(solution)/shard_map/all_to_all | solution.py:274
  258.3 1.2 copy-start.1
  258.3 1.5 copy-start.2
  353.9 2.0 copy-start
  357.0 5.1 %collective-permute-start = (f32[128,256]{1,0:T(8,128)S(1)}, f32[128,256]{1,0:T(8,128)S(1)}, u32[]{:S(2)}, u32[]{:S(2)}) collective-permute-start(f32[128,256]{1,0:T(8,128)S(1)} %bitcast_multiply_fusion), channel_id=1, source_target_pairs={{0,1},{1,2},{2,3},{3,4},{4,5},{5,6},{6,7},{7,8},{8,9},{9,10},{10,1... | collective-permute-start | bytes 393224 | tf_op jit(solution)/shard_map/ppermute | solution.py:280
  362.0 0.6 copy-start.4

commit v2 on v1

--- a/solution.py
+++ b/solution.py
@@ -73,13 +73,11 @@
     return jnp.dot(left, right, preferred_element_type=F32)
 
 
-def filter_kernel(
-    skip_ref, signal_ref, kernel_ref, enter_ref, cos_ref, sin_ref, forward_ref, backward_ref,
-    leave_ref, out_ref, spread_ref,
-):
+def filter_channel(signal, kernel, skip, enter_ref, cos_ref, sin_ref, forward_ref, backward_ref,
+                   leave_ref, spread_ref):
     rows = cos_ref.shape[0]
-    for index, ref in enumerate((signal_ref, kernel_ref)):
-        turned = dot(enter_ref[...], split_cat(ref[...].reshape(rows, LANES), 0))
+    for index, value in enumerate((signal, kernel)):
+        turned = dot(enter_ref[...], split_cat(value, 0))
         real_in, imag_in = turned[:rows], turned[rows:]
         real = real_in * cos_ref[...] + imag_in * sin_ref[...]
         imag = imag_in * cos_ref[...] - real_in * sin_ref[...]
@@ -109,9 +107,19 @@
         [real * cos_ref[...] - imag * sin_ref[...], imag * cos_ref[...] + real * sin_ref[...]],
         axis=0,
     )
-    result = dot(leave_ref[...], split_cat(turned, 0))
-    skip = skip_ref[pl.program_id(0)]
-    result = result + skip * signal_ref[...].reshape(rows, LANES)
+    return dot(leave_ref[...], split_cat(turned, 0)) + skip * signal
+
+
+def filter_kernel(
+    skip_ref, signal_ref, kernel_ref, enter_ref, cos_ref, sin_ref, forward_ref, backward_ref,
+    leave_ref, out_ref, spread_ref,
+):
+    rows = cos_ref.shape[0]
+    result = filter_channel(
+        signal_ref[...].reshape(rows, LANES), kernel_ref[...].reshape(rows, LANES),
+        skip_ref[pl.program_id(0)], enter_ref, cos_ref, sin_ref, forward_ref, backward_ref,
+        leave_ref, spread_ref,
+    )
     out_ref[...] = result.reshape(out_ref.shape)
 
 
@@ -161,24 +169,11 @@
     return result
 
 
-def mix_kernel(
-    conv_ref, gate_ref, halo_ref, tap_ref, gain_ref, up_ref, bias_ref, down_ref, out_ref,
-    window_ref, high_ref, low_ref, mix_ref,
-):
-    block = gate_ref.shape[0]
-    width = gate_ref.shape[1]
+def mix_block(window_ref, tap_ref, gain_ref, up_ref, bias_ref, down_ref, out_ref, high_ref, low_ref,
+              mix_ref):
+    block, width = out_ref.shape
     reach = TAPS + 1
     head_width = width // HEADS
-
-    @pl.when(pl.program_id(0) == 0)
-    def _():
-        window_ref[:reach, :] = halo_ref[...]
-
-    @pl.when(pl.program_id(0) > 0)
-    def _():
-        window_ref[:reach, :] = window_ref[block : block + reach, :]
-
-    window_ref[reach:, :] = jnp.transpose(conv_ref[0], (1, 0)) * gate_ref[...]
     high, low = halves(window_ref[...])
     high_ref[...] = high
     low_ref[...] = low
@@ -206,24 +201,50 @@
     out_ref[...] = mixed + dot(split_cat(hidden, 1), down_ref[...])
 
 
+def mix_kernel(
+    conv_ref, gate_ref, halo_ref, tap_ref, gain_ref, up_ref, bias_ref, down_ref, out_ref,
+    window_ref, high_ref, low_ref, mix_ref,
+):
+    block = gate_ref.shape[0]
+    reach = TAPS + 1
+
+    @pl.when(pl.program_id(0) == 0)
+    def _():
+        window_ref[:reach, :] = halo_ref[...]
+
+    @pl.when(pl.program_id(0) > 0)
+    def _():
+        window_ref[:reach, :] = window_ref[block : block + reach, :]
+
+    window_ref[reach:, :] = jnp.transpose(conv_ref[0], (1, 0)) * gate_ref[...]
+    mix_block(
+        window_ref, tap_ref, gain_ref, up_ref, bias_ref, down_ref, out_ref, high_ref, low_ref, mix_ref
+    )
+
+
 def weight_split(weight):
     high = lax.reduce_precision(weight, 8, 7)
     low = weight - high
     return jnp.concatenate([high, high, low], axis=0).astype(BF16)
 
 
-def tail(conv_blocks, gate_input, halo, tap_weight, norm_gain, up_weight, up_bias, down_weight):
-    count, width, block = conv_blocks.shape
-    reach = TAPS + 1
+def fixed_operands(tap_weight, norm_gain, up_weight, up_bias, down_weight):
+    width = tap_weight.shape[0]
     taps = tap_weight.reshape(width, HEADS, TAPS)[:, :, ::-1]
-    taps = jnp.pad(taps, ((0, 0), (0, 0), (1, 0))).reshape(width, HEADS * reach)
-    fixed = (
+    taps = jnp.pad(taps, ((0, 0), (0, 0), (1, 0))).reshape(width, HEADS * (TAPS + 1))
+    return (
         weight_split(taps),
         norm_gain.reshape(1, -1),
         weight_split(up_weight),
         up_bias.reshape(1, -1),
         weight_split(down_weight),
     )
+
+
+def tail(conv_blocks, gate_input, halo, fixed):
+    count, width, block = conv_blocks.shape
+    reach = TAPS + 1
+    hidden = fixed[3].shape[1]
 
     def whole(array):
         return pl.BlockSpec(array.shape, lambda r: (0,) * array.ndim)
@@ -247,12 +268,291 @@
         ],
         compiler_params=pltpu.CompilerParams(vmem_limit_bytes=VMEM_LIMIT),
         cost_estimate=pl.CostEstimate(
-            flops=count * block * 3 * 2 * (2 * width * up_weight.shape[1] + 3 * width * width),
+            flops=count * block * 3 * 2 * (2 * width * hidden + 3 * width * width),
             bytes_accessed=count * block * width * 12,
-            transcendentals=count * block * up_weight.shape[1],
+            transcendentals=count * block * hidden,
         ),
         name="mix_and_mlp",
     )(conv_blocks, gate_input, halo, *fixed)
+
+
+def turn_kernel(signal_ref, kernel_ref, *out_refs):
+    chunk = signal_ref.shape[0]
+    half = 8 // 2
+    for tile in range(chunk // 128):
+        span = slice(tile * 128, (tile + 1) * 128)
+        s = jnp.transpose(signal_ref[span, :], (1, 0))
+        k = jnp.transpose(kernel_ref[span, :], (1, 0))
+        lower = lax.broadcasted_iota(jnp.int32, s.shape, 0) % 8 < half
+        first = jnp.where(lower, s, pltpu.roll(k, half, 0))
+        second = jnp.where(lower, pltpu.roll(s, s.shape[0] - half, 0), k)
+        for ref, value in zip(out_refs, (first, second)):
+            ref[:, tile] = value.reshape(ref.shape[0], 8, 128)
+
+
+def turn(signal, kernel, groups):
+    frames, width = signal.shape
+    chunk = 1024
+    tiles = chunk // 128
+    block = pl.BlockSpec((chunk, width), lambda i: (i, 0))
+    out_block = pl.BlockSpec((groups, tiles, 8, 128), lambda i: (0, i, 0, 0))
+    shape = jax.ShapeDtypeStruct((groups, frames // 128, 8, 128), F32)
+    return pl.pallas_call(
+        turn_kernel,
+        grid=(frames // chunk,),
+        in_specs=[block, block],
+        out_specs=[out_block, out_block],
+        out_shape=[shape, shape],
+        compiler_params=pltpu.CompilerParams(vmem_limit_bytes=VMEM_LIMIT),
+        name="turn",
+    )(signal, kernel)
+
+
+def gather_channel(ref, slot, rows):
+    tiles = LANES // 128
+    return jnp.concatenate(
+        [ref[pl.ds(8 * j + slot, rows, stride=8 * tiles), :] for j in range(tiles)], axis=1
+    )
+
+
+def scatter_channel(ref, slot, value):
+    tiles = LANES // 128
+    for j in range(tiles):
+        ref[pl.ds(8 * j + slot, value.shape[0], stride=8 * tiles), :] = (
+            value[:, j * 128 : (j + 1) * 128]
+        )
+
+
+def first_half_kernel(skip_ref, data_ref, *rest):
+    *table_refs, out_ref, spread_ref = rest
+    rows = table_refs[1].shape[0]
+    c = pl.program_id(0)
+    result = filter_channel(
+        gather_channel(data_ref, c, rows), gather_channel(data_ref, c + 4, rows), skip_ref[c],
+        *table_refs, spread_ref,
+    )
+    scatter_channel(out_ref, c, result)
+
+
+def second_half_kernel(late, skip_ref, data_ref, *rest):
+    *table_refs, before_ref, late_ref, early_ref, spread_ref, held_ref, sems = rest
+    rows = table_refs[1].shape[0]
+    c = pl.program_id(0)
+    devices, tiles = late_ref.shape[0], late_ref.shape[1] + early_ref.shape[1]
+    load = pltpu.make_async_copy(before_ref, held_ref, sems.at[0])
+
+    @pl.when(c == 0)
+    def _():
+        load.start()
+
+    result = filter_channel(
+        gather_channel(data_ref, c, rows), gather_channel(data_ref, c + 4, rows),
+        skip_ref[c + 4], *table_refs, spread_ref,
+    )
+
+    @pl.when(c == 0)
+    def _():
+        load.wait()
+
+    scatter_channel(held_ref, c + 4, result)
+
+    @pl.when(c == pl.num_programs(0) - 1)
+    def _():
+        shaped = held_ref.reshape(devices, tiles, 8, 128)
+        copies = [
+            pltpu.make_async_copy(
+                shaped.at[:, late:tiles], late_ref.at[:, 0 : tiles - late], sems.at[1]
+            ),
+            pltpu.make_async_copy(
+                shaped.at[:, late - 1 : late],
+                late_ref.at[:, tiles - late : tiles - late + 1],
+                sems.at[2],
+            ),
+            pltpu.make_async_copy(shaped.at[:, 0 : late - 1], early_ref, sems.at[3]),
+        ]
+        for copy in copies:
+            copy.start()
+        for copy in copies:
+            copy.wait()
+
+
+def filter_half(data, skip, before, devices, late):
+    flat = data.reshape(-1, 128)
+    rows = flat.shape[0] // (8 * (LANES // 128))
+    tiles = flat.shape[0] // (8 * devices)
+    held = tables(rows)
+
+    def whole(array):
+        return pl.BlockSpec(array.shape, lambda c: (0,) * array.ndim)
+
+    in_specs = [pl.BlockSpec(memory_space=pltpu.SMEM), whole(flat)] + [whole(t) for t in held]
+    spread = pltpu.VMEM((RADIX, 2 * rows, 6 * SUB), BF16)
+    options = dict(
+        grid=(4,),
+        compiler_params=pltpu.CompilerParams(vmem_limit_bytes=VMEM_LIMIT),
+        cost_estimate=pl.CostEstimate(
+            flops=4 * rows * LANES * 2048 * 3 * 3,
+            bytes_accessed=4 * rows * LANES * 12,
+            transcendentals=0,
+        ),
+    )
+    if before is None:
+        return pl.pallas_call(
+            first_half_kernel,
+            in_specs=in_specs,
+            out_specs=whole(flat),
+            out_shape=jax.ShapeDtypeStruct(flat.shape, F32),
+            scratch_shapes=[spread],
+            name="filter_first",
+            **options,
+        )(skip, flat, *held)
+    anywhere = pl.BlockSpec(memory_space=pl.ANY)
+    return pl.pallas_call(
+        functools.partial(second_half_kernel, late),
+        in_specs=in_specs + [anywhere],
+        out_specs=[anywhere, anywhere],
+        out_shape=[
+            jax.ShapeDtypeStruct((devices, tiles - late + 1, 8, 128), F32),
+            jax.ShapeDtypeStruct((devices, late - 1, 8, 128), F32),
+        ],
+        scratch_shapes=[spread, pltpu.VMEM(flat.shape, F32), pltpu.SemaphoreType.DMA((4,))],
+        name="filter_second",
+        **options,
+    )(skip, flat, *held, before)
+
+
+def frames_by_channels(tile):
+    paired = tile.reshape(tile.shape[0] // HEADS, HEADS, 8, 128)
+    return jnp.concatenate(
+        [jnp.transpose(paired[:, h].reshape(-1, 128), (1, 0)) for h in range(HEADS)], axis=1
+    )
+
+
+def late_kernel(conv_ref, edge_ref, gate_ref, edge_gate_ref, *rest):
+    *fixed, out_ref, window_ref, high_ref, low_ref, mix_ref = rest
+    block = gate_ref.shape[0]
+    reach = TAPS + 1
+
+    @pl.when(pl.program_id(0) == 0)
+    def _():
+        window_ref[:reach, :] = frames_by_channels(edge_ref[:, 0]) * edge_gate_ref[...]
+
+    @pl.when(pl.program_id(0) > 0)
+    def _():
+        window_ref[:reach, :] = window_ref[block : block + reach, :]
+
+    for j in range(block // reach):
+        span = slice(j * reach, (j + 1) * reach)
+        window_ref[reach + j * reach : 2 * reach + j * reach, :] = (
+            frames_by_channels(conv_ref[:, j]) * gate_ref[span, :]
+        )
+    mix_block(window_ref, *fixed, out_ref, high_ref, low_ref, mix_ref)
+
+
+def early_kernel(conv_ref, edge_ref, gate_ref, halo_ref, *rest):
+    *fixed, _, out_ref, window_ref, high_ref, low_ref, mix_ref = rest
+    block = gate_ref.shape[0]
+    reach = TAPS + 1
+    last = pl.program_id(0) == pl.num_programs(0) - 1
+
+    @pl.when(pl.program_id(0) == 0)
+    def _():
+        window_ref[:reach, :] = halo_ref[...]
+
+    @pl.when(pl.program_id(0) > 0)
+    def _():
+        window_ref[:reach, :] = window_ref[block : block + reach, :]
+
+    count = block // reach
+    for j in range(count):
+        tile = conv_ref[:, j]
+        if j == count - 1:
+            tile = jnp.where(last, edge_ref[:, 0], tile)
+        span = slice(j * reach, (j + 1) * reach)
+        window_ref[reach + j * reach : 2 * reach + j * reach, :] = (
+            frames_by_channels(tile) * gate_ref[span, :]
+        )
+    mix_block(window_ref, *fixed, out_ref, high_ref, low_ref, mix_ref)
+
+
+def tail_part(conv, late, gate_input, halo, before, late_tiles, fixed):
+    devices = conv.shape[0]
+    frames, width = gate_input.shape
+    reach = TAPS + 1
+    block = 512
+    per_block = block // 128
+    edge = late.shape[1] - 1
+    first = before is not None
+
+    def whole(array):
+        return pl.BlockSpec(array.shape, lambda r: (0,) * array.ndim)
+
+    start = 0 if first else late_tiles // per_block
+    count = (late_tiles if first else edge) // per_block
+    in_specs = [
+        pl.BlockSpec((devices, per_block, 8, 128), lambda r: (0, r, 0, 0)),
+        pl.BlockSpec((devices, 1, 8, 128), lambda r: (0, edge, 0, 0)),
+        pl.BlockSpec((block, width), lambda r: (r + start, 0)),
+    ]
+    operands = [conv, late, gate_input]
+    if first:
+        in_specs += [whole(halo)]
+        operands += [halo]
+    else:
+        in_specs += [pl.BlockSpec((reach, width), lambda r: (late_tiles - 1, 0))]
+        operands += [gate_input]
+    in_specs += [whole(array) for array in fixed]
+    operands += fixed
+    aliases = {}
+    if first:
+        aliases = {len(operands): 0}
+        in_specs += [pl.BlockSpec(memory_space=pl.ANY)]
+        operands += [before]
+    hidden = fixed[3].shape[1]
+    return pl.pallas_call(
+        early_kernel if first else late_kernel,
+        grid=(count,),
+        in_specs=in_specs,
+        out_specs=pl.BlockSpec((block, width), lambda r: (r + start, 0)),
+        out_shape=jax.ShapeDtypeStruct(gate_input.shape, F32),
+        input_output_aliases=aliases,
+        scratch_shapes=[
+            pltpu.VMEM((block + reach, width), F32),
+            pltpu.VMEM((block + reach, width), BF16),
+            pltpu.VMEM((block + reach, width), BF16),
+            pltpu.VMEM((block, width), F32),
+        ],
+        compiler_params=pltpu.CompilerParams(vmem_limit_bytes=VMEM_LIMIT),
+        cost_estimate=pl.CostEstimate(
+            flops=count * block * 3 * 2 * (2 * width * hidden + 3 * width * width),
+            bytes_accessed=count * block * width * 12,
+            transcendentals=count * block * hidden,
+        ),
+        name="mix_early" if first else "mix_late",
+    )(*operands)
+
+
+def owned_eight(signal, kernel, skip_here, gate_input, fixed):
+    groups = lax.axis_size("tm")
+    devices = groups * lax.axis_size("chan")
+    reach = TAPS + 1
+    late_tiles = 2 * (512 // 128)
+
+    def enter(array):
+        return lax.all_to_all(array, "tm", split_axis=0, concat_axis=0, tiled=True)
+
+    def leave(array):
+        return lax.all_to_all(array, ("tm", "chan"), split_axis=0, concat_axis=0, tiled=True)
+
+    one, two = turn(signal, kernel, groups)
+    before = filter_half(enter(one), skip_here, None, devices, late_tiles)
+    late, early = filter_half(enter(two), skip_here, before, devices, late_tiles)
+    late = leave(late)
+    final = frames_by_channels(late[:, late.shape[1] - 2]) * gate_input[-reach:]
+    halo = lax.ppermute(final, ("tm", "chan"), [(i, i + 1) for i in range(devices - 1)])
+    early = leave(early)
+    part = tail_part(late, late, gate_input, None, None, late_tiles, fixed)
+    return tail_part(early, late, gate_input, halo, part, late_tiles, fixed)
 
 
 def on_device(
@@ -265,6 +565,11 @@
     width = gate_input.shape[1]
     first_channel = lax.axis_index("chan") * channels_here + lax.axis_index("tm") * owned
     skip_here = lax.dynamic_slice_in_dim(skip_gain, first_channel, owned)
+    fixed = fixed_operands(tap_weight, norm_gain, up_weight, up_bias, down_weight)
+    window = frames_here * groups
+    if owned == 8 and channels_here == 128 and pair == HEADS and window == 256 * LANES:
+        if gate_input.shape[0] % 512 == 0 and gate_input.shape[0] >= 2048:
+            return owned_eight(signal, kernel, skip_here, gate_input, fixed)
 
     def enter(array):
         shaped = array.reshape(frames_here // LANES, LANES, groups, owned).transpose(2, 3, 0, 1)
@@ -278,7 +583,7 @@
     last = blocks[-1, :, LANES - reach :].T * gate_input[-reach:]
     devices = groups * pair
     halo = lax.ppermute(last, ("tm", "chan"), [(i, i + 1) for i in range(devices - 1)])
-    return tail(blocks, gate_input, halo, tap_weight, norm_gain, up_weight, up_bias, down_weight)
+    return tail(blocks, gate_input, halo, fixed)
 
 
 def solution(mesh):

time: 405 us -> 368 us (0.909)
  waiting for transfers between devices: 254 us -> 121 us
  blocking collectives: 0 us -> 98.1 us
  local copies, waits for them, and re-layouts: 35.3 us -> 7.11 us
  Pallas kernels: 78.3 us -> 106 us
    all_to_all x3, waiting for transfers between devices: 254 us -> 121 us  [the longest x2 61 us: leave(): lax.all_to_all(array, ('tm', 'chan'), split_axis=0, concat_axis=0, tiled=...]
    all_to_all x0 -> x1, blocking collectives: none -> 98.1 us  [enter(): return lax.all_to_all(array, 'tm', split_axis=0, concat_axis=0, tiled=True)]
    unnamed x17 -> x12, local copies, waits for them, and re-layouts: 29.3 us -> 0.66 us
    pallas_call x2 -> x5, Pallas kernels: 78.3 us -> 106 us  [the longest x2 40.6 us: tail_part(): pl.pallas_call(early_kernel if first else late_kernel, grid=(count,), in_...]
  transfers between devices with their start and end apart: 4 -> 4, of which waited for: 3 -> 2; matrix products, arithmetic and copies ran while one was open for 5% -> 4% of each run, Pallas kernels for 0% -> 15%
where the time goes in v2:
time: 368 us; the launch traced here: 366 us
  waiting for transfers between devices  121 us (33%)
  Pallas kernels  106 us (29%)
  blocking collectives  98.1 us (27%)
  starting transfers between devices  25.5 us (7%)
  other arithmetic  7.42 us (2%)
  local copies, waits for them, and re-layouts  7.11 us (2%)
    all_to_all x1, blocking collectives, enter(): return lax.all_to_all(array, 'tm', split_axis=0, concat_axis=0, tiled=True)  98.1 us
    all_to_all x2, waiting for transfers between devices, leave(): lax.all_to_all(array, ('tm', 'chan'), split_axis=0, concat_axis=0, tiled=...  61 us
    all_to_all x1, waiting for transfers between devices, enter(): return lax.all_to_all(array, 'tm', split_axis=0, concat_axis=0, tiled=True)  60.1 us
    pallas_call x2, Pallas kernels, tail_part(): pl.pallas_call(early_kernel if first else late_kernel, grid=(count,), in_...  40.6 us
    pallas_call x1, Pallas kernels, filter_half(): pl.pallas_call(functools.partial(second_half_kernel, late), in_specs=in_s...  28.6 us
    pallas_call x1, Pallas kernels, filter_half(): pl.pallas_call(first_half_kernel, in_specs=in_specs, out_specs=whole(flat...  27.4 us
    all_to_all x2, starting transfers between devices, leave(): lax.all_to_all(array, ('tm', 'chan'), split_axis=0, concat_axis=0, tiled=...  16.3 us
    pallas_call x1, Pallas kernels, turn(): pl.pallas_call(turn_kernel, grid=(frames // chunk,), in_specs=[block, blo...  9.86 us
  transfers between devices with their start and end apart: 4, of which 2 were waited for; matrix products, arithmetic and copies ran while one was open for 4% of the time, Pallas kernels for 15%

profile of v2, /device:TPU:11, one launch (start us, length us, event | category | flops | bytes accessed | tf_op | source)
XLA Modules:
  0.0 365.8 jit_solution(2534184006089710105)
XLA Ops:
  0.0 9.9 %turn.1 = (f32[16,64,8,128]{3,2,1,0:T(8,128)}, f32[16,64,8,128]{3,2,1,0:T(8,128)}) custom-call(f32[8192,128]{1,0:T(8,128)} %signal_ref.1, f32[8192,128]{1,0:T(8,128)} %kernel_ref.1), custom_call_target="tpu_custom_call" | custom-call | tf_op jit(solution)/shard_map/turn/pallas_call | solution.py:300
  9.9 98.1 %all_to_all.20 = f32[16,64,8,128]{3,2,1,0:T(8,128)} all-to-all(f32[16,64,8,128]{3,2,1,0:T(8,128)} %get-tuple-element.10), channel_id=1, replica_groups=mesh['grp'=1,'tm'=16,'chan'=2] {'tm'}, dimensions={0} | all-to-all | bytes 8388608 | tf_op jit(solution)/shard_map/all_to_all | solution.py:542
  108.0 5.7 %all-to-all-start = ((f32[16,64,8,128]{3,2,1,0:T(8,128)}), f32[16,64,8,128]{3,2,1,0:T(8,128)}, u32[]{:S(2)}, u32[]{:S(2)}) async-start(f32[16,64,8,128]{3,2,1,0:T(8,128)} %get-tuple-element.9), calls=%async_computation | async-start | bytes 8388608 | tf_op jit(solution)/shard_map/all_to_all | solution.py:542
  113.7 0.6 dynamic_slice.3.skip_ref
  114.3 27.4 %filter_first.1.rest_6_ = f32[8192,128]{1,0:T(8,128)} custom-call(f32[8]{0:T(128)} %dynamic_slice.3.skip_ref, f32[8192,128]{1,0:T(8,128)} %bitcast.16, bf16[512,768]{1,0:T(8,128)(2,1)} %constant.30.clone.rest_0_, f32[256,512]{1,0:T(8,128)} %constant.31.clone.rest_1_, f32[256,512]{1,0:T(8,128)} %constant.32.clone.rest_2_, ...), custom_call_target="tpu_custom_call" | custom-call | flops 9663676416 | bytes 6291456 | tf_op jit(solution)/shard_map/filter_first/pallas_call | solution.py:400
  141.7 60.1 %all-to-all-done = f32[16,64,8,128]{3,2,1,0:T(8,128)} async-done(((f32[16,64,8,128]{3,2,1,0:T(8,128)}), f32[16,64,8,128]{3,2,1,0:T(8,128)}, u32[]{:S(2)}, u32[]{:S(2)}) %all-to-all-start) | async-done | bytes 4194336 | tf_op jit(solution)/shard_map/all_to_all | solution.py:542
  201.8 28.6 %filter_second.1 = (f32[32,25,8,128]{3,2,1,0:T(8,128)}, f32[32,7,8,128]{3,2,1,0:T(8,128)}) custom-call(f32[8]{0:T(128)} %dynamic_slice.3.skip_ref, f32[8192,128]{1,0:T(8,128)} %bitcast.data_ref, bf16[512,768]{1,0:T(8,128)(2,1)} %constant.30.clone.rest_0_, f32[256,512]{1,0:T(8,128)} %constant.31.clone.rest_1_, f32[256,512]{1,0:T(8,128)} %constant.32.clone.rest_2_, ...), custom_call_target="tpu_custom_call" | custom-call | flops 9663676416 | bytes 6291456 | tf_op jit(solution)/shard_map/filter_second/pallas_call | solution.py:410
  230.4 9.8 %all-to-all-start.3 = ((f32[32,25,8,128]{3,2,1,0:T(8,128)}), f32[32,25,8,128]{3,2,1,0:T(8,128)S(1)}, u32[]{:S(2)}, u32[]{:S(2)}) async-start(f32[32,25,8,128]{3,2,1,0:T(8,128)} %get-tuple-element.12), calls=%async_computation.3 | async-start | bytes 6553600 | tf_op jit(solution)/shard_map/all_to_all | solution.py:545
  240.2 1.2 reshape.24
  241.3 0.9 copy.25
  242.2 1.8 rev.3
  244.0 0.7 pad.4
  244.7 1.1 copy.26
  245.8 0.0 copy-start.1
  245.8 1.5 reduce-precision_convert_fusion.1
  247.3 1.4 pad_maximum_fusion.rest_2_
  248.7 0.7 reduce-precision_convert_fusion.2
  249.4 0.0 copy-done.1
  249.4 0.2 reduce-precision_convert_fusion
  249.6 1.3 pad_maximum_fusion.1.rest_4_
  250.9 61.0 %all-to-all-done.3.conv_ref.edge_ref = f32[32,25,8,128]{3,2,1,0:T(8,128)S(1)} async-done(((f32[32,25,8,128]{3,2,1,0:T(8,128)}), f32[32,25,8,128]{3,2,1,0:T(8,128)S(1)}, u32[]{:S(2)}, u32[]{:S(2)}) %all-to-all-start.3) | async-done | bytes 3276832 | tf_op jit(solution)/shard_map/all_to_all | solution.py:545
  311.9 6.5 %all-to-all-start.2 = ((f32[32,7,8,128]{3,2,1,0:T(8,128)}), f32[32,7,8,128]{3,2,1,0:T(8,128)}, u32[]{:S(2)}, u32[]{:S(2)}) async-start(f32[32,7,8,128]{3,2,1,0:T(8,128)} %get-tuple-element.11), calls=%async_computation.2 | async-start | bytes 1835008 | tf_op jit(solution)/shard_map/all_to_all | solution.py:545
  318.4 0.8 pad_maximum_fusion.2.rest_0_
  319.3 0.1 copy.20
  319.4 0.1 copy.22
  319.5 1.6 maximum_multiply_fusion
  321.0 3.5 collective-permute-start
  324.6 28.9 %mix_late.1.rest_5_ = f32[4096,256]{1,0:T(8,128)} custom-call(f32[32,25,8,128]{3,2,1,0:T(8,128)} %copy-done, f32[32,25,8,128]{3,2,1,0:T(8,128)} %copy-done, f32[4096,256]{1,0:T(8,128)} %gate_ref.3, f32[4096,256]{1,0:T(8,128)} %gate_ref.3, bf16[768,256]{1,0:T(8,128)(2,1)} %pad_maximum_fusion.2.rest_0_, f32[1,256]{1,0:T(1,128)} %bitcast.23, ...), custom_call_target="tpu_custom_call" | custom-call | flops 13287555072 | bytes 9437184 | tf_op jit(solution)/shard_map/mix_late/pallas_call | solution.py:512
  353.4 0.0 all-to-all-done.2.conv_ref
  353.4 0.0 collective-permute-done.halo_ref
  353.5 0.6 copy-done.4
  354.1 11.7 %mix_early.1 = f32[4096,256]{1,0:T(8,128)} custom-call(f32[32,7,8,128]{3,2,1,0:T(8,128)} %all-to-all-done.2.conv_ref, f32[32,25,8,128]{3,2,1,0:T(8,128)} %copy-done, f32[4096,256]{1,0:T(8,128)} %gate_ref.3, f32[128,256]{1,0:T(8,128)} %copy-done.4, bf16[768,256]{1,0:T(8,128)(2,1)} %pad_maximum_fusion.2.rest_0_, ...), custom_call_target="tpu_custom_call", output_to_operand_aliasing={{}: (9, {})} | custom-call | flops 4429185024 | bytes 3145728 | tf_op jit(solution)/shard_map/mix_early/pallas_call | solution.py:512
  (11 shorter events, 0.0 us)
Async XLA Ops:
  108.0 5.7 %copy-start.5 = (f32[256]{0:T(256)S(1)}, f32[256]{0:T(256)}, u32[]{:S(2)}) copy-start(f32[256]{0:T(256)} %param.17) | copy-start | bytes 3076
  108.0 93.8 %all-to-all-start = ((f32[16,64,8,128]{3,2,1,0:T(8,128)}), f32[16,64,8,128]{3,2,1,0:T(8,128)}, u32[]{:S(2)}, u32[]{:S(2)}) async-start(f32[16,64,8,128]{3,2,1,0:T(8,128)} %get-tuple-element.9), calls=%async_computation | async-start | bytes 8388608 | tf_op jit(solution)/shard_map/all_to_all | solution.py:542
  230.4 81.5 %all-to-all-start.3 = ((f32[32,25,8,128]{3,2,1,0:T(8,128)}), f32[32,25,8,128]{3,2,1,0:T(8,128)S(1)}, u32[]{:S(2)}, u32[]{:S(2)}) async-start(f32[32,25,8,128]{3,2,1,0:T(8,128)} %get-tuple-element.12), calls=%async_computation.3 | async-start | bytes 6553600 | tf_op jit(solution)/shard_map/all_to_all | solution.py:545
  245.8 3.6 copy-start.1
  249.4 69.0 %copy-start.2 = (bf16[256,256]{1,0:T(8,128)(2,1)S(1)}, bf16[256,256]{1,0:T(8,128)(2,1)}, u32[]{:S(2)}) copy-start(bf16[256,256]{1,0:T(8,128)(2,1)} %get-tuple-element.17) | copy-start | bytes 393220
  249.4 69.0 %copy-start.3 = (bf16[256,256]{1,0:T(8,128)(2,1)S(1)}, bf16[256,256]{1,0:T(8,128)(2,1)}, u32[]{:S(2)}) copy-start(bf16[256,256]{1,0:T(8,128)(2,1)} %get-tuple-element.18) | copy-start | bytes 393220
  311.9 12.7 %copy-start = (f32[32,25,8,128]{3,2,1,0:T(8,128)}, f32[32,25,8,128]{3,2,1,0:T(8,128)S(1)}, u32[]{:S(2)}) copy-start(f32[32,25,8,128]{3,2,1,0:T(8,128)S(1)} %all-to-all-done.3.conv_ref.edge_ref) | copy-start | bytes 9830404
  311.9 41.6 %all-to-all-start.2 = ((f32[32,7,8,128]{3,2,1,0:T(8,128)}), f32[32,7,8,128]{3,2,1,0:T(8,128)}, u32[]{:S(2)}, u32[]{:S(2)}) async-start(f32[32,7,8,128]{3,2,1,0:T(8,128)} %get-tuple-element.11), calls=%async_computation.2 | async-start | bytes 1835008 | tf_op jit(solution)/shard_map/all_to_all | solution.py:545
  321.0 32.4 %collective-permute-start = (f32[128,256]{1,0:T(8,128)}, f32[128,256]{1,0:T(8,128)S(1)}, u32[]{:S(2)}, u32[]{:S(2)}) collective-permute-start(f32[128,256]{1,0:T(8,128)} %maximum_multiply_fusion), channel_id=1, source_target_pairs={{0,1},{1,2},{2,3},{3,4},{4,5},{5,6},{6,7},{7,8},{8,9},{9,10},{10,1... | collective-permute-start | bytes 393224 | tf_op jit(solution)/shard_map/ppermute | solution.py:552
  353.5 0.7 copy-start.4

commit v3 on v2

--- a/solution.py
+++ b/solution.py
@@ -276,42 +276,70 @@
     )(conv_blocks, gate_input, halo, *fixed)
 
 
-def turn_kernel(signal_ref, kernel_ref, *out_refs):
-    chunk = signal_ref.shape[0]
-    half = 8 // 2
-    for tile in range(chunk // 128):
-        span = slice(tile * 128, (tile + 1) * 128)
-        s = jnp.transpose(signal_ref[span, :], (1, 0))
-        k = jnp.transpose(kernel_ref[span, :], (1, 0))
-        lower = lax.broadcasted_iota(jnp.int32, s.shape, 0) % 8 < half
-        first = jnp.where(lower, s, pltpu.roll(k, half, 0))
-        second = jnp.where(lower, pltpu.roll(s, s.shape[0] - half, 0), k)
-        for ref, value in zip(out_refs, (first, second)):
-            ref[:, tile] = value.reshape(ref.shape[0], 8, 128)
+FIRST_PAIRS = 3
+
+
+def exchange(low, high, distance):
+    count = low.shape[0]
+    lower = lax.broadcasted_iota(jnp.int32, low.shape, 0) % (2 * distance) < distance
+    return (
+        jnp.where(lower, low, pltpu.roll(high, distance, 0)),
+        jnp.where(lower, pltpu.roll(low, count - distance, 0), high),
+    )
+
+
+def turn_kernel(signal_ref, kernel_ref, first_ref, second_ref):
+    groups, pairs = first_ref.shape[:2]
+    for j in range(LANES // 128):
+        parts = []
+        for row in range(2):
+            span = slice(row * LANES + j * 128, row * LANES + (j + 1) * 128)
+            parts.append(jnp.transpose(signal_ref[span, :], (1, 0)))
+            parts.append(jnp.transpose(kernel_ref[span, :], (1, 0)))
+        a0, a2 = exchange(parts[0], parts[2], 4)
+        a1, a3 = exchange(parts[1], parts[3], 4)
+        for q, value in enumerate(exchange(a0, a1, 2) + exchange(a2, a3, 2)):
+            value = value.reshape(groups, 8, 128)
+            if q < pairs:
+                first_ref[:, q, j, 0] = value
+            else:
+                second_ref[:, q - pairs, j, 0] = value
 
 
 def turn(signal, kernel, groups):
     frames, width = signal.shape
-    chunk = 1024
-    tiles = chunk // 128
+    chunk = 2 * LANES
+    steps = frames // chunk
+    lane_tiles = LANES // 128
     block = pl.BlockSpec((chunk, width), lambda i: (i, 0))
-    out_block = pl.BlockSpec((groups, tiles, 8, 128), lambda i: (0, i, 0, 0))
-    shape = jax.ShapeDtypeStruct((groups, frames // 128, 8, 128), F32)
+    counts = (FIRST_PAIRS, 4 - FIRST_PAIRS)
     return pl.pallas_call(
         turn_kernel,
-        grid=(frames // chunk,),
+        grid=(steps,),
         in_specs=[block, block],
-        out_specs=[out_block, out_block],
-        out_shape=[shape, shape],
+        out_specs=[
+            pl.BlockSpec((groups, n, lane_tiles, 1, 8, 128), lambda i: (0, 0, 0, i, 0, 0))
+            for n in counts
+        ],
+        out_shape=[
+            jax.ShapeDtypeStruct((groups, n, lane_tiles, steps, 8, 128), F32) for n in counts
+        ],
         compiler_params=pltpu.CompilerParams(vmem_limit_bytes=VMEM_LIMIT),
         name="turn",
     )(signal, kernel)
 
 
-def gather_channel(ref, slot, rows):
-    tiles = LANES // 128
+def gather_channel(ref, slot):
+    groups, _, lane_tiles, depth, _ = ref.shape
+    rows = depth // 4
     return jnp.concatenate(
-        [ref[pl.ds(8 * j + slot, rows, stride=8 * tiles), :] for j in range(tiles)], axis=1
+        [
+            jnp.concatenate(
+                [ref[g, 0, j, pl.ds(slot, rows, stride=4), :] for g in range(groups)], axis=0
+            )
+            for j in range(lane_tiles)
+        ],
+        axis=1,
     )
 
 
@@ -323,22 +351,21 @@
         )
 
 
-def first_half_kernel(skip_ref, data_ref, *rest):
+def first_channels_kernel(skip_ref, data_ref, *rest):
     *table_refs, out_ref, spread_ref = rest
-    rows = table_refs[1].shape[0]
     c = pl.program_id(0)
     result = filter_channel(
-        gather_channel(data_ref, c, rows), gather_channel(data_ref, c + 4, rows), skip_ref[c],
+        gather_channel(data_ref, c % 2), gather_channel(data_ref, 2 + c % 2), skip_ref[c],
         *table_refs, spread_ref,
     )
     scatter_channel(out_ref, c, result)
 
 
-def second_half_kernel(late, skip_ref, data_ref, *rest):
-    *table_refs, before_ref, late_ref, early_ref, spread_ref, held_ref, sems = rest
-    rows = table_refs[1].shape[0]
+def last_channels_kernel(late, skip_ref, data_ref, *rest):
+    *table_refs, before_ref, _, _, _, _, late_ref, early_ref, spread_ref, held_ref, sems = rest
     c = pl.program_id(0)
-    devices, tiles = late_ref.shape[0], late_ref.shape[1] + early_ref.shape[1]
+    channel = c + 2 * FIRST_PAIRS
+    devices, tiles = late_ref.shape[0], late_ref.shape[1] + early_ref.shape[1] - 1
     load = pltpu.make_async_copy(before_ref, held_ref, sems.at[0])
 
     @pl.when(c == 0)
@@ -346,29 +373,30 @@
         load.start()
 
     result = filter_channel(
-        gather_channel(data_ref, c, rows), gather_channel(data_ref, c + 4, rows),
-        skip_ref[c + 4], *table_refs, spread_ref,
+        gather_channel(data_ref, c % 2), gather_channel(data_ref, 2 + c % 2),
+        skip_ref[channel], *table_refs, spread_ref,
     )
 
     @pl.when(c == 0)
     def _():
         load.wait()
 
-    scatter_channel(held_ref, c + 4, result)
+    scatter_channel(held_ref, channel, result)
 
     @pl.when(c == pl.num_programs(0) - 1)
     def _():
         shaped = held_ref.reshape(devices, tiles, 8, 128)
+        final = shaped.at[:, tiles - 1 : tiles]
+        pairs = (
+            (shaped.at[:, late:tiles], late_ref.at[:, 0 : tiles - late]),
+            (shaped.at[:, late - 1 : late], late_ref.at[:, tiles - late : tiles - late + 1]),
+            (shaped.at[:, 0 : late - 1], early_ref.at[:, 0 : late - 1]),
+            (final.at[0 : devices - 1], early_ref.at[1:devices, late - 1 : late]),
+            (final.at[devices - 1 : devices], early_ref.at[0:1, late - 1 : late]),
+        )
         copies = [
-            pltpu.make_async_copy(
-                shaped.at[:, late:tiles], late_ref.at[:, 0 : tiles - late], sems.at[1]
-            ),
-            pltpu.make_async_copy(
-                shaped.at[:, late - 1 : late],
-                late_ref.at[:, tiles - late : tiles - late + 1],
-                sems.at[2],
-            ),
-            pltpu.make_async_copy(shaped.at[:, 0 : late - 1], early_ref, sems.at[3]),
+            pltpu.make_async_copy(here, there, sems.at[1 + i])
+            for i, (here, there) in enumerate(pairs)
         ]
         for copy in copies:
             copy.start()
@@ -376,49 +404,56 @@
             copy.wait()
 
 
-def filter_half(data, skip, before, devices, late):
-    flat = data.reshape(-1, 128)
-    rows = flat.shape[0] // (8 * (LANES // 128))
-    tiles = flat.shape[0] // (8 * devices)
+def filter_pairs(data, skip, before, devices, late, ready=()):
+    groups, pairs, lane_tiles, row_pairs, _, _ = data.shape
+    flat = data.reshape(groups, pairs, lane_tiles, row_pairs * 8, 128)
+    rows = groups * row_pairs * 2
+    tiles = rows * lane_tiles // devices
     held = tables(rows)
+    held_shape = (rows * lane_tiles * 8, 128)
 
     def whole(array):
         return pl.BlockSpec(array.shape, lambda c: (0,) * array.ndim)
 
-    in_specs = [pl.BlockSpec(memory_space=pltpu.SMEM), whole(flat)] + [whole(t) for t in held]
+    in_specs = [
+        pl.BlockSpec(memory_space=pltpu.SMEM),
+        pl.BlockSpec(
+            (groups, 1, lane_tiles, row_pairs * 8, 128), lambda c: (0, c // 2, 0, 0, 0)
+        ),
+    ] + [whole(t) for t in held]
     spread = pltpu.VMEM((RADIX, 2 * rows, 6 * SUB), BF16)
     options = dict(
-        grid=(4,),
+        grid=(2 * pairs,),
         compiler_params=pltpu.CompilerParams(vmem_limit_bytes=VMEM_LIMIT),
         cost_estimate=pl.CostEstimate(
-            flops=4 * rows * LANES * 2048 * 3 * 3,
-            bytes_accessed=4 * rows * LANES * 12,
+            flops=2 * pairs * rows * LANES * 2048 * 3 * 3,
+            bytes_accessed=2 * pairs * rows * LANES * 12,
             transcendentals=0,
         ),
     )
     if before is None:
         return pl.pallas_call(
-            first_half_kernel,
+            first_channels_kernel,
             in_specs=in_specs,
-            out_specs=whole(flat),
-            out_shape=jax.ShapeDtypeStruct(flat.shape, F32),
+            out_specs=pl.BlockSpec(held_shape, lambda c: (0, 0)),
+            out_shape=jax.ShapeDtypeStruct(held_shape, F32),
             scratch_shapes=[spread],
             name="filter_first",
             **options,
         )(skip, flat, *held)
     anywhere = pl.BlockSpec(memory_space=pl.ANY)
     return pl.pallas_call(
-        functools.partial(second_half_kernel, late),
-        in_specs=in_specs + [anywhere],
+        functools.partial(last_channels_kernel, late),
+        in_specs=in_specs + [anywhere] * (1 + len(ready)),
         out_specs=[anywhere, anywhere],
         out_shape=[
             jax.ShapeDtypeStruct((devices, tiles - late + 1, 8, 128), F32),
-            jax.ShapeDtypeStruct((devices, late - 1, 8, 128), F32),
+            jax.ShapeDtypeStruct((devices, late, 8, 128), F32),
         ],
-        scratch_shapes=[spread, pltpu.VMEM(flat.shape, F32), pltpu.SemaphoreType.DMA((4,))],
-        name="filter_second",
+        scratch_shapes=[spread, pltpu.VMEM(held_shape, F32), pltpu.SemaphoreType.DMA((6,))],
+        name="filter_last",
         **options,
-    )(skip, flat, *held, before)
+    )(skip, flat, *held, before, *ready)
 
 
 def frames_by_channels(tile):
@@ -449,7 +484,7 @@
     mix_block(window_ref, *fixed, out_ref, high_ref, low_ref, mix_ref)
 
 
-def early_kernel(conv_ref, edge_ref, gate_ref, halo_ref, *rest):
+def early_kernel(conv_ref, edge_ref, gate_ref, halo_ref, halo_gate_ref, *rest):
     *fixed, _, out_ref, window_ref, high_ref, low_ref, mix_ref = rest
     block = gate_ref.shape[0]
     reach = TAPS + 1
@@ -457,7 +492,7 @@
 
     @pl.when(pl.program_id(0) == 0)
     def _():
-        window_ref[:reach, :] = halo_ref[...]
+        window_ref[:reach, :] = frames_by_channels(halo_ref[:, 0]) * halo_gate_ref[...]
 
     @pl.when(pl.program_id(0) > 0)
     def _():
@@ -475,7 +510,7 @@
     mix_block(window_ref, *fixed, out_ref, high_ref, low_ref, mix_ref)
 
 
-def tail_part(conv, late, gate_input, halo, before, late_tiles, fixed):
+def tail_part(conv, late, gate_input, halo_gate, before, late_tiles, fixed):
     devices = conv.shape[0]
     frames, width = gate_input.shape
     reach = TAPS + 1
@@ -496,8 +531,9 @@
     ]
     operands = [conv, late, gate_input]
     if first:
-        in_specs += [whole(halo)]
-        operands += [halo]
+        ahead = late_tiles - 1
+        in_specs += [pl.BlockSpec((devices, 1, 8, 128), lambda r: (0, ahead, 0, 0)), whole(halo_gate)]
+        operands += [conv, halo_gate]
     else:
         in_specs += [pl.BlockSpec((reach, width), lambda r: (late_tiles - 1, 0))]
         operands += [gate_input]
@@ -544,15 +580,16 @@
     def leave(array):
         return lax.all_to_all(array, ("tm", "chan"), split_axis=0, concat_axis=0, tiled=True)
 
+    ring = [(i, i + 1) for i in range(devices - 1)]
+    halo_gate = lax.ppermute(gate_input[-reach:], ("tm", "chan"), ring)
     one, two = turn(signal, kernel, groups)
-    before = filter_half(enter(one), skip_here, None, devices, late_tiles)
-    late, early = filter_half(enter(two), skip_here, before, devices, late_tiles)
+    before = filter_pairs(enter(one), skip_here, None, devices, late_tiles)
+    ready = (fixed[0], fixed[2], fixed[4], halo_gate)
+    late, early = filter_pairs(enter(two), skip_here, before, devices, late_tiles, ready)
     late = leave(late)
-    final = frames_by_channels(late[:, late.shape[1] - 2]) * gate_input[-reach:]
-    halo = lax.ppermute(final, ("tm", "chan"), [(i, i + 1) for i in range(devices - 1)])
     early = leave(early)
     part = tail_part(late, late, gate_input, None, None, late_tiles, fixed)
-    return tail_part(early, late, gate_input, halo, part, late_tiles, fixed)
+    return tail_part(early, late, gate_input, halo_gate, part, late_tiles, fixed)
 
 
 def on_device(

time: 368 us -> 353 us (0.959)
  blocking collectives: 98.1 us -> 221 us
  waiting for transfers between devices: 121 us -> 0.01 us
  starting transfers between devices: 25.5 us -> 15.5 us
  Pallas kernels: 106 us -> 102 us
    all_to_all x0 -> x1, blocking collectives: none -> 78.1 us  [leave(): lax.all_to_all(array, ('tm', 'chan'), split_axis=0, concat_axis=0, tiled=...]
    all_to_all x2 -> x1, waiting for transfers between devices: 61 us -> 0.01 us  [leave(): lax.all_to_all(array, ('tm', 'chan'), split_axis=0, concat_axis=0, tiled=...]
    all_to_all x1, waiting for transfers between devices: 60.1 us -> 0.01 us  [enter(): return lax.all_to_all(array, 'tm', split_axis=0, concat_axis=0, tiled=True)]
    all_to_all x1, blocking collectives: 98.1 us -> 143 us  [enter(): return lax.all_to_all(array, 'tm', split_axis=0, concat_axis=0, tiled=True)]
    all_to_all x2 -> x1, starting transfers between devices: 16.3 us -> 4.81 us  [leave(): lax.all_to_all(array, ('tm', 'chan'), split_axis=0, concat_axis=0, tiled=...]
    pallas_call x3, Pallas kernels: 65.9 us -> 61.4 us  [the longest x1 35.4 us: filter_pairs(): pl.pallas_call(first_channels_kernel, in_specs=in_specs, out_specs=pl.Blo...]
  transfers between devices with their start and end apart: 4 -> 3, of which waited for: 2 -> 0; matrix products, arithmetic and copies ran while one was open for 4% -> 3% of each run, Pallas kernels for 15% -> 18%
where the time goes in v3:
time: 353 us; the launch traced here: 351 us
  blocking collectives  221 us (63%)
  Pallas kernels  102 us (29%)
  starting transfers between devices  15.5 us (4%)
  other arithmetic  5.99 us (2%)
  local copies, waits for them, and re-layouts  5.91 us (2%)
    all_to_all x1, blocking collectives, enter(): return lax.all_to_all(array, 'tm', split_axis=0, concat_axis=0, tiled=True)  143 us
    all_to_all x1, blocking collectives, leave(): lax.all_to_all(array, ('tm', 'chan'), split_axis=0, concat_axis=0, tiled=...  78.1 us
    pallas_call x2, Pallas kernels, tail_part(): pl.pallas_call(early_kernel if first else late_kernel, grid=(count,), in_...  40.7 us
    pallas_call x1, Pallas kernels, filter_pairs(): pl.pallas_call(first_channels_kernel, in_specs=in_specs, out_specs=pl.Blo...  35.4 us
    pallas_call x1, Pallas kernels, filter_pairs(): pl.pallas_call(functools.partial(last_channels_kernel, late), in_specs=in...  16 us
    pallas_call x1, Pallas kernels, turn(): pl.pallas_call(turn_kernel, grid=(steps,), in_specs=[block, block], out_s...  9.99 us
  transfers between devices with their start and end apart: 3, of which 0 were waited for; matrix products, arithmetic and copies ran while one was open for 3% of the time, Pallas kernels for 18%

profile of v3, /device:TPU:11, one launch (start us, length us, event | category | flops | bytes accessed | tf_op | source)
XLA Modules:
  0.0 350.7 jit_solution(16876547968971351544)
XLA Ops:
  0.0 10.0 %turn.1 = (f32[16,3,4,8,8,128]{5,4,3,2,1,0:T(8,128)}, f32[16,1,4,8,8,128]{5,4,3,2,1,0:T(8,128)}) custom-call(f32[8192,128]{1,0:T(8,128)} %signal_ref.1, f32[8192,128]{1,0:T(8,128)} %kernel_ref.1), custom_call_target="tpu_custom_call" | custom-call | tf_op jit(solution)/shard_map/turn/pallas_call | solution.py:316
  10.0 143.0 %all_to_all.20 = f32[16,3,4,8,8,128]{5,4,3,2,1,0:T(8,128)} all-to-all(f32[16,3,4,8,8,128]{5,4,3,2,1,0:T(8,128)} %get-tuple-element.10), channel_id=1, replica_groups=mesh['grp'=1,'tm'=16,'chan'=2] {'tm'}, dimensions={0} | all-to-all | bytes 12582912 | tf_op jit(solution)/shard_map/all_to_all | solution.py:578
  153.0 5.7 %all-to-all-start = ((f32[16,1,4,8,8,128]{5,4,3,2,1,0:T(8,128)}), f32[16,1,4,8,8,128]{5,4,3,2,1,0:T(8,128)S(1)}, u32[]{:S(2)}, u32[]{:S(2)}) async-start(f32[16,1,4,8,8,128]{5,4,3,2,1,0:T(8,128)} %get-tuple-element.9), calls=%async_computation | async-start | bytes 4194304 | tf_op jit(solution)/shard_map/all_to_all | solution.py:578
  158.7 1.6 slice.3
  160.3 5.0 %collective-permute-start = (f32[128,256]{1,0:T(8,128)}, f32[128,256]{1,0:T(8,128)S(1)}, u32[]{:S(2)}, u32[]{:S(2)}) collective-permute-start(f32[128,256]{1,0:T(8,128)} %slice.3), channel_id=1, source_target_pairs={{0,1},{1,2},{2,3},{3,4},{4,5},{5,6},{6,7},{7,8},{8,9},{9,10},{10,1... | collective-permute-start | bytes 393224 | tf_op jit(solution)/shard_map/ppermute | solution.py:584
  165.3 0.0 copy-done.3
  165.3 0.2 reshape.24
  165.5 0.2 copy.19
  165.6 0.2 rev.3
  165.9 0.0 copy-start.2
  165.9 0.8 copy.20
  166.7 0.0 copy-done.5
  166.7 0.6 dynamic_slice.3.skip_ref
  167.3 1.0 reduce-precision_convert_fusion.2
  168.3 0.8 pad_maximum_fusion.2.rest_7_.rest_0_
  169.1 1.4 reduce-precision_convert_fusion.1
  170.5 1.3 pad_maximum_fusion.rest_8_.rest_2_
  171.8 0.0 copy-done.2
  171.8 0.2 reduce-precision_convert_fusion
  172.0 1.3 pad_maximum_fusion.1.rest_9_.rest_4_
  173.3 35.4 %filter_first.1.rest_6_ = f32[8192,128]{1,0:T(8,128)} custom-call(f32[8]{0:T(128)} %dynamic_slice.3.skip_ref, f32[16,3,4,64,128]{4,3,2,1,0:T(8,128)} %bitcast.5, bf16[512,768]{1,0:T(8,128)(2,1)} %constant.30.clone.rest_0_, f32[256,512]{1,0:T(8,128)} %constant.31.clone.rest_1_, f32[256,512]{1,0:T(8,128)} %constant.32.clone.rest_2_, ...), custom_call_target="tpu_custom_call" | custom-call | flops 14495514624 | bytes 9437184 | tf_op jit(solution)/shard_map/filter_first/pallas_call | solution.py:435
  208.7 0.0 collective-permute-done.rest_10_.halo_gate_ref
  208.8 0.0 all-to-all-done
  208.8 0.6 copy-done.4
  209.4 0.7 copy-done.1
  210.1 16.0 %filter_last.1 = (f32[32,25,8,128]{3,2,1,0:T(8,128)}, f32[32,8,8,128]{3,2,1,0:T(8,128)}) custom-call(f32[8]{0:T(128)} %dynamic_slice.3.skip_ref, f32[16,1,4,64,128]{4,3,2,1,0:T(8,128)} %bitcast.6, bf16[512,768]{1,0:T(8,128)(2,1)} %constant.30.clone.rest_0_, f32[256,512]{1,0:T(8,128)} %constant.31.clone.rest_1_, f32[256,512]{1,0:T(8,128)} %constant.32.clone.rest_2_, ...), custom_call_target="tpu_custom_call" | custom-call | flops 4831838208 | bytes 3145728 | tf_op jit(solution)/shard_map/filter_last/pallas_call | solution.py:445
  226.1 78.1 %all_to_all.21.conv_ref.edge_ref = f32[32,25,8,128]{3,2,1,0:T(8,128)} all-to-all(f32[32,25,8,128]{3,2,1,0:T(8,128)} %get-tuple-element.12), channel_id=1, replica_groups=mesh['grp'=1,'tm'=16,'chan'=2] {'tm','chan'}, dimensions={0} | all-to-all | bytes 6553600 | tf_op jit(solution)/shard_map/all_to_all | solution.py:581
  304.2 4.8 %all-to-all-start.2 = ((f32[32,8,8,128]{3,2,1,0:T(8,128)}), f32[32,8,8,128]{3,2,1,0:T(8,128)S(1)}, u32[]{:S(2)}, u32[]{:S(2)}) async-start(f32[32,8,8,128]{3,2,1,0:T(8,128)} %get-tuple-element.11), calls=%async_computation.2 | async-start | bytes 2097152 | tf_op jit(solution)/shard_map/all_to_all | solution.py:581
  309.0 28.9 %mix_late.1.rest_5_ = f32[4096,256]{1,0:T(8,128)} custom-call(f32[32,25,8,128]{3,2,1,0:T(8,128)} %all_to_all.21.conv_ref.edge_ref, f32[32,25,8,128]{3,2,1,0:T(8,128)} %all_to_all.21.conv_ref.edge_ref, f32[4096,256]{1,0:T(8,128)} %gate_ref.3, f32[4096,256]{1,0:T(8,128)} %gate_ref.3, bf16[768,256]{1,0:T(8,128)(2,1)} %pad_maximum_fusion.2.rest_7_.rest_0_, ...), custom_call_target="tpu_custom_call" | custom-call | flops 13287555072 | bytes 9437184 | tf_op jit(solution)/shard_map/mix_late/pallas_call | solution.py:548
  337.9 0.0 all-to-all-done.2.conv_ref.halo_ref
  337.9 1.0 copy-done
  338.9 11.8 %mix_early.1 = f32[4096,256]{1,0:T(8,128)} custom-call(f32[32,8,8,128]{3,2,1,0:T(8,128)} %copy-done, f32[32,25,8,128]{3,2,1,0:T(8,128)} %all_to_all.21.conv_ref.edge_ref, f32[4096,256]{1,0:T(8,128)} %gate_ref.3, f32[32,8,8,128]{3,2,1,0:T(8,128)} %copy-done, f32[128,256]{1,0:T(8,128)} %copy-done.4, ...), custom_call_target="tpu_custom_call", output_to_operand_aliasing={{}: (10, {})} | custom-call | flops 4429185024 | bytes 3145728 | tf_op jit(solution)/shard_map/mix_early/pallas_call | solution.py:548
  (6 shorter events, 0.0 us)
Async XLA Ops:
  153.0 12.2 %copy-start.3 = (f32[256,254]{1,0:T(8,128)S(1)}, f32[256,254]{1,0:T(8,128)}, u32[]{:S(2)}) copy-start(f32[256,254]{1,0:T(8,128)} %param.19) | copy-start | bytes 780292
  153.0 13.7 %copy-start.5 = (f32[256]{0:T(256)S(1)}, f32[256]{0:T(256)}, u32[]{:S(2)}) copy-start(f32[256]{0:T(256)} %param.17) | copy-start | bytes 3076
  153.0 55.7 %all-to-all-start = ((f32[16,1,4,8,8,128]{5,4,3,2,1,0:T(8,128)}), f32[16,1,4,8,8,128]{5,4,3,2,1,0:T(8,128)S(1)}, u32[]{:S(2)}, u32[]{:S(2)}) async-start(f32[16,1,4,8,8,128]{5,4,3,2,1,0:T(8,128)} %get-tuple-element.9), calls=%async_computation | async-start | bytes 4194304 | tf_op jit(solution)/shard_map/all_to_all | solution.py:578
  160.3 48.5 %collective-permute-start = (f32[128,256]{1,0:T(8,128)}, f32[128,256]{1,0:T(8,128)S(1)}, u32[]{:S(2)}, u32[]{:S(2)}) collective-permute-start(f32[128,256]{1,0:T(8,128)} %slice.3), channel_id=1, source_target_pairs={{0,1},{1,2},{2,3},{3,4},{4,5},{5,6},{6,7},{7,8},{8,9},{9,10},{10,1... | collective-permute-start | bytes 393224 | tf_op jit(solution)/shard_map/ppermute | solution.py:584
  165.9 6.0 %copy-start.2 = (f32[1024,256]{1,0:T(8,128)S(1)}, f32[1024,256]{1,0:T(8,128)}, u32[]{:S(2)}) copy-start(f32[1024,256]{1,0:T(8,128)} %param.23) | copy-start | bytes 3145732
  208.7 0.6 copy-start.4
  208.8 1.4 copy-start.1
  304.2 33.7 %all-to-all-start.2 = ((f32[32,8,8,128]{3,2,1,0:T(8,128)}), f32[32,8,8,128]{3,2,1,0:T(8,128)S(1)}, u32[]{:S(2)}, u32[]{:S(2)}) async-start(f32[32,8,8,128]{3,2,1,0:T(8,128)} %get-tuple-element.11), calls=%async_computation.2 | async-start | bytes 2097152 | tf_op jit(solution)/shard_map/all_to_all | solution.py:581
  337.9 1.0 copy-start

commit v4 on v3

--- a/solution.py
+++ b/solution.py
@@ -74,10 +74,11 @@
 
 
 def filter_channel(signal, kernel, skip, enter_ref, cos_ref, sin_ref, forward_ref, backward_ref,
-                   leave_ref, spread_ref):
+                   leave_ref):
     rows = cos_ref.shape[0]
-    for index, value in enumerate((signal, kernel)):
-        turned = dot(enter_ref[...], split_cat(value, 0))
+    entered = [dot(enter_ref[...], split_cat(value, 0)) for value in (signal, kernel)]
+    spectra = []
+    for turned in entered:
         real_in, imag_in = turned[:rows], turned[rows:]
         real = real_in * cos_ref[...] + imag_in * sin_ref[...]
         imag = imag_in * cos_ref[...] - real_in * sin_ref[...]
@@ -86,17 +87,19 @@
         er, ei, fr, fi = r0 + r2, i0 + i2, r0 - r2, i0 - i2
         gr, gi, hr, hi = r1 + r3, i1 + i3, r1 - r3, i1 - i3
         spread = ((er + gr, ei + gi), (fr + hi, fi - hr), (er - gr, ei - gi), (fr - hi, fi + hr))
-        for r, pair in enumerate(spread):
-            spread_ref[r, index * rows : (index + 1) * rows, :] = split_cat(
-                jnp.concatenate(pair, axis=1), 1
-            )
+        spectra.append([
+            dot(split_cat(jnp.concatenate(pair, axis=1), 1), forward_ref[r])
+            for r, pair in enumerate(spread)
+        ])
+    products = []
+    for s, k in zip(*spectra):
+        sr, si = s[:, :SUB], s[:, SUB:]
+        kr, ki = k[:, :SUB], k[:, SUB:]
+        product = jnp.concatenate([sr * kr - si * ki, sr * ki + si * kr], axis=1)
+        products.append(split_cat(product, 1))
     back = []
     for r in range(RADIX):
-        both = dot(spread_ref[r], forward_ref[r])
-        sr, si = both[:rows, :SUB], both[:rows, SUB:]
-        kr, ki = both[rows:, :SUB], both[rows:, SUB:]
-        product = jnp.concatenate([sr * kr - si * ki, sr * ki + si * kr], axis=1)
-        turned = dot(split_cat(product, 1), backward_ref[r])
+        turned = dot(products[r], backward_ref[r])
         back.append((turned[:, :SUB], turned[:, SUB:]))
     (r0, i0), (r1, i1), (r2, i2), (r3, i3) = back
     er, ei, fr, fi = r0 + r2, i0 + i2, r0 - r2, i0 - i2
@@ -112,13 +115,13 @@
 
 def filter_kernel(
     skip_ref, signal_ref, kernel_ref, enter_ref, cos_ref, sin_ref, forward_ref, backward_ref,
-    leave_ref, out_ref, spread_ref,
+    leave_ref, out_ref,
 ):
     rows = cos_ref.shape[0]
     result = filter_channel(
         signal_ref[...].reshape(rows, LANES), kernel_ref[...].reshape(rows, LANES),
         skip_ref[pl.program_id(0)], enter_ref, cos_ref, sin_ref, forward_ref, backward_ref,
-        leave_ref, spread_ref,
+        leave_ref,
     )
     out_ref[...] = result.reshape(out_ref.shape)
 
@@ -154,7 +157,6 @@
         + [whole(table) for table in held],
         out_specs=pl.BlockSpec(out_block, along),
         out_shape=jax.ShapeDtypeStruct(out_shape, F32),
-        scratch_shapes=[pltpu.VMEM((RADIX, 2 * rows, 6 * SUB), BF16)],
         compiler_params=pltpu.CompilerParams(vmem_limit_bytes=VMEM_LIMIT),
         cost_estimate=pl.CostEstimate(
             flops=channels * rows * LANES * 2048 * 3 * 3,
@@ -169,8 +171,21 @@
     return result
 
 
-def mix_block(window_ref, tap_ref, gain_ref, up_ref, bias_ref, down_ref, out_ref, high_ref, low_ref,
-              mix_ref):
+def split_weights(tap_ref, up_ref, down_ref, taps_ref, ups_ref, downs_ref):
+    def stacked(weight):
+        high, low = halves(weight)
+        return jnp.concatenate([high, high, low], axis=0)
+
+    taps_ref[...] = stacked(tap_ref[...])
+    chunks, _, chunk = ups_ref.shape
+    for n in range(chunks):
+        span = slice(n * chunk, (n + 1) * chunk)
+        ups_ref[n] = stacked(up_ref[:, span])
+        downs_ref[n] = stacked(down_ref[span, :])
+
+
+def mix_block(window_ref, gain_ref, bias_ref, out_ref, high_ref, low_ref, mix_ref, taps_ref, ups_ref,
+              downs_ref):
     block, width = out_ref.shape
     reach = TAPS + 1
     head_width = width // HEADS
@@ -178,7 +193,7 @@
     high_ref[...] = high
     low_ref[...] = low
     taps = dot(
-        jnp.concatenate([high[reach:], low[reach:], high[reach:]], axis=1), tap_ref[...]
+        jnp.concatenate([high[reach:], low[reach:], high[reach:]], axis=1), taps_ref[...]
     )
     for b in range(block // reach):
         for h in range(HEADS):
@@ -194,17 +209,45 @@
             )
     mixed = mix_ref[...]
     mean_square = jnp.mean(mixed * mixed, axis=1, keepdims=True)
-    normed = mixed * lax.rsqrt(mean_square + EPSILON) * gain_ref[...]
-    raised = dot(split_cat(normed, 1), up_ref[...]) + bias_ref[...]
-    inner = math.sqrt(2.0 / math.pi) * (raised + 0.044715 * (raised * raised * raised))
-    hidden = 0.5 * raised * (1.0 + jnp.tanh(inner))
-    out_ref[...] = mixed + dot(split_cat(hidden, 1), down_ref[...])
-
-
-def mix_kernel(
-    conv_ref, gate_ref, halo_ref, tap_ref, gain_ref, up_ref, bias_ref, down_ref, out_ref,
-    window_ref, high_ref, low_ref, mix_ref,
-):
+    normed = split_cat(mixed * lax.rsqrt(mean_square + EPSILON) * gain_ref[...], 1)
+    total = mixed
+    chunks, _, chunk = ups_ref.shape
+    scale = math.sqrt(2.0 / math.pi)
+    for n in range(chunks):
+        raised = dot(normed, ups_ref[n]) + bias_ref[:, n * chunk : (n + 1) * chunk]
+        inner = raised * (scale + (scale * 0.044715) * (raised * raised))
+        half = 0.5 * raised
+        total = total + dot(split_cat(half + half * jnp.tanh(inner), 1), downs_ref[n])
+    out_ref[...] = total
+
+
+def mix_scratch(block, width, hidden):
+    reach = TAPS + 1
+    chunk = 256 if hidden % 256 == 0 else hidden
+    return [
+        pltpu.VMEM((block + reach, width), F32),
+        pltpu.VMEM((block + reach, width), BF16),
+        pltpu.VMEM((block + reach, width), BF16),
+        pltpu.VMEM((block, width), F32),
+        pltpu.VMEM((3 * width, HEADS * reach), BF16),
+        pltpu.VMEM((hidden // chunk, 3 * width, chunk), BF16),
+        pltpu.VMEM((hidden // chunk, 3 * chunk, width), BF16),
+    ]
+
+
+def mix_window(window_ref, fixed, scratch, out_ref):
+    tap_ref, gain_ref, up_ref, bias_ref, down_ref = fixed
+    weights = scratch[3:]
+
+    @pl.when(pl.program_id(0) == 0)
+    def _():
+        split_weights(tap_ref, up_ref, down_ref, *weights)
+
+    mix_block(window_ref, gain_ref, bias_ref, out_ref, *scratch)
+
+
+def mix_kernel(conv_ref, gate_ref, halo_ref, *rest):
+    fixed, out_ref, window_ref, scratch = rest[:5], rest[5], rest[6], rest[7:]
     block = gate_ref.shape[0]
     reach = TAPS + 1
 
@@ -217,15 +260,7 @@
         window_ref[:reach, :] = window_ref[block : block + reach, :]
 
     window_ref[reach:, :] = jnp.transpose(conv_ref[0], (1, 0)) * gate_ref[...]
-    mix_block(
-        window_ref, tap_ref, gain_ref, up_ref, bias_ref, down_ref, out_ref, high_ref, low_ref, mix_ref
-    )
-
-
-def weight_split(weight):
-    high = lax.reduce_precision(weight, 8, 7)
-    low = weight - high
-    return jnp.concatenate([high, high, low], axis=0).astype(BF16)
+    mix_window(window_ref, fixed, scratch, out_ref)
 
 
 def fixed_operands(tap_weight, norm_gain, up_weight, up_bias, down_weight):
@@ -233,11 +268,11 @@
     taps = tap_weight.reshape(width, HEADS, TAPS)[:, :, ::-1]
     taps = jnp.pad(taps, ((0, 0), (0, 0), (1, 0))).reshape(width, HEADS * (TAPS + 1))
     return (
-        weight_split(taps),
+        taps,
         norm_gain.reshape(1, -1),
-        weight_split(up_weight),
+        up_weight,
         up_bias.reshape(1, -1),
-        weight_split(down_weight),
+        down_weight,
     )
 
 
@@ -260,12 +295,7 @@
         + [whole(array) for array in fixed],
         out_specs=pl.BlockSpec((block, width), lambda r: (r, 0)),
         out_shape=jax.ShapeDtypeStruct(gate_input.shape, F32),
-        scratch_shapes=[
-            pltpu.VMEM((block + reach, width), F32),
-            pltpu.VMEM((block + reach, width), BF16),
-            pltpu.VMEM((block + reach, width), BF16),
-            pltpu.VMEM((block, width), F32),
-        ],
+        scratch_shapes=mix_scratch(block, width, hidden),
         compiler_params=pltpu.CompilerParams(vmem_limit_bytes=VMEM_LIMIT),
         cost_estimate=pl.CostEstimate(
             flops=count * block * 3 * 2 * (2 * width * hidden + 3 * width * width),
@@ -276,70 +306,54 @@
     )(conv_blocks, gate_input, halo, *fixed)
 
 
-FIRST_PAIRS = 3
-
-
-def exchange(low, high, distance):
-    count = low.shape[0]
-    lower = lax.broadcasted_iota(jnp.int32, low.shape, 0) % (2 * distance) < distance
-    return (
-        jnp.where(lower, low, pltpu.roll(high, distance, 0)),
-        jnp.where(lower, pltpu.roll(low, count - distance, 0), high),
-    )
+FIRST_CHANNELS = 7
+TURN_ROWS = 4
 
 
 def turn_kernel(signal_ref, kernel_ref, first_ref, second_ref):
-    groups, pairs = first_ref.shape[:2]
-    for j in range(LANES // 128):
-        parts = []
-        for row in range(2):
+    groups, early, rows = first_ref.shape[:3]
+    late = second_ref.shape[1]
+    stride = rows * 8
+    first = first_ref.reshape(groups * early * stride, 128)
+    second = second_ref.reshape(groups * late * stride, 128)
+    for row in range(rows):
+        for j in range(LANES // 128):
             span = slice(row * LANES + j * 128, row * LANES + (j + 1) * 128)
-            parts.append(jnp.transpose(signal_ref[span, :], (1, 0)))
-            parts.append(jnp.transpose(kernel_ref[span, :], (1, 0)))
-        a0, a2 = exchange(parts[0], parts[2], 4)
-        a1, a3 = exchange(parts[1], parts[3], 4)
-        for q, value in enumerate(exchange(a0, a1, 2) + exchange(a2, a3, 2)):
-            value = value.reshape(groups, 8, 128)
-            if q < pairs:
-                first_ref[:, q, j, 0] = value
-            else:
-                second_ref[:, q - pairs, j, 0] = value
+            for which, ref in enumerate((signal_ref, kernel_ref)):
+                turned = jnp.transpose(ref[span, :], (1, 0))
+                place = row * 8 + j * 2 + which
+                for g in range(groups):
+                    own = turned[g * 8 : (g + 1) * 8]
+                    first[pl.ds(g * early * stride + place, early, stride=stride), :] = own[:early]
+                    second[pl.ds(g * late * stride + place, late, stride=stride), :] = own[early:]
 
 
 def turn(signal, kernel, groups):
     frames, width = signal.shape
-    chunk = 2 * LANES
-    steps = frames // chunk
-    lane_tiles = LANES // 128
+    chunk = TURN_ROWS * LANES
+    rows = frames // LANES
     block = pl.BlockSpec((chunk, width), lambda i: (i, 0))
-    counts = (FIRST_PAIRS, 4 - FIRST_PAIRS)
+    counts = (FIRST_CHANNELS, 8 - FIRST_CHANNELS)
     return pl.pallas_call(
         turn_kernel,
-        grid=(steps,),
+        grid=(frames // chunk,),
         in_specs=[block, block],
         out_specs=[
-            pl.BlockSpec((groups, n, lane_tiles, 1, 8, 128), lambda i: (0, 0, 0, i, 0, 0))
-            for n in counts
+            pl.BlockSpec((groups, n, TURN_ROWS, 8, 128), lambda i: (0, 0, i, 0, 0)) for n in counts
         ],
-        out_shape=[
-            jax.ShapeDtypeStruct((groups, n, lane_tiles, steps, 8, 128), F32) for n in counts
-        ],
+        out_shape=[jax.ShapeDtypeStruct((groups, n, rows, 8, 128), F32) for n in counts],
         compiler_params=pltpu.CompilerParams(vmem_limit_bytes=VMEM_LIMIT),
         name="turn",
     )(signal, kernel)
 
 
-def gather_channel(ref, slot):
-    groups, _, lane_tiles, depth, _ = ref.shape
-    rows = depth // 4
+def gather_channel(ref, which):
+    groups, _, depth, _ = ref.shape
+    tiles = LANES // 128
+    flat = ref.reshape(groups * depth, 128)
+    rows = groups * depth // 8
     return jnp.concatenate(
-        [
-            jnp.concatenate(
-                [ref[g, 0, j, pl.ds(slot, rows, stride=4), :] for g in range(groups)], axis=0
-            )
-            for j in range(lane_tiles)
-        ],
-        axis=1,
+        [flat[pl.ds(2 * j + which, rows, stride=8), :] for j in range(tiles)], axis=1
     )
 
 
@@ -352,19 +366,20 @@
 
 
 def first_channels_kernel(skip_ref, data_ref, *rest):
-    *table_refs, out_ref, spread_ref = rest
+    *table_refs, out_ref = rest
     c = pl.program_id(0)
     result = filter_channel(
-        gather_channel(data_ref, c % 2), gather_channel(data_ref, 2 + c % 2), skip_ref[c],
-        *table_refs, spread_ref,
+        gather_channel(data_ref, 0), gather_channel(data_ref, 1), skip_ref[c],
+        *table_refs,
     )
     scatter_channel(out_ref, c, result)
 
 
-def last_channels_kernel(late, skip_ref, data_ref, *rest):
-    *table_refs, before_ref, _, _, _, _, late_ref, early_ref, spread_ref, held_ref, sems = rest
+def last_channels_kernel(late, extra, skip_ref, data_ref, *rest):
+    *table_refs, before_ref = rest[: len(rest) - 4 - extra]
+    late_ref, early_ref, held_ref, sems = rest[-4:]
     c = pl.program_id(0)
-    channel = c + 2 * FIRST_PAIRS
+    channel = c + FIRST_CHANNELS
     devices, tiles = late_ref.shape[0], late_ref.shape[1] + early_ref.shape[1] - 1
     load = pltpu.make_async_copy(before_ref, held_ref, sems.at[0])
 
@@ -373,8 +388,8 @@
         load.start()
 
     result = filter_channel(
-        gather_channel(data_ref, c % 2), gather_channel(data_ref, 2 + c % 2),
-        skip_ref[channel], *table_refs, spread_ref,
+        gather_channel(data_ref, 0), gather_channel(data_ref, 1),
+        skip_ref[channel], *table_refs,
     )
 
     @pl.when(c == 0)
@@ -404,10 +419,11 @@
             copy.wait()
 
 
-def filter_pairs(data, skip, before, devices, late, ready=()):
-    groups, pairs, lane_tiles, row_pairs, _, _ = data.shape
-    flat = data.reshape(groups, pairs, lane_tiles, row_pairs * 8, 128)
-    rows = groups * row_pairs * 2
+def filter_channels(data, skip, before, devices, late, ready=()):
+    groups, channels, group_rows, _, _ = data.shape
+    flat = data.reshape(groups, channels, group_rows * 8, 128)
+    rows = groups * group_rows
+    lane_tiles = LANES // 128
     tiles = rows * lane_tiles // devices
     held = tables(rows)
     held_shape = (rows * lane_tiles * 8, 128)
@@ -418,16 +434,15 @@
     in_specs = [
         pl.BlockSpec(memory_space=pltpu.SMEM),
         pl.BlockSpec(
-            (groups, 1, lane_tiles, row_pairs * 8, 128), lambda c: (0, c // 2, 0, 0, 0)
+            (groups, 1, group_rows * 8, 128), lambda c: (0, c, 0, 0)
         ),
     ] + [whole(t) for t in held]
-    spread = pltpu.VMEM((RADIX, 2 * rows, 6 * SUB), BF16)
     options = dict(
-        grid=(2 * pairs,),
+        grid=(channels,),
         compiler_params=pltpu.CompilerParams(vmem_limit_bytes=VMEM_LIMIT),
         cost_estimate=pl.CostEstimate(
-            flops=2 * pairs * rows * LANES * 2048 * 3 * 3,
-            bytes_accessed=2 * pairs * rows * LANES * 12,
+            flops=channels * rows * LANES * 2048 * 3 * 3,
+            bytes_accessed=channels * rows * LANES * 12,
             transcendentals=0,
         ),
     )
@@ -437,20 +452,19 @@
             in_specs=in_specs,
             out_specs=pl.BlockSpec(held_shape, lambda c: (0, 0)),
             out_shape=jax.ShapeDtypeStruct(held_shape, F32),
-            scratch_shapes=[spread],
             name="filter_first",
             **options,
         )(skip, flat, *held)
     anywhere = pl.BlockSpec(memory_space=pl.ANY)
     return pl.pallas_call(
-        functools.partial(last_channels_kernel, late),
+        functools.partial(last_channels_kernel, late, len(ready)),
         in_specs=in_specs + [anywhere] * (1 + len(ready)),
         out_specs=[anywhere, anywhere],
         out_shape=[
             jax.ShapeDtypeStruct((devices, tiles - late + 1, 8, 128), F32),
             jax.ShapeDtypeStruct((devices, late, 8, 128), F32),
         ],
-        scratch_shapes=[spread, pltpu.VMEM(held_shape, F32), pltpu.SemaphoreType.DMA((6,))],
+        scratch_shapes=[pltpu.VMEM(held_shape, F32), pltpu.SemaphoreType.DMA((6,))],
         name="filter_last",
         **options,
     )(skip, flat, *held, before, *ready)
@@ -464,7 +478,7 @@
 
 
 def late_kernel(conv_ref, edge_ref, gate_ref, edge_gate_ref, *rest):
-    *fixed, out_ref, window_ref, high_ref, low_ref, mix_ref = rest
+    fixed, out_ref, window_ref, scratch = rest[:5], rest[5], rest[6], rest[7:]
     block = gate_ref.shape[0]
     reach = TAPS + 1
 
@@ -481,11 +495,11 @@
         window_ref[reach + j * reach : 2 * reach + j * reach, :] = (
             frames_by_channels(conv_ref[:, j]) * gate_ref[span, :]
         )
-    mix_block(window_ref, *fixed, out_ref, high_ref, low_ref, mix_ref)
+    mix_window(window_ref, fixed, scratch, out_ref)
 
 
 def early_kernel(conv_ref, edge_ref, gate_ref, halo_ref, halo_gate_ref, *rest):
-    *fixed, _, out_ref, window_ref, high_ref, low_ref, mix_ref = rest
+    fixed, out_ref, window_ref, scratch = rest[:5], rest[6], rest[7], rest[8:]
     block = gate_ref.shape[0]
     reach = TAPS + 1
     last = pl.program_id(0) == pl.num_programs(0) - 1
@@ -507,7 +521,7 @@
         window_ref[reach + j * reach : 2 * reach + j * reach, :] = (
             frames_by_channels(tile) * gate_ref[span, :]
         )
-    mix_block(window_ref, *fixed, out_ref, high_ref, low_ref, mix_ref)
+    mix_window(window_ref, fixed, scratch, out_ref)
 
 
 def tail_part(conv, late, gate_input, halo_gate, before, late_tiles, fixed):
@@ -552,12 +566,7 @@
         out_specs=pl.BlockSpec((block, width), lambda r: (r + start, 0)),
         out_shape=jax.ShapeDtypeStruct(gate_input.shape, F32),
         input_output_aliases=aliases,
-        scratch_shapes=[
-            pltpu.VMEM((block + reach, width), F32),
-            pltpu.VMEM((block + reach, width), BF16),
-            pltpu.VMEM((block + reach, width), BF16),
-            pltpu.VMEM((block, width), F32),
-        ],
+        scratch_shapes=mix_scratch(block, width, hidden),
         compiler_params=pltpu.CompilerParams(vmem_limit_bytes=VMEM_LIMIT),
         cost_estimate=pl.CostEstimate(
             flops=count * block * 3 * 2 * (2 * width * hidden + 3 * width * width),
@@ -583,9 +592,9 @@
     ring = [(i, i + 1) for i in range(devices - 1)]
     halo_gate = lax.ppermute(gate_input[-reach:], ("tm", "chan"), ring)
     one, two = turn(signal, kernel, groups)
-    before = filter_pairs(enter(one), skip_here, None, devices, late_tiles)
-    ready = (fixed[0], fixed[2], fixed[4], halo_gate)
-    late, early = filter_pairs(enter(two), skip_here, before, devices, late_tiles, ready)
+    before = filter_channels(enter(one), skip_here, None, devices, late_tiles)
+    ready = (fixed[0], halo_gate)
+    late, early = filter_channels(enter(two), skip_here, before, devices, late_tiles, ready)
     late = leave(late)
     early = leave(early)
     part = tail_part(late, late, gate_input, None, None, late_tiles, fixed)

time: 353 us -> 352 us (level)
  blocking collectives: 221 us -> 244 us
  Pallas kernels: 102 us -> 85.3 us
  other arithmetic: 5.99 us -> 0 us
    all_to_all x1, blocking collectives: 143 us -> 166 us  [enter(): return lax.all_to_all(array, 'tm', split_axis=0, concat_axis=0, tiled=True)]
    pallas_call x3, Pallas kernels: 61.4 us -> 49.3 us  [the longest x1 30.5 us: filter_channels(): pl.pallas_call(first_channels_kernel, in_specs=in_specs, out_specs=pl.Blo...]
    pallas_call x2, Pallas kernels: 40.7 us -> 36 us  [tail_part(): pl.pallas_call(early_kernel if first else late_kernel, grid=(count,), in_...]
  transfers between devices with their start and end apart: 3 -> 3, of which waited for: 0 -> 0; matrix products, arithmetic and copies ran while one was open for 3% -> 1% of each run, Pallas kernels for 18% -> 16%
where the time goes in v4:
time: 352 us; the launch traced here: 350 us
  blocking collectives  244 us (69%)
  Pallas kernels  85.3 us (24%)
  starting transfers between devices  15.5 us (4%)
  local copies, waits for them, and re-layouts  4.9 us (1%)
    all_to_all x1, blocking collectives, enter(): return lax.all_to_all(array, 'tm', split_axis=0, concat_axis=0, tiled=True)  166 us
    all_to_all x1, blocking collectives, leave(): lax.all_to_all(array, ('tm', 'chan'), split_axis=0, concat_axis=0, tiled=...  78.1 us
    pallas_call x2, Pallas kernels, tail_part(): pl.pallas_call(early_kernel if first else late_kernel, grid=(count,), in_...  36 us
    pallas_call x1, Pallas kernels, filter_channels(): pl.pallas_call(first_channels_kernel, in_specs=in_specs, out_specs=pl.Blo...  30.5 us
    pallas_call x1, Pallas kernels, turn(): pl.pallas_call(turn_kernel, grid=(frames // chunk,), in_specs=[block, blo...  9.93 us
    pallas_call x1, Pallas kernels, filter_channels(): pl.pallas_call(functools.partial(last_channels_kernel, late, len(ready)),...  8.88 us
  transfers between devices with their start and end apart: 3, of which 0 were waited for; matrix products, arithmetic and copies ran while one was open for 1% of the time, Pallas kernels for 16%

profile of v4, /device:TPU:11, one launch (start us, length us, event | category | flops | bytes accessed | tf_op | source)
XLA Modules:
  0.0 349.5 jit_solution(18044560896428044586)
XLA Ops:
  0.0 9.9 %turn.1 = (f32[16,7,16,8,128]{4,3,2,1,0:T(8,128)}, f32[16,1,16,8,128]{4,3,2,1,0:T(8,128)}) custom-call(f32[8192,128]{1,0:T(8,128)} %signal_ref.1, f32[8192,128]{1,0:T(8,128)} %kernel_ref.1), custom_call_target="tpu_custom_call" | custom-call | tf_op jit(solution)/shard_map/turn/pallas_call | solution.py:337
  9.9 0.0 copy-start.3
  9.9 165.6 %all_to_all.20 = f32[16,7,16,8,128]{4,3,2,1,0:T(8,128)} all-to-all(f32[16,7,16,8,128]{4,3,2,1,0:T(8,128)} %get-tuple-element.10), channel_id=1, replica_groups=mesh['grp'=1,'tm'=16,'chan'=2] {'tm'}, dimensions={0} | all-to-all | bytes 14680064 | tf_op jit(solution)/shard_map/all_to_all | solution.py:587
  175.6 0.0 copy-start.4
  175.6 5.7 %all-to-all-start = ((f32[16,1,16,8,128]{4,3,2,1,0:T(8,128)}), f32[16,1,16,8,128]{4,3,2,1,0:T(8,128)S(1)}, u32[]{:S(2)}, u32[]{:S(2)}) async-start(f32[16,1,16,8,128]{4,3,2,1,0:T(8,128)} %get-tuple-element.9), calls=%async_computation | async-start | bytes 2097152 | tf_op jit(solution)/shard_map/all_to_all | solution.py:587
  181.3 0.9 slice.3
  182.2 5.0 %collective-permute-start = (f32[128,256]{1,0:T(8,128)S(1)}, f32[128,256]{1,0:T(8,128)S(1)}, u32[]{:S(2)}, u32[]{:S(2)}) collective-permute-start(f32[128,256]{1,0:T(8,128)S(1)} %slice.3), channel_id=1, source_target_pairs={{0,1},{1,2},{2,3},{3,4},{4,5},{5,6},{6,7},{7,8},{8,9},{9,10},{10,1... | collective-permute-start | bytes 393224 | tf_op jit(solution)/shard_map/ppermute | solution.py:593
  187.2 0.0 copy-done.3
  187.2 0.2 reshape.24
  187.4 0.2 copy.19
  187.6 0.2 rev.3
  187.8 0.8 copy.20.rest_7_.rest_0_
  188.6 0.0 copy-done.4
  188.6 0.6 dynamic_slice.3.skip_ref
  189.2 30.5 %filter_first.1.rest_6_ = f32[8192,128]{1,0:T(8,128)} custom-call(f32[8]{0:T(128)} %dynamic_slice.3.skip_ref, f32[16,7,128,128]{3,2,1,0:T(8,128)} %bitcast.5, bf16[512,768]{1,0:T(8,128)(2,1)} %constant.30.clone.rest_0_, f32[256,512]{1,0:T(8,128)} %constant.31.clone.rest_1_, f32[256,512]{1,0:T(8,128)} %constant.32.clone.rest_2_, ...), custom_call_target="tpu_custom_call" | custom-call | flops 16911433728 | bytes 11010048 | tf_op jit(solution)/shard_map/filter_first/pallas_call | solution.py:450
  219.7 0.0 collective-permute-done.rest_8_.halo_gate_ref
  219.7 0.0 copy-start.2
  219.7 0.0 all-to-all-done
  219.7 0.0 copy-start.1
  219.7 0.6 copy-done.2
  220.3 0.4 copy-done.1
  220.7 8.9 %filter_last.1 = (f32[32,25,8,128]{3,2,1,0:T(8,128)}, f32[32,8,8,128]{3,2,1,0:T(8,128)}) custom-call(f32[8]{0:T(128)} %dynamic_slice.3.skip_ref, f32[16,1,128,128]{3,2,1,0:T(8,128)} %bitcast.6, bf16[512,768]{1,0:T(8,128)(2,1)} %constant.30.clone.rest_0_, f32[256,512]{1,0:T(8,128)} %constant.31.clone.rest_1_, f32[256,512]{1,0:T(8,128)} %constant.32.clone.rest_2_, ...), custom_call_target="tpu_custom_call" | custom-call | flops 2415919104 | bytes 1572864 | tf_op jit(solution)/shard_map/filter_last/pallas_call | solution.py:459
  229.6 78.1 %all_to_all.21.conv_ref.edge_ref = f32[32,25,8,128]{3,2,1,0:T(8,128)} all-to-all(f32[32,25,8,128]{3,2,1,0:T(8,128)} %get-tuple-element.12), channel_id=1, replica_groups=mesh['grp'=1,'tm'=16,'chan'=2] {'tm','chan'}, dimensions={0} | all-to-all | bytes 6553600 | tf_op jit(solution)/shard_map/all_to_all | solution.py:590
  307.7 4.8 %all-to-all-start.2 = ((f32[32,8,8,128]{3,2,1,0:T(8,128)}), f32[32,8,8,128]{3,2,1,0:T(8,128)S(1)}, u32[]{:S(2)}, u32[]{:S(2)}) async-start(f32[32,8,8,128]{3,2,1,0:T(8,128)} %get-tuple-element.11), calls=%async_computation.2 | async-start | bytes 2097152 | tf_op jit(solution)/shard_map/all_to_all | solution.py:590
  312.5 25.4 %mix_late.1.rest_5_ = f32[4096,256]{1,0:T(8,128)} custom-call(f32[32,25,8,128]{3,2,1,0:T(8,128)} %all_to_all.21.conv_ref.edge_ref, f32[32,25,8,128]{3,2,1,0:T(8,128)} %all_to_all.21.conv_ref.edge_ref, f32[4096,256]{1,0:T(8,128)} %gate_ref.3, f32[4096,256]{1,0:T(8,128)} %gate_ref.3, f32[256,256]{1,0:T(8,128)} %copy.20.rest_7_.rest_0_, f32[1,256]{1,0:T(1,128)} %bitcast.10, ...), custom_call_target="tpu_custom_call" | custom-call | flops 13287555072 | bytes 9437184 | tf_op jit(solution)/shard_map/mix_late/pallas_call | solution.py:562
  337.9 0.0 all-to-all-done.2.conv_ref.halo_ref
  337.9 0.0 copy-start
  337.9 1.0 copy-done
  338.9 10.6 %mix_early.1 = f32[4096,256]{1,0:T(8,128)} custom-call(f32[32,8,8,128]{3,2,1,0:T(8,128)} %copy-done, f32[32,25,8,128]{3,2,1,0:T(8,128)} %all_to_all.21.conv_ref.edge_ref, f32[4096,256]{1,0:T(8,128)} %gate_ref.3, f32[32,8,8,128]{3,2,1,0:T(8,128)} %copy-done, f32[128,256]{1,0:T(8,128)} %copy-done.2, ...), custom_call_target="tpu_custom_call", output_to_operand_aliasing={{}: (10, {})} | custom-call | flops 4429185024 | bytes 3145728 | tf_op jit(solution)/shard_map/mix_early/pallas_call | solution.py:562
  (1 shorter events, 0.0 us)
Async XLA Ops:
  9.9 177.2 %copy-start.3 = (f32[256,254]{1,0:T(8,128)S(1)}, f32[256,254]{1,0:T(8,128)}, u32[]{:S(2)}) copy-start(f32[256,254]{1,0:T(8,128)} %param.19) | copy-start | bytes 780292
  175.6 13.0 %copy-start.4 = (f32[256]{0:T(256)S(1)}, f32[256]{0:T(256)}, u32[]{:S(2)}) copy-start(f32[256]{0:T(256)} %param.17) | copy-start | bytes 3076
  175.6 44.1 %all-to-all-start = ((f32[16,1,16,8,128]{4,3,2,1,0:T(8,128)}), f32[16,1,16,8,128]{4,3,2,1,0:T(8,128)S(1)}, u32[]{:S(2)}, u32[]{:S(2)}) async-start(f32[16,1,16,8,128]{4,3,2,1,0:T(8,128)} %get-tuple-element.9), calls=%async_computation | async-start | bytes 2097152 | tf_op jit(solution)/shard_map/all_to_all | solution.py:587
  182.2 37.5 %collective-permute-start = (f32[128,256]{1,0:T(8,128)S(1)}, f32[128,256]{1,0:T(8,128)S(1)}, u32[]{:S(2)}, u32[]{:S(2)}) collective-permute-start(f32[128,256]{1,0:T(8,128)S(1)} %slice.3), channel_id=1, source_target_pairs={{0,1},{1,2},{2,3},{3,4},{4,5},{5,6},{6,7},{7,8},{8,9},{9,10},{10,1... | collective-permute-start | bytes 393224 | tf_op jit(solution)/shard_map/ppermute | solution.py:593
  219.7 0.7 copy-start.2
  219.7 1.0 copy-start.1
  307.7 30.2 %all-to-all-start.2 = ((f32[32,8,8,128]{3,2,1,0:T(8,128)}), f32[32,8,8,128]{3,2,1,0:T(8,128)S(1)}, u32[]{:S(2)}, u32[]{:S(2)}) async-start(f32[32,8,8,128]{3,2,1,0:T(8,128)} %get-tuple-element.11), calls=%async_computation.2 | async-start | bytes 2097152 | tf_op jit(solution)/shard_map/all_to_all | solution.py:590
  337.9 1.0 copy-start

commit v5 on v4

--- a/solution.py
+++ b/solution.py
@@ -36,18 +36,18 @@
     n2 = np.arange(LANES, dtype=np.float64)
     m = np.arange(SUB, dtype=np.float64)
     first = turn * np.outer(n1 + 0.25, n1) / rows
-    enter = table_split(np.concatenate([np.cos(first), -np.sin(first)], axis=0), 1, "hhl")
+    enter = table_split(np.concatenate([np.cos(first), -np.sin(first)], axis=0), 1, "hl")
     leave = table_split(
-        np.concatenate([np.cos(first.T), -np.sin(first.T)], axis=1) / length, 1, "hhl"
+        np.concatenate([np.cos(first.T), -np.sin(first.T)], axis=1) / length, 1, "hl"
     )
     twiddle = turn * np.outer(n1 + 0.25, n2) / length
     forward, backward = [], []
     for r in range(RADIX):
         phase = turn * np.outer(m, m / SUB + r / LANES)
         c, s = np.cos(phase), np.sin(phase)
-        forward.append(table_split(np.block([[c, -s], [s, c]]), 0, "hhl"))
+        forward.append(table_split(np.block([[c, -s], [s, c]]), 0, "hl"))
         c, s = c.T, s.T
-        backward.append(table_split(np.block([[c, s], [-s, c]]), 0, "hhl"))
+        backward.append(table_split(np.block([[c, s], [-s, c]]), 0, "hl"))
     return (
         enter,
         np.cos(twiddle).astype(np.float32),
@@ -69,6 +69,13 @@
     return jnp.concatenate([high, low, high], axis=axis)
 
 
+def high_high_low(table, axis):
+    size = table.shape[axis] // 2
+    high = lax.slice_in_dim(table, 0, size, axis=axis)
+    low = lax.slice_in_dim(table, size, 2 * size, axis=axis)
+    return jnp.concatenate([high, high, low], axis=axis)
+
+
 def dot(left, right):
     return jnp.dot(left, right, preferred_element_type=F32)
 
@@ -76,7 +83,8 @@
 def filter_channel(signal, kernel, skip, enter_ref, cos_ref, sin_ref, forward_ref, backward_ref,
                    leave_ref):
     rows = cos_ref.shape[0]
-    entered = [dot(enter_ref[...], split_cat(value, 0)) for value in (signal, kernel)]
+    enter = high_high_low(enter_ref[...], 1)
+    entered = [dot(enter, split_cat(value, 0)) for value in (signal, kernel)]
     spectra = []
     for turned in entered:
         real_in, imag_in = turned[:rows], turned[rows:]
@@ -88,7 +96,7 @@
         gr, gi, hr, hi = r1 + r3, i1 + i3, r1 - r3, i1 - i3
         spread = ((er + gr, ei + gi), (fr + hi, fi - hr), (er - gr, ei - gi), (fr - hi, fi + hr))
         spectra.append([
-            dot(split_cat(jnp.concatenate(pair, axis=1), 1), forward_ref[r])
+            dot(split_cat(jnp.concatenate(pair, axis=1), 1), high_high_low(forward_ref[r], 0))
             for r, pair in enumerate(spread)
         ])
     products = []
@@ -99,7 +107,7 @@
         products.append(split_cat(product, 1))
     back = []
     for r in range(RADIX):
-        turned = dot(products[r], backward_ref[r])
+        turned = dot(products[r], high_high_low(backward_ref[r], 0))
         back.append((turned[:, :SUB], turned[:, SUB:]))
     (r0, i0), (r1, i1), (r2, i2), (r3, i3) = back
     er, ei, fr, fi = r0 + r2, i0 + i2, r0 - r2, i0 - i2
@@ -110,7 +118,7 @@
         [real * cos_ref[...] - imag * sin_ref[...], imag * cos_ref[...] + real * sin_ref[...]],
         axis=0,
     )
-    return dot(leave_ref[...], split_cat(turned, 0)) + skip * signal
+    return dot(high_high_low(leave_ref[...], 1), split_cat(turned, 0)) + skip * signal
 
 
 def filter_kernel(
@@ -306,26 +314,52 @@
     )(conv_blocks, gate_input, halo, *fixed)
 
 
-FIRST_CHANNELS = 7
-TURN_ROWS = 4
-
-
-def turn_kernel(signal_ref, kernel_ref, first_ref, second_ref):
-    groups, early, rows = first_ref.shape[:3]
-    late = second_ref.shape[1]
-    stride = rows * 8
-    first = first_ref.reshape(groups * early * stride, 128)
-    second = second_ref.reshape(groups * late * stride, 128)
+FIRST_CHANNELS = 6
+TURN_ROWS = 8
+
+
+def turn_kernel(signal_ref, kernel_ref, first_ref, second_ref, held_ref, sems):
+    groups, early = first_ref.shape[:2]
+    rows = signal_ref.shape[0] // LANES
+    step, steps = pl.program_id(0), pl.num_programs(0)
+    slot = step % 2
+
+    def copies(at, slot):
+        shaped = held_ref.at[slot].reshape(groups, 8, rows + 1, 8, 128)
+        there = pl.ds(at * rows, rows)
+        return (
+            pltpu.make_async_copy(
+                shaped.at[:, :early, :rows], first_ref.at[:, :, there], sems.at[slot, 0]
+            ),
+            pltpu.make_async_copy(
+                shaped.at[:, early:, :rows], second_ref.at[:, :, there], sems.at[slot, 1]
+            ),
+        )
+
+    @pl.when(step >= 2)
+    def _():
+        for copy in copies(step - 2, slot):
+            copy.wait()
+
     for row in range(rows):
         for j in range(LANES // 128):
             span = slice(row * LANES + j * 128, row * LANES + (j + 1) * 128)
             for which, ref in enumerate((signal_ref, kernel_ref)):
                 turned = jnp.transpose(ref[span, :], (1, 0))
                 place = row * 8 + j * 2 + which
-                for g in range(groups):
-                    own = turned[g * 8 : (g + 1) * 8]
-                    first[pl.ds(g * early * stride + place, early, stride=stride), :] = own[:early]
-                    second[pl.ds(g * late * stride + place, late, stride=stride), :] = own[early:]
+                held_ref[slot, pl.ds(place, turned.shape[0], stride=(rows + 1) * 8), :] = turned
+    for copy in copies(step, slot):
+        copy.start()
+
+    @pl.when(step == steps - 1)
+    def _():
+        for copy in copies(step, slot):
+            copy.wait()
+
+    @pl.when((step == steps - 1) & (step >= 1))
+    def _():
+        for copy in copies(step - 1, 1 - slot):
+            copy.wait()
 
 
 def turn(signal, kernel, groups):
@@ -338,10 +372,12 @@
         turn_kernel,
         grid=(frames // chunk,),
         in_specs=[block, block],
-        out_specs=[
-            pl.BlockSpec((groups, n, TURN_ROWS, 8, 128), lambda i: (0, 0, i, 0, 0)) for n in counts
+        out_specs=[pl.BlockSpec(memory_space=pl.ANY)] * 2,
+        out_shape=[jax.ShapeDtypeStruct((groups, n, rows, 8, 128), F32) for n in counts],
+        scratch_shapes=[
+            pltpu.VMEM((2, width * (TURN_ROWS + 1) * 8, 128), F32),
+            pltpu.SemaphoreType.DMA((2, 2)),
         ],
-        out_shape=[jax.ShapeDtypeStruct((groups, n, rows, 8, 128), F32) for n in counts],
         compiler_params=pltpu.CompilerParams(vmem_limit_bytes=VMEM_LIMIT),
         name="turn",
     )(signal, kernel)

time: 352 us -> 340 us (0.966)
  blocking collectives: 244 us -> 224 us
  waiting for transfers between devices: 0.01 us -> 11.6 us
  Pallas kernels: 85.3 us -> 81.4 us
    all_to_all x1, blocking collectives: 166 us -> 143 us  [enter(): return lax.all_to_all(array, 'tm', split_axis=0, concat_axis=0, tiled=True)]
    all_to_all x1, waiting for transfers between devices: 0.01 us -> 11.6 us  [enter(): return lax.all_to_all(array, 'tm', split_axis=0, concat_axis=0, tiled=True)]
    pallas_call x1, Pallas kernels: 30.5 us -> 26.3 us  [filter_channels(): pl.pallas_call(first_channels_kernel, in_specs=in_specs, out_specs=pl.Blo...]
  transfers between devices with their start and end apart: 3 -> 3, of which waited for: 0 -> 1; matrix products, arithmetic and copies ran while one was open for 1% -> 1% of each run, Pallas kernels for 16% -> 15%
where the time goes in v5:
time: 340 us; the launch traced here: 338 us
  blocking collectives  224 us (66%)
  Pallas kernels  81.4 us (24%)
  starting transfers between devices  15.5 us (5%)
  waiting for transfers between devices  11.6 us (3%)
  local copies, waits for them, and re-layouts  5.24 us (2%)
    all_to_all x1, blocking collectives, enter(): return lax.all_to_all(array, 'tm', split_axis=0, concat_axis=0, tiled=True)  143 us
    all_to_all x1, blocking collectives, leave(): lax.all_to_all(array, ('tm', 'chan'), split_axis=0, concat_axis=0, tiled=...  81.3 us
    pallas_call x2, Pallas kernels, tail_part(): pl.pallas_call(early_kernel if first else late_kernel, grid=(count,), in_...  36 us
    pallas_call x1, Pallas kernels, filter_channels(): pl.pallas_call(first_channels_kernel, in_specs=in_specs, out_specs=pl.Blo...  26.3 us
    pallas_call x1, Pallas kernels, filter_channels(): pl.pallas_call(functools.partial(last_channels_kernel, late, len(ready)),...  12.3 us
    all_to_all x1, waiting for transfers between devices, enter(): return lax.all_to_all(array, 'tm', split_axis=0, concat_axis=0, tiled=True)  11.6 us
  transfers between devices with their start and end apart: 3, of which 1 were waited for; matrix products, arithmetic and copies ran while one was open for 1% of the time, Pallas kernels for 15%

profile of v5, /device:TPU:11, one launch (start us, length us, event | category | flops | bytes accessed | tf_op | source)
XLA Modules:
  0.0 338.1 jit_solution(5411061997228195207)
XLA Ops:
  0.0 6.7 %turn.1 = (f32[16,6,16,8,128]{4,3,2,1,0:T(8,128)}, f32[16,2,16,8,128]{4,3,2,1,0:T(8,128)}) custom-call(f32[8192,128]{1,0:T(8,128)} %signal_ref.1, f32[8192,128]{1,0:T(8,128)} %kernel_ref.1), custom_call_target="tpu_custom_call" | custom-call | tf_op jit(solution)/shard_map/turn/pallas_call | solution.py:371
  6.7 143.0 %all_to_all.20 = f32[16,6,16,8,128]{4,3,2,1,0:T(8,128)} all-to-all(f32[16,6,16,8,128]{4,3,2,1,0:T(8,128)} %get-tuple-element.10), channel_id=1, replica_groups=mesh['grp'=1,'tm'=16,'chan'=2] {'tm'}, dimensions={0} | all-to-all | bytes 12582912 | tf_op jit(solution)/shard_map/all_to_all | solution.py:623
  149.8 0.0 copy-start.2
  149.8 0.0 copy-start.4
  149.8 5.7 %all-to-all-start = ((f32[16,2,16,8,128]{4,3,2,1,0:T(8,128)}), f32[16,2,16,8,128]{4,3,2,1,0:T(8,128)S(1)}, u32[]{:S(2)}, u32[]{:S(2)}) async-start(f32[16,2,16,8,128]{4,3,2,1,0:T(8,128)} %get-tuple-element.9), calls=%async_computation | async-start | bytes 4194304 | tf_op jit(solution)/shard_map/all_to_all | solution.py:623
  155.5 0.9 slice.3
  156.4 5.0 %collective-permute-start = (f32[128,256]{1,0:T(8,128)S(1)}, f32[128,256]{1,0:T(8,128)S(1)}, u32[]{:S(2)}, u32[]{:S(2)}) collective-permute-start(f32[128,256]{1,0:T(8,128)S(1)} %slice.3), channel_id=1, source_target_pairs={{0,1},{1,2},{2,3},{3,4},{4,5},{5,6},{6,7},{7,8},{8,9},{9,10},{10,1... | collective-permute-start | bytes 393224 | tf_op jit(solution)/shard_map/ppermute | solution.py:629
  161.4 0.0 copy-done.2
  161.4 0.2 reshape.24
  161.6 0.2 copy.19
  161.8 0.2 rev.3
  162.0 0.8 copy.20.rest_7_.rest_0_
  162.8 0.0 copy-done.4
  162.8 0.6 dynamic_slice.3.skip_ref
  163.4 26.3 %filter_first.1.rest_6_ = f32[8192,128]{1,0:T(8,128)} custom-call(f32[8]{0:T(128)} %dynamic_slice.3.skip_ref, f32[16,6,128,128]{3,2,1,0:T(8,128)} %bitcast.5, bf16[512,512]{1,0:T(8,128)(2,1)} %constant.30.clone.rest_0_, f32[256,512]{1,0:T(8,128)} %constant.31.clone.rest_1_, f32[256,512]{1,0:T(8,128)} %constant.32.clone.rest_2_, ...), custom_call_target="tpu_custom_call" | custom-call | flops 14495514624 | bytes 9437184 | tf_op jit(solution)/shard_map/filter_first/pallas_call | solution.py:486
  189.7 0.0 collective-permute-done.rest_8_.halo_gate_ref
  189.7 0.0 copy-start.3
  189.7 11.6 %all-to-all-done = f32[16,2,16,8,128]{4,3,2,1,0:T(8,128)S(1)} async-done(((f32[16,2,16,8,128]{4,3,2,1,0:T(8,128)}), f32[16,2,16,8,128]{4,3,2,1,0:T(8,128)S(1)}, u32[]{:S(2)}, u32[]{:S(2)}) %all-to-all-start) | async-done | bytes 2097184 | tf_op jit(solution)/shard_map/all_to_all | solution.py:623
  201.3 0.0 copy-start.1
  201.3 0.0 copy-done.3
  201.3 1.3 copy-done.1
  202.6 12.3 %filter_last.1 = (f32[32,25,8,128]{3,2,1,0:T(8,128)}, f32[32,8,8,128]{3,2,1,0:T(8,128)}) custom-call(f32[8]{0:T(128)} %dynamic_slice.3.skip_ref, f32[16,2,128,128]{3,2,1,0:T(8,128)} %bitcast.6, bf16[512,512]{1,0:T(8,128)(2,1)} %constant.30.clone.rest_0_, f32[256,512]{1,0:T(8,128)} %constant.31.clone.rest_1_, f32[256,512]{1,0:T(8,128)} %constant.32.clone.rest_2_, ...), custom_call_target="tpu_custom_call" | custom-call | flops 4831838208 | bytes 3145728 | tf_op jit(solution)/shard_map/filter_last/pallas_call | solution.py:495
  214.9 81.3 %all_to_all.21.conv_ref.edge_ref = f32[32,25,8,128]{3,2,1,0:T(8,128)} all-to-all(f32[32,25,8,128]{3,2,1,0:T(8,128)} %get-tuple-element.12), channel_id=1, replica_groups=mesh['grp'=1,'tm'=16,'chan'=2] {'tm','chan'}, dimensions={0} | all-to-all | bytes 6553600 | tf_op jit(solution)/shard_map/all_to_all | solution.py:626
  296.3 4.8 %all-to-all-start.2 = ((f32[32,8,8,128]{3,2,1,0:T(8,128)}), f32[32,8,8,128]{3,2,1,0:T(8,128)S(1)}, u32[]{:S(2)}, u32[]{:S(2)}) async-start(f32[32,8,8,128]{3,2,1,0:T(8,128)} %get-tuple-element.11), calls=%async_computation.2 | async-start | bytes 2097152 | tf_op jit(solution)/shard_map/all_to_all | solution.py:626
  301.1 25.4 %mix_late.1.rest_5_ = f32[4096,256]{1,0:T(8,128)} custom-call(f32[32,25,8,128]{3,2,1,0:T(8,128)} %all_to_all.21.conv_ref.edge_ref, f32[32,25,8,128]{3,2,1,0:T(8,128)} %all_to_all.21.conv_ref.edge_ref, f32[4096,256]{1,0:T(8,128)} %gate_ref.3, f32[4096,256]{1,0:T(8,128)} %gate_ref.3, f32[256,256]{1,0:T(8,128)} %copy.20.rest_7_.rest_0_, f32[1,256]{1,0:T(1,128)} %bitcast.10, ...), custom_call_target="tpu_custom_call" | custom-call | flops 13287555072 | bytes 9437184 | tf_op jit(solution)/shard_map/mix_late/pallas_call | solution.py:598
  326.5 0.0 all-to-all-done.2.conv_ref.halo_ref
  326.5 0.0 copy-start
  326.5 1.0 copy-done
  327.5 10.6 %mix_early.1 = f32[4096,256]{1,0:T(8,128)} custom-call(f32[32,8,8,128]{3,2,1,0:T(8,128)} %copy-done, f32[32,25,8,128]{3,2,1,0:T(8,128)} %all_to_all.21.conv_ref.edge_ref, f32[4096,256]{1,0:T(8,128)} %gate_ref.3, f32[32,8,8,128]{3,2,1,0:T(8,128)} %copy-done, f32[128,256]{1,0:T(8,128)} %copy-done.3, ...), custom_call_target="tpu_custom_call", output_to_operand_aliasing={{}: (10, {})} | custom-call | flops 4429185024 | bytes 3145728 | tf_op jit(solution)/shard_map/mix_early/pallas_call | solution.py:598
  (1 shorter events, 0.0 us)
Async XLA Ops:
  149.8 11.6 %copy-start.2 = (f32[256,254]{1,0:T(8,128)S(1)}, f32[256,254]{1,0:T(8,128)}, u32[]{:S(2)}) copy-start(f32[256,254]{1,0:T(8,128)} %param.19) | copy-start | bytes 780292
  149.8 13.0 %copy-start.4 = (f32[256]{0:T(256)S(1)}, f32[256]{0:T(256)}, u32[]{:S(2)}) copy-start(f32[256]{0:T(256)} %param.17) | copy-start | bytes 3076
  149.8 51.5 %all-to-all-start = ((f32[16,2,16,8,128]{4,3,2,1,0:T(8,128)}), f32[16,2,16,8,128]{4,3,2,1,0:T(8,128)S(1)}, u32[]{:S(2)}, u32[]{:S(2)}) async-start(f32[16,2,16,8,128]{4,3,2,1,0:T(8,128)} %get-tuple-element.9), calls=%async_computation | async-start | bytes 4194304 | tf_op jit(solution)/shard_map/all_to_all | solution.py:623
  156.4 33.4 %collective-permute-start = (f32[128,256]{1,0:T(8,128)S(1)}, f32[128,256]{1,0:T(8,128)S(1)}, u32[]{:S(2)}, u32[]{:S(2)}) collective-permute-start(f32[128,256]{1,0:T(8,128)S(1)} %slice.3), channel_id=1, source_target_pairs={{0,1},{1,2},{2,3},{3,4},{4,5},{5,6},{6,7},{7,8},{8,9},{9,10},{10,1... | collective-permute-start | bytes 393224 | tf_op jit(solution)/shard_map/ppermute | solution.py:629
  189.7 11.6 %copy-start.3 = (f32[128,256]{1,0:T(8,128)}, f32[128,256]{1,0:T(8,128)S(1)}, u32[]{:S(2)}) copy-start(f32[128,256]{1,0:T(8,128)S(1)} %collective-permute-done.rest_8_.halo_gate_ref) | copy-start | bytes 393220
  201.3 1.3 copy-start.1
  296.3 30.2 %all-to-all-start.2 = ((f32[32,8,8,128]{3,2,1,0:T(8,128)}), f32[32,8,8,128]{3,2,1,0:T(8,128)S(1)}, u32[]{:S(2)}, u32[]{:S(2)}) async-start(f32[32,8,8,128]{3,2,1,0:T(8,128)} %get-tuple-element.11), calls=%async_computation.2 | async-start | bytes 2097152 | tf_op jit(solution)/shard_map/all_to_all | solution.py:626
  326.5 1.0 copy-start

commit v6 on v5

--- a/solution.py
+++ b/solution.py
@@ -18,7 +18,7 @@
 EPSILON = 1e-06
 BF16 = jnp.bfloat16
 F32 = jnp.float32
-VMEM_LIMIT = 56 * 1024 * 1024
+VMEM_LIMIT = 63 * 1024 * 1024
 
 
 def table_split(table, axis, order):
@@ -393,10 +393,10 @@
     )
 
 
-def scatter_channel(ref, slot, value):
+def scatter_channel(ref, slot, value, spare=0):
     tiles = LANES // 128
     for j in range(tiles):
-        ref[pl.ds(8 * j + slot, value.shape[0], stride=8 * tiles), :] = (
+        ref[pl.ds(8 * j + slot, value.shape[0], stride=8 * (tiles + spare)), :] = (
             value[:, j * 128 : (j + 1) * 128]
         )
 
@@ -417,7 +417,10 @@
     c = pl.program_id(0)
     channel = c + FIRST_CHANNELS
     devices, tiles = late_ref.shape[0], late_ref.shape[1] + early_ref.shape[1] - 1
-    load = pltpu.make_async_copy(before_ref, held_ref, sems.at[0])
+    per_row = LANES // 128
+    rows = tiles // per_row
+    shaped = held_ref.reshape(devices, rows, per_row + 1, 8, 128)
+    load = pltpu.make_async_copy(before_ref, shaped.at[:, :, :per_row], sems.at[0])
 
     @pl.when(c == 0)
     def _():
@@ -432,19 +435,23 @@
     def _():
         load.wait()
 
-    scatter_channel(held_ref, channel, result)
+    scatter_channel(held_ref, channel, result, spare=1)
 
     @pl.when(c == pl.num_programs(0) - 1)
     def _():
-        shaped = held_ref.reshape(devices, tiles, 8, 128)
-        final = shaped.at[:, tiles - 1 : tiles]
-        pairs = (
-            (shaped.at[:, late:tiles], late_ref.at[:, 0 : tiles - late]),
-            (shaped.at[:, late - 1 : late], late_ref.at[:, tiles - late : tiles - late + 1]),
-            (shaped.at[:, 0 : late - 1], early_ref.at[:, 0 : late - 1]),
-            (final.at[0 : devices - 1], early_ref.at[1:devices, late - 1 : late]),
-            (final.at[devices - 1 : devices], early_ref.at[0:1, late - 1 : late]),
-        )
+        pairs = []
+        for row in range(late // per_row, rows):
+            at = row * per_row - late
+            pairs.append((shaped.at[:, row, :per_row], late_ref.at[:, at : at + per_row]))
+        for row in range(late // per_row):
+            at = row * per_row
+            count = min(per_row, late - 1 - at)
+            pairs.append((shaped.at[:, row, :count], early_ref.at[:, at : at + count]))
+        edge = shaped.at[:, late // per_row - 1, per_row - 1 : per_row]
+        pairs.append((edge, late_ref.at[:, tiles - late : tiles - late + 1]))
+        final = shaped.at[:, rows - 1, per_row - 1 : per_row]
+        pairs.append((final.at[0 : devices - 1], early_ref.at[1:devices, late - 1 : late]))
+        pairs.append((final.at[devices - 1 : devices], early_ref.at[0:1, late - 1 : late]))
         copies = [
             pltpu.make_async_copy(here, there, sems.at[1 + i])
             for i, (here, there) in enumerate(pairs)
@@ -500,10 +507,13 @@
             jax.ShapeDtypeStruct((devices, tiles - late + 1, 8, 128), F32),
             jax.ShapeDtypeStruct((devices, late, 8, 128), F32),
         ],
-        scratch_shapes=[pltpu.VMEM(held_shape, F32), pltpu.SemaphoreType.DMA((6,))],
+        scratch_shapes=[
+            pltpu.VMEM((rows * (lane_tiles + 1) * 8, 128), F32),
+            pltpu.SemaphoreType.DMA((4 + tiles // lane_tiles,)),
+        ],
         name="filter_last",
         **options,
-    )(skip, flat, *held, before, *ready)
+    )(skip, flat, *held, before.reshape(devices, -1, lane_tiles, 8, 128), *ready)
 
 
 def frames_by_channels(tile):

time: 340 us -> 338 us (level)
  no operation moved by 1% of the time
where the time goes in v6:
time: 338 us; the launch traced here: 336 us
  blocking collectives  225 us (67%)
  Pallas kernels  80.8 us (24%)
  starting transfers between devices  16.6 us (5%)
  waiting for transfers between devices  11.2 us (3%)
    all_to_all x1, blocking collectives, enter(): return lax.all_to_all(array, 'tm', split_axis=0, concat_axis=0, tiled=True)  143 us
    all_to_all x1, blocking collectives, leave(): lax.all_to_all(array, ('tm', 'chan'), split_axis=0, concat_axis=0, tiled=...  81.6 us
    pallas_call x2, Pallas kernels, tail_part(): pl.pallas_call(early_kernel if first else late_kernel, grid=(count,), in_...  36.1 us
    pallas_call x1, Pallas kernels, filter_channels(): pl.pallas_call(first_channels_kernel, in_specs=in_specs, out_specs=pl.Blo...  26.3 us
    pallas_call x1, Pallas kernels, filter_channels(): pl.pallas_call(functools.partial(last_channels_kernel, late, len(ready)),...  11.8 us
    all_to_all x1, waiting for transfers between devices, enter(): return lax.all_to_all(array, 'tm', split_axis=0, concat_axis=0, tiled=True)  11.2 us
  transfers between devices with their start and end apart: 3, of which 1 were waited for; matrix products, arithmetic and copies ran while one was open for 1% of the time, Pallas kernels for 15%

profile of v6, /device:TPU:11, one launch (start us, length us, event | category | flops | bytes accessed | tf_op | source)
XLA Modules:
  0.0 336.2 jit_solution(8107573052867074312)
XLA Ops:
  0.0 6.7 %turn.1 = (f32[16,6,16,8,128]{4,3,2,1,0:T(8,128)}, f32[16,2,16,8,128]{4,3,2,1,0:T(8,128)}) custom-call(f32[8192,128]{1,0:T(8,128)} %signal_ref.1, f32[8192,128]{1,0:T(8,128)} %kernel_ref.1), custom_call_target="tpu_custom_call" | custom-call | tf_op jit(solution)/shard_map/turn/pallas_call | solution.py:371
  6.7 143.0 %all_to_all.20 = f32[16,6,16,8,128]{4,3,2,1,0:T(8,128)} all-to-all(f32[16,6,16,8,128]{4,3,2,1,0:T(8,128)} %get-tuple-element.10), channel_id=1, replica_groups=mesh['grp'=1,'tm'=16,'chan'=2] {'tm'}, dimensions={0} | all-to-all | bytes 12582912 | tf_op jit(solution)/shard_map/all_to_all | solution.py:633
  149.7 0.0 copy-start
  149.7 0.0 copy-start.2
  149.7 5.7 %all-to-all-start = ((f32[16,2,16,8,128]{4,3,2,1,0:T(8,128)}), f32[16,2,16,8,128]{4,3,2,1,0:T(8,128)}, u32[]{:S(2)}, u32[]{:S(2)}) async-start(f32[16,2,16,8,128]{4,3,2,1,0:T(8,128)} %get-tuple-element.9), calls=%async_computation | async-start | bytes 4194304 | tf_op jit(solution)/shard_map/all_to_all | solution.py:633
  155.4 0.9 slice.3
  156.3 5.4 %collective-permute-start = (f32[128,256]{1,0:T(8,128)S(1)}, f32[128,256]{1,0:T(8,128)S(1)}, u32[]{:S(2)}, u32[]{:S(2)}) collective-permute-start(f32[128,256]{1,0:T(8,128)S(1)} %slice.3), channel_id=1, source_target_pairs={{0,1},{1,2},{2,3},{3,4},{4,5},{5,6},{6,7},{7,8},{8,9},{9,10},{10,1... | collective-permute-start | bytes 393224 | tf_op jit(solution)/shard_map/ppermute | solution.py:639
  161.7 0.0 copy-done
  161.7 0.2 reshape.28
  161.9 0.2 copy.19
  162.1 0.2 rev.3
  162.3 0.8 copy.20.rest_7_.rest_0_
  163.2 0.0 copy-done.2
  163.2 0.6 dynamic_slice.3.skip_ref
  163.8 26.3 %filter_first.1 = f32[8192,128]{1,0:T(8,128)} custom-call(f32[8]{0:T(128)} %dynamic_slice.3.skip_ref, f32[16,6,128,128]{3,2,1,0:T(8,128)} %bitcast.6, bf16[512,512]{1,0:T(8,128)(2,1)} %constant.30.clone.rest_0_, f32[256,512]{1,0:T(8,128)} %constant.31.clone.rest_1_, f32[256,512]{1,0:T(8,128)} %constant.32.clone.rest_2_, ...), custom_call_target="tpu_custom_call" | custom-call | flops 14495514624 | bytes 9437184 | tf_op jit(solution)/shard_map/filter_first/pallas_call | solution.py:493
  190.1 0.0 collective-permute-done.rest_8_.halo_gate_ref
  190.1 0.0 copy-start.1
  190.1 11.2 %all-to-all-done = f32[16,2,16,8,128]{4,3,2,1,0:T(8,128)} async-done(((f32[16,2,16,8,128]{4,3,2,1,0:T(8,128)}), f32[16,2,16,8,128]{4,3,2,1,0:T(8,128)}, u32[]{:S(2)}, u32[]{:S(2)}) %all-to-all-start) | async-done | bytes 2097184 | tf_op jit(solution)/shard_map/all_to_all | solution.py:633
  201.3 0.0 copy-done.1
  201.3 11.8 %filter_last.1 = (f32[32,25,8,128]{3,2,1,0:T(8,128)}, f32[32,8,8,128]{3,2,1,0:T(8,128)}) custom-call(f32[8]{0:T(128)} %dynamic_slice.3.skip_ref, f32[16,2,128,128]{3,2,1,0:T(8,128)} %bitcast.data_ref, bf16[512,512]{1,0:T(8,128)(2,1)} %constant.30.clone.rest_0_, f32[256,512]{1,0:T(8,128)} %constant.31.clone.rest_1_, f32[256,512]{1,0:T(8,128)} %constant.32.clone.rest_2_, ...), custom_call_target="tpu_custom_call" | custom-call | flops 4831838208 | bytes 3145728 | tf_op jit(solution)/shard_map/filter_last/pallas_call | solution.py:502
  213.1 81.6 %all_to_all.21.conv_ref.edge_ref = f32[32,25,8,128]{3,2,1,0:T(8,128)} all-to-all(f32[32,25,8,128]{3,2,1,0:T(8,128)} %get-tuple-element.12), channel_id=1, replica_groups=mesh['grp'=1,'tm'=16,'chan'=2] {'tm','chan'}, dimensions={0} | all-to-all | bytes 6553600 | tf_op jit(solution)/shard_map/all_to_all | solution.py:636
  294.7 5.5 %all-to-all-start.2 = ((f32[32,8,8,128]{3,2,1,0:T(8,128)}), f32[32,8,8,128]{3,2,1,0:T(8,128)}, u32[]{:S(2)}, u32[]{:S(2)}) async-start(f32[32,8,8,128]{3,2,1,0:T(8,128)} %get-tuple-element.11), calls=%async_computation.2 | async-start | bytes 2097152 | tf_op jit(solution)/shard_map/all_to_all | solution.py:636
  300.2 25.4 %mix_late.1.rest_5_ = f32[4096,256]{1,0:T(8,128)} custom-call(f32[32,25,8,128]{3,2,1,0:T(8,128)} %all_to_all.21.conv_ref.edge_ref, f32[32,25,8,128]{3,2,1,0:T(8,128)} %all_to_all.21.conv_ref.edge_ref, f32[4096,256]{1,0:T(8,128)} %gate_ref.3, f32[4096,256]{1,0:T(8,128)} %gate_ref.3, f32[256,256]{1,0:T(8,128)} %copy.20.rest_7_.rest_0_, f32[1,256]{1,0:T(1,128)} %bitcast.10, ...), custom_call_target="tpu_custom_call" | custom-call | flops 13287555072 | bytes 9437184 | tf_op jit(solution)/shard_map/mix_late/pallas_call | solution.py:608
  325.5 0.0 all-to-all-done.2.conv_ref.halo_ref
  325.5 10.7 %mix_early.1 = f32[4096,256]{1,0:T(8,128)} custom-call(f32[32,8,8,128]{3,2,1,0:T(8,128)} %all-to-all-done.2.conv_ref.halo_ref, f32[32,25,8,128]{3,2,1,0:T(8,128)} %all_to_all.21.conv_ref.edge_ref, f32[4096,256]{1,0:T(8,128)} %gate_ref.3, f32[32,8,8,128]{3,2,1,0:T(8,128)} %all-to-all-done.2.conv_ref.halo_ref, ...), custom_call_target="tpu_custom_call", output_to_operand_aliasing={{}: (10, {})} | custom-call | flops 4429185024 | bytes 3145728 | tf_op jit(solution)/shard_map/mix_early/pallas_call | solution.py:608
  (1 shorter events, 0.0 us)
Async XLA Ops:
  149.7 12.0 %copy-start = (f32[256,254]{1,0:T(8,128)S(1)}, f32[256,254]{1,0:T(8,128)}, u32[]{:S(2)}) copy-start(f32[256,254]{1,0:T(8,128)} %param.19) | copy-start | bytes 780292
  149.7 13.4 %copy-start.2 = (f32[256]{0:T(256)S(1)}, f32[256]{0:T(256)}, u32[]{:S(2)}) copy-start(f32[256]{0:T(256)} %param.17) | copy-start | bytes 3076
  149.7 51.6 %all-to-all-start = ((f32[16,2,16,8,128]{4,3,2,1,0:T(8,128)}), f32[16,2,16,8,128]{4,3,2,1,0:T(8,128)}, u32[]{:S(2)}, u32[]{:S(2)}) async-start(f32[16,2,16,8,128]{4,3,2,1,0:T(8,128)} %get-tuple-element.9), calls=%async_computation | async-start | bytes 4194304 | tf_op jit(solution)/shard_map/all_to_all | solution.py:633
  156.3 33.8 %collective-permute-start = (f32[128,256]{1,0:T(8,128)S(1)}, f32[128,256]{1,0:T(8,128)S(1)}, u32[]{:S(2)}, u32[]{:S(2)}) collective-permute-start(f32[128,256]{1,0:T(8,128)S(1)} %slice.3), channel_id=1, source_target_pairs={{0,1},{1,2},{2,3},{3,4},{4,5},{5,6},{6,7},{7,8},{8,9},{9,10},{10,1... | collective-permute-start | bytes 393224 | tf_op jit(solution)/shard_map/ppermute | solution.py:639
  190.1 11.2 %copy-start.1 = (f32[128,256]{1,0:T(8,128)}, f32[128,256]{1,0:T(8,128)S(1)}, u32[]{:S(2)}) copy-start(f32[128,256]{1,0:T(8,128)S(1)} %collective-permute-done.rest_8_.halo_gate_ref) | copy-start | bytes 393220
  294.7 30.9 %all-to-all-start.2 = ((f32[32,8,8,128]{3,2,1,0:T(8,128)}), f32[32,8,8,128]{3,2,1,0:T(8,128)}, u32[]{:S(2)}, u32[]{:S(2)}) async-start(f32[32,8,8,128]{3,2,1,0:T(8,128)} %get-tuple-element.11), calls=%async_computation.2 | async-start | bytes 2097152 | tf_op jit(solution)/shard_map/all_to_all | solution.py:636

commit v7 on v6

--- a/solution.py
+++ b/solution.py
@@ -574,7 +574,7 @@
     devices = conv.shape[0]
     frames, width = gate_input.shape
     reach = TAPS + 1
-    block = 512
+    block = 1024
     per_block = block // 128
     edge = late.shape[1] - 1
     first = before is not None
@@ -660,7 +660,7 @@
     fixed = fixed_operands(tap_weight, norm_gain, up_weight, up_bias, down_weight)
     window = frames_here * groups
     if owned == 8 and channels_here == 128 and pair == HEADS and window == 256 * LANES:
-        if gate_input.shape[0] % 512 == 0 and gate_input.shape[0] >= 2048:
+        if gate_input.shape[0] % 1024 == 0 and gate_input.shape[0] >= 2048:
             return owned_eight(signal, kernel, skip_here, gate_input, fixed)
 
     def enter(array):

time: 338 us -> 338 us (level)
  transfers between devices with their start and end apart: 3 -> 3, of which waited for: 1 -> 2; matrix products, arithmetic and copies ran while one was open for 1% -> 1% of each run, Pallas kernels for 15% -> 15%
where the time goes in v7:
time: 338 us; the launch traced here: 335 us
  blocking collectives  225 us (67%)
  Pallas kernels  78.3 us (23%)
  starting transfers between devices  16.6 us (5%)
  waiting for transfers between devices  12.9 us (4%)
    all_to_all x1, blocking collectives, enter(): return lax.all_to_all(array, 'tm', split_axis=0, concat_axis=0, tiled=True)  143 us
    all_to_all x1, blocking collectives, leave(): lax.all_to_all(array, ('tm', 'chan'), split_axis=0, concat_axis=0, tiled=...  81.6 us
    pallas_call x2, Pallas kernels, tail_part(): pl.pallas_call(early_kernel if first else late_kernel, grid=(count,), in_...  33.6 us
    pallas_call x1, Pallas kernels, filter_channels(): pl.pallas_call(first_channels_kernel, in_specs=in_specs, out_specs=pl.Blo...  26.3 us
    pallas_call x1, Pallas kernels, filter_channels(): pl.pallas_call(functools.partial(last_channels_kernel, late, len(ready)),...  11.8 us
    all_to_all x1, waiting for transfers between devices, enter(): return lax.all_to_all(array, 'tm', split_axis=0, concat_axis=0, tiled=True)  11.2 us
  transfers between devices with their start and end apart: 3, of which 2 were waited for; matrix products, arithmetic and copies ran while one was open for 1% of the time, Pallas kernels for 15%

profile of v7, /device:TPU:11, one launch (start us, length us, event | category | flops | bytes accessed | tf_op | source)
XLA Modules:
  0.0 335.3 jit_solution(4180801009853801216)
XLA Ops:
  0.0 6.7 %turn.1 = (f32[16,6,16,8,128]{4,3,2,1,0:T(8,128)}, f32[16,2,16,8,128]{4,3,2,1,0:T(8,128)}) custom-call(f32[8192,128]{1,0:T(8,128)} %signal_ref.1, f32[8192,128]{1,0:T(8,128)} %kernel_ref.1), custom_call_target="tpu_custom_call" | custom-call | tf_op jit(solution)/shard_map/turn/pallas_call | solution.py:371
  6.7 143.0 %all_to_all.20 = f32[16,6,16,8,128]{4,3,2,1,0:T(8,128)} all-to-all(f32[16,6,16,8,128]{4,3,2,1,0:T(8,128)} %get-tuple-element.10), channel_id=1, replica_groups=mesh['grp'=1,'tm'=16,'chan'=2] {'tm'}, dimensions={0} | all-to-all | bytes 12582912 | tf_op jit(solution)/shard_map/all_to_all | solution.py:633
  149.7 0.0 copy-start
  149.7 0.0 copy-start.2
  149.7 5.7 %all-to-all-start = ((f32[16,2,16,8,128]{4,3,2,1,0:T(8,128)}), f32[16,2,16,8,128]{4,3,2,1,0:T(8,128)}, u32[]{:S(2)}, u32[]{:S(2)}) async-start(f32[16,2,16,8,128]{4,3,2,1,0:T(8,128)} %get-tuple-element.9), calls=%async_computation | async-start | bytes 4194304 | tf_op jit(solution)/shard_map/all_to_all | solution.py:633
  155.4 0.9 slice.3
  156.3 5.4 %collective-permute-start = (f32[128,256]{1,0:T(8,128)S(1)}, f32[128,256]{1,0:T(8,128)S(1)}, u32[]{:S(2)}, u32[]{:S(2)}) collective-permute-start(f32[128,256]{1,0:T(8,128)S(1)} %slice.3), channel_id=1, source_target_pairs={{0,1},{1,2},{2,3},{3,4},{4,5},{5,6},{6,7},{7,8},{8,9},{9,10},{10,1... | collective-permute-start | bytes 393224 | tf_op jit(solution)/shard_map/ppermute | solution.py:639
  161.7 0.0 copy-done
  161.7 0.2 reshape.28
  161.9 0.2 copy.19
  162.1 0.2 rev.3
  162.3 0.8 copy.20.rest_7_.rest_0_
  163.2 0.0 copy-done.2
  163.2 0.6 dynamic_slice.3.skip_ref
  163.8 26.3 %filter_first.1 = f32[8192,128]{1,0:T(8,128)} custom-call(f32[8]{0:T(128)} %dynamic_slice.3.skip_ref, f32[16,6,128,128]{3,2,1,0:T(8,128)} %bitcast.6, bf16[512,512]{1,0:T(8,128)(2,1)} %constant.30.clone.rest_0_, f32[256,512]{1,0:T(8,128)} %constant.31.clone.rest_1_, f32[256,512]{1,0:T(8,128)} %constant.32.clone.rest_2_, ...), custom_call_target="tpu_custom_call" | custom-call | flops 14495514624 | bytes 9437184 | tf_op jit(solution)/shard_map/filter_first/pallas_call | solution.py:493
  190.1 0.0 collective-permute-done.rest_8_.halo_gate_ref
  190.1 0.0 copy-start.1
  190.1 11.2 %all-to-all-done = f32[16,2,16,8,128]{4,3,2,1,0:T(8,128)} async-done(((f32[16,2,16,8,128]{4,3,2,1,0:T(8,128)}), f32[16,2,16,8,128]{4,3,2,1,0:T(8,128)}, u32[]{:S(2)}, u32[]{:S(2)}) %all-to-all-start) | async-done | bytes 2097184 | tf_op jit(solution)/shard_map/all_to_all | solution.py:633
  201.3 0.0 copy-done.1
  201.3 11.8 %filter_last.1 = (f32[32,25,8,128]{3,2,1,0:T(8,128)}, f32[32,8,8,128]{3,2,1,0:T(8,128)}) custom-call(f32[8]{0:T(128)} %dynamic_slice.3.skip_ref, f32[16,2,128,128]{3,2,1,0:T(8,128)} %bitcast.data_ref, bf16[512,512]{1,0:T(8,128)(2,1)} %constant.30.clone.rest_0_, f32[256,512]{1,0:T(8,128)} %constant.31.clone.rest_1_, f32[256,512]{1,0:T(8,128)} %constant.32.clone.rest_2_, ...), custom_call_target="tpu_custom_call" | custom-call | flops 4831838208 | bytes 3145728 | tf_op jit(solution)/shard_map/filter_last/pallas_call | solution.py:502
  213.1 81.6 %all_to_all.21.conv_ref.edge_ref = f32[32,25,8,128]{3,2,1,0:T(8,128)} all-to-all(f32[32,25,8,128]{3,2,1,0:T(8,128)} %get-tuple-element.12), channel_id=1, replica_groups=mesh['grp'=1,'tm'=16,'chan'=2] {'tm','chan'}, dimensions={0} | all-to-all | bytes 6553600 | tf_op jit(solution)/shard_map/all_to_all | solution.py:636
  294.7 5.5 %all-to-all-start.2 = ((f32[32,8,8,128]{3,2,1,0:T(8,128)}), f32[32,8,8,128]{3,2,1,0:T(8,128)}, u32[]{:S(2)}, u32[]{:S(2)}) async-start(f32[32,8,8,128]{3,2,1,0:T(8,128)} %get-tuple-element.11), calls=%async_computation.2 | async-start | bytes 2097152 | tf_op jit(solution)/shard_map/all_to_all | solution.py:636
  300.2 23.8 %mix_late.1.rest_5_ = f32[4096,256]{1,0:T(8,128)} custom-call(f32[32,25,8,128]{3,2,1,0:T(8,128)} %all_to_all.21.conv_ref.edge_ref, f32[32,25,8,128]{3,2,1,0:T(8,128)} %all_to_all.21.conv_ref.edge_ref, f32[4096,256]{1,0:T(8,128)} %gate_ref.3, f32[4096,256]{1,0:T(8,128)} %gate_ref.3, f32[256,256]{1,0:T(8,128)} %copy.20.rest_7_.rest_0_, f32[1,256]{1,0:T(1,128)} %bitcast.10, ...), custom_call_target="tpu_custom_call" | custom-call | flops 13287555072 | bytes 9437184 | tf_op jit(solution)/shard_map/mix_late/pallas_call | solution.py:608
  323.9 1.6 all-to-all-done.2.conv_ref.halo_ref
  325.5 9.8 %mix_early.1 = f32[4096,256]{1,0:T(8,128)} custom-call(f32[32,8,8,128]{3,2,1,0:T(8,128)} %all-to-all-done.2.conv_ref.halo_ref, f32[32,25,8,128]{3,2,1,0:T(8,128)} %all_to_all.21.conv_ref.edge_ref, f32[4096,256]{1,0:T(8,128)} %gate_ref.3, f32[32,8,8,128]{3,2,1,0:T(8,128)} %all-to-all-done.2.conv_ref.halo_ref, ...), custom_call_target="tpu_custom_call", output_to_operand_aliasing={{}: (10, {})} | custom-call | flops 4429185024 | bytes 3145728 | tf_op jit(solution)/shard_map/mix_early/pallas_call | solution.py:608
  (1 shorter events, 0.0 us)
Async XLA Ops:
  149.7 12.0 %copy-start = (f32[256,254]{1,0:T(8,128)S(1)}, f32[256,254]{1,0:T(8,128)}, u32[]{:S(2)}) copy-start(f32[256,254]{1,0:T(8,128)} %param.19) | copy-start | bytes 780292
  149.7 13.4 %copy-start.2 = (f32[256]{0:T(256)S(1)}, f32[256]{0:T(256)}, u32[]{:S(2)}) copy-start(f32[256]{0:T(256)} %param.17) | copy-start | bytes 3076
  149.7 51.6 %all-to-all-start = ((f32[16,2,16,8,128]{4,3,2,1,0:T(8,128)}), f32[16,2,16,8,128]{4,3,2,1,0:T(8,128)}, u32[]{:S(2)}, u32[]{:S(2)}) async-start(f32[16,2,16,8,128]{4,3,2,1,0:T(8,128)} %get-tuple-element.9), calls=%async_computation | async-start | bytes 4194304 | tf_op jit(solution)/shard_map/all_to_all | solution.py:633
  156.3 33.8 %collective-permute-start = (f32[128,256]{1,0:T(8,128)S(1)}, f32[128,256]{1,0:T(8,128)S(1)}, u32[]{:S(2)}, u32[]{:S(2)}) collective-permute-start(f32[128,256]{1,0:T(8,128)S(1)} %slice.3), channel_id=1, source_target_pairs={{0,1},{1,2},{2,3},{3,4},{4,5},{5,6},{6,7},{7,8},{8,9},{9,10},{10,1... | collective-permute-start | bytes 393224 | tf_op jit(solution)/shard_map/ppermute | solution.py:639
  190.1 11.2 %copy-start.1 = (f32[128,256]{1,0:T(8,128)}, f32[128,256]{1,0:T(8,128)S(1)}, u32[]{:S(2)}) copy-start(f32[128,256]{1,0:T(8,128)S(1)} %collective-permute-done.rest_8_.halo_gate_ref) | copy-start | bytes 393220
  294.7 30.9 %all-to-all-start.2 = ((f32[32,8,8,128]{3,2,1,0:T(8,128)}), f32[32,8,8,128]{3,2,1,0:T(8,128)}, u32[]{:S(2)}, u32[]{:S(2)}) async-start(f32[32,8,8,128]{3,2,1,0:T(8,128)} %get-tuple-element.11), calls=%async_computation.2 | async-start | bytes 2097152 | tf_op jit(solution)/shard_map/all_to_all | solution.py:636

commit v8 on v7

--- a/solution.py
+++ b/solution.py
@@ -318,8 +318,8 @@
 TURN_ROWS = 8
 
 
-def turn_kernel(signal_ref, kernel_ref, first_ref, second_ref, held_ref, sems):
-    groups, early = first_ref.shape[:2]
+def turn_kernel(low, signal_ref, kernel_ref, out_ref, held_ref, sems):
+    groups, channels = out_ref.shape[:2]
     rows = signal_ref.shape[0] // LANES
     step, steps = pl.program_id(0), pl.num_programs(0)
     slot = step % 2
@@ -329,10 +329,7 @@
         there = pl.ds(at * rows, rows)
         return (
             pltpu.make_async_copy(
-                shaped.at[:, :early, :rows], first_ref.at[:, :, there], sems.at[slot, 0]
-            ),
-            pltpu.make_async_copy(
-                shaped.at[:, early:, :rows], second_ref.at[:, :, there], sems.at[slot, 1]
+                shaped.at[:, low : low + channels, :rows], out_ref.at[:, :, there], sems.at[slot]
             ),
         )
 
@@ -362,24 +359,25 @@
             copy.wait()
 
 
-def turn(signal, kernel, groups):
+def turn(signal, kernel, groups, low, high):
     frames, width = signal.shape
     chunk = TURN_ROWS * LANES
-    rows = frames // LANES
     block = pl.BlockSpec((chunk, width), lambda i: (i, 0))
-    counts = (FIRST_CHANNELS, 8 - FIRST_CHANNELS)
     return pl.pallas_call(
-        turn_kernel,
+        functools.partial(turn_kernel, low),
         grid=(frames // chunk,),
         in_specs=[block, block],
-        out_specs=[pl.BlockSpec(memory_space=pl.ANY)] * 2,
-        out_shape=[jax.ShapeDtypeStruct((groups, n, rows, 8, 128), F32) for n in counts],
+        out_specs=pl.BlockSpec(memory_space=pl.ANY),
+        out_shape=jax.ShapeDtypeStruct((groups, high - low, frames // LANES, 8, 128), F32),
         scratch_shapes=[
             pltpu.VMEM((2, width * (TURN_ROWS + 1) * 8, 128), F32),
-            pltpu.SemaphoreType.DMA((2, 2)),
+            pltpu.SemaphoreType.DMA((2,)),
         ],
         compiler_params=pltpu.CompilerParams(vmem_limit_bytes=VMEM_LIMIT),
-        name="turn",
+        cost_estimate=pl.CostEstimate(
+            flops=0, bytes_accessed=frames * width * 12, transcendentals=0
+        ),
+        name="turn_first" if low == 0 else "turn_rest",
     )(signal, kernel)
 
 
@@ -637,7 +635,8 @@
 
     ring = [(i, i + 1) for i in range(devices - 1)]
     halo_gate = lax.ppermute(gate_input[-reach:], ("tm", "chan"), ring)
-    one, two = turn(signal, kernel, groups)
+    one = turn(signal, kernel, groups, 0, FIRST_CHANNELS)
+    two = turn(signal, kernel, groups, FIRST_CHANNELS, 8)
     before = filter_channels(enter(one), skip_here, None, devices, late_tiles)
     ready = (fixed[0], halo_gate)
     late, early = filter_channels(enter(two), skip_here, before, devices, late_tiles, ready)

time: 338 us -> 342 us (1.012)
  blocking collectives: 225 us -> 81.5 us
  waiting for transfers between devices: 12.9 us -> 147 us
  starting transfers between devices: 16.6 us -> 24.9 us
  Pallas kernels: 78.3 us -> 83.7 us
    all_to_all x1 -> x0, blocking collectives: 143 us -> none  [enter(): return lax.all_to_all(array, 'tm', split_axis=0, concat_axis=0, tiled=True)]
    all_to_all x1 -> x2, waiting for transfers between devices: 11.2 us -> 145 us  [enter(): return lax.all_to_all(array, 'tm', split_axis=0, concat_axis=0, tiled=True)]
    all_to_all x1 -> x2, starting transfers between devices: 5.69 us -> 14 us  [enter(): return lax.all_to_all(array, 'tm', split_axis=0, concat_axis=0, tiled=True)]
    pallas_call x1 -> x2, Pallas kernels: 6.66 us -> 12 us  [turn(): pl.pallas_call(functools.partial(turn_kernel, low), grid=(frames // chunk...]
  transfers between devices with their start and end apart: 3 -> 4, of which waited for: 2 -> 3; matrix products, arithmetic and copies ran while one was open for 1% -> 1% of each run, Pallas kernels for 15% -> 16%
where the time goes in v8:
time: 342 us; the launch traced here: 340 us
  waiting for transfers between devices  147 us (43%)
  Pallas kernels  83.7 us (24%)
  blocking collectives  81.5 us (24%)
  starting transfers between devices  24.9 us (7%)
    all_to_all x2, waiting for transfers between devices, enter(): return lax.all_to_all(array, 'tm', split_axis=0, concat_axis=0, tiled=True)  145 us
    all_to_all x1, blocking collectives, leave(): lax.all_to_all(array, ('tm', 'chan'), split_axis=0, concat_axis=0, tiled=...  81.5 us
    pallas_call x2, Pallas kernels, tail_part(): pl.pallas_call(early_kernel if first else late_kernel, grid=(count,), in_...  33.6 us
    pallas_call x1, Pallas kernels, filter_channels(): pl.pallas_call(first_channels_kernel, in_specs=in_specs, out_specs=pl.Blo...  26.3 us
    all_to_all x2, starting transfers between devices, enter(): return lax.all_to_all(array, 'tm', split_axis=0, concat_axis=0, tiled=True)  14 us
    pallas_call x2, Pallas kernels, turn(): pl.pallas_call(functools.partial(turn_kernel, low), grid=(frames // chunk...  12 us
    pallas_call x1, Pallas kernels, filter_channels(): pl.pallas_call(functools.partial(last_channels_kernel, late, len(ready)),...  11.8 us
  transfers between devices with their start and end apart: 4, of which 3 were waited for; matrix products, arithmetic and copies ran while one was open for 1% of the time, Pallas kernels for 16%

profile of v8, /device:TPU:11, one launch (start us, length us, event | category | flops | bytes accessed | tf_op | source)
XLA Modules:
  0.0 340.0 jit_solution(11403664772307803056)
XLA Ops:
  0.0 6.4 %turn_first.1 = f32[16,6,16,8,128]{4,3,2,1,0:T(8,128)} custom-call(f32[8192,128]{1,0:T(8,128)} %signal_ref.3, f32[8192,128]{1,0:T(8,128)} %kernel_ref.3), custom_call_target="tpu_custom_call" | custom-call | bytes 12582912 | tf_op jit(solution)/shard_map/turn_first/pallas_call | solution.py:366
  6.4 6.6 %all-to-all-start.1 = ((f32[16,6,16,8,128]{4,3,2,1,0:T(8,128)}), f32[16,6,16,8,128]{4,3,2,1,0:T(8,128)}, u32[]{:S(2)}, u32[]{:S(2)}) async-start(f32[16,6,16,8,128]{4,3,2,1,0:T(8,128)} %turn_first.1), calls=%async_computation.1 | async-start | bytes 12582912 | tf_op jit(solution)/shard_map/all_to_all | solution.py:631
  13.0 5.6 %turn_rest.1 = f32[16,2,16,8,128]{4,3,2,1,0:T(8,128)} custom-call(f32[8192,128]{1,0:T(8,128)} %signal_ref.3, f32[8192,128]{1,0:T(8,128)} %kernel_ref.3), custom_call_target="tpu_custom_call" | custom-call | bytes 12582912 | tf_op jit(solution)/shard_map/turn_rest/pallas_call | solution.py:366
  18.7 0.0 copy-start
  18.7 0.0 copy-start.2
  18.7 134.0 %all-to-all-done.1 = f32[16,6,16,8,128]{4,3,2,1,0:T(8,128)} async-done(((f32[16,6,16,8,128]{4,3,2,1,0:T(8,128)}), f32[16,6,16,8,128]{4,3,2,1,0:T(8,128)}, u32[]{:S(2)}, u32[]{:S(2)}) %all-to-all-start.1) | async-done | bytes 6291488 | tf_op jit(solution)/shard_map/all_to_all | solution.py:631
  152.7 7.4 %all-to-all-start = ((f32[16,2,16,8,128]{4,3,2,1,0:T(8,128)}), f32[16,2,16,8,128]{4,3,2,1,0:T(8,128)}, u32[]{:S(2)}, u32[]{:S(2)}) async-start(f32[16,2,16,8,128]{4,3,2,1,0:T(8,128)} %turn_rest.1), calls=%async_computation | async-start | bytes 4194304 | tf_op jit(solution)/shard_map/all_to_all | solution.py:631
  160.1 0.9 slice.3
  161.0 5.4 %collective-permute-start = (f32[128,256]{1,0:T(8,128)S(1)}, f32[128,256]{1,0:T(8,128)S(1)}, u32[]{:S(2)}, u32[]{:S(2)}) collective-permute-start(f32[128,256]{1,0:T(8,128)S(1)} %slice.3), channel_id=1, source_target_pairs={{0,1},{1,2},{2,3},{3,4},{4,5},{5,6},{6,7},{7,8},{8,9},{9,10},{10,1... | collective-permute-start | bytes 393224 | tf_op jit(solution)/shard_map/ppermute | solution.py:637
  166.4 0.0 copy-done
  166.4 0.2 reshape.28
  166.6 0.2 copy.19
  166.8 0.2 rev.3
  167.0 0.8 copy.20.rest_7_.rest_0_
  167.9 0.0 copy-done.2
  167.9 0.7 dynamic_slice.3.skip_ref
  168.5 26.3 %filter_first.1 = f32[8192,128]{1,0:T(8,128)} custom-call(f32[8]{0:T(128)} %dynamic_slice.3.skip_ref, f32[16,6,128,128]{3,2,1,0:T(8,128)} %bitcast.1.data_ref, bf16[512,512]{1,0:T(8,128)(2,1)} %constant.30.clone.rest_0_, f32[256,512]{1,0:T(8,128)} %constant.31.clone.rest_1_, f32[256,512]{1,0:T(8,128)} %constant.32.clone.rest_2_, ...), custom_call_target="tpu_custom_call" | custom-call | flops 14495514624 | bytes 9437184 | tf_op jit(solution)/shard_map/filter_first/pallas_call | solution.py:491
  194.8 0.0 collective-permute-done.rest_8_.halo_gate_ref
  194.8 0.0 copy-start.1
  194.9 11.2 %all-to-all-done = f32[16,2,16,8,128]{4,3,2,1,0:T(8,128)} async-done(((f32[16,2,16,8,128]{4,3,2,1,0:T(8,128)}), f32[16,2,16,8,128]{4,3,2,1,0:T(8,128)}, u32[]{:S(2)}, u32[]{:S(2)}) %all-to-all-start) | async-done | bytes 2097184 | tf_op jit(solution)/shard_map/all_to_all | solution.py:631
  206.0 0.0 copy-done.1
  206.0 11.8 %filter_last.1 = (f32[32,25,8,128]{3,2,1,0:T(8,128)}, f32[32,8,8,128]{3,2,1,0:T(8,128)}) custom-call(f32[8]{0:T(128)} %dynamic_slice.3.skip_ref, f32[16,2,128,128]{3,2,1,0:T(8,128)} %bitcast.data_ref, bf16[512,512]{1,0:T(8,128)(2,1)} %constant.30.clone.rest_0_, f32[256,512]{1,0:T(8,128)} %constant.31.clone.rest_1_, f32[256,512]{1,0:T(8,128)} %constant.32.clone.rest_2_, ...), custom_call_target="tpu_custom_call" | custom-call | flops 4831838208 | bytes 3145728 | tf_op jit(solution)/shard_map/filter_last/pallas_call | solution.py:500
  217.8 81.5 %all_to_all.20.conv_ref.edge_ref = f32[32,25,8,128]{3,2,1,0:T(8,128)} all-to-all(f32[32,25,8,128]{3,2,1,0:T(8,128)} %get-tuple-element.8), channel_id=1, replica_groups=mesh['grp'=1,'tm'=16,'chan'=2] {'tm','chan'}, dimensions={0} | all-to-all | bytes 6553600 | tf_op jit(solution)/shard_map/all_to_all | solution.py:634
  299.3 5.5 %all-to-all-start.2 = ((f32[32,8,8,128]{3,2,1,0:T(8,128)}), f32[32,8,8,128]{3,2,1,0:T(8,128)}, u32[]{:S(2)}, u32[]{:S(2)}) async-start(f32[32,8,8,128]{3,2,1,0:T(8,128)} %get-tuple-element.7), calls=%async_computation.2 | async-start | bytes 2097152 | tf_op jit(solution)/shard_map/all_to_all | solution.py:634
  304.8 23.8 %mix_late.1.rest_5_ = f32[4096,256]{1,0:T(8,128)} custom-call(f32[32,25,8,128]{3,2,1,0:T(8,128)} %all_to_all.20.conv_ref.edge_ref, f32[32,25,8,128]{3,2,1,0:T(8,128)} %all_to_all.20.conv_ref.edge_ref, f32[4096,256]{1,0:T(8,128)} %gate_ref.3, f32[4096,256]{1,0:T(8,128)} %gate_ref.3, f32[256,256]{1,0:T(8,128)} %copy.20.rest_7_.rest_0_, f32[1,256]{1,0:T(1,128)} %bitcast.9, ...), custom_call_target="tpu_custom_call" | custom-call | flops 13287555072 | bytes 9437184 | tf_op jit(solution)/shard_map/mix_late/pallas_call | solution.py:606
  328.6 1.6 all-to-all-done.2.conv_ref.halo_ref
  330.2 9.8 %mix_early.1 = f32[4096,256]{1,0:T(8,128)} custom-call(f32[32,8,8,128]{3,2,1,0:T(8,128)} %all-to-all-done.2.conv_ref.halo_ref, f32[32,25,8,128]{3,2,1,0:T(8,128)} %all_to_all.20.conv_ref.edge_ref, f32[4096,256]{1,0:T(8,128)} %gate_ref.3, f32[32,8,8,128]{3,2,1,0:T(8,128)} %all-to-all-done.2.conv_ref.halo_ref, ...), custom_call_target="tpu_custom_call", output_to_operand_aliasing={{}: (10, {})} | custom-call | flops 4429185024 | bytes 3145728 | tf_op jit(solution)/shard_map/mix_early/pallas_call | solution.py:606
  (1 shorter events, 0.0 us)
Async XLA Ops:
  6.4 146.3 %all-to-all-start.1 = ((f32[16,6,16,8,128]{4,3,2,1,0:T(8,128)}), f32[16,6,16,8,128]{4,3,2,1,0:T(8,128)}, u32[]{:S(2)}, u32[]{:S(2)}) async-start(f32[16,6,16,8,128]{4,3,2,1,0:T(8,128)} %turn_first.1), calls=%async_computation.1 | async-start | bytes 12582912 | tf_op jit(solution)/shard_map/all_to_all | solution.py:631
  18.7 147.7 %copy-start = (f32[256,254]{1,0:T(8,128)S(1)}, f32[256,254]{1,0:T(8,128)}, u32[]{:S(2)}) copy-start(f32[256,254]{1,0:T(8,128)} %param.19) | copy-start | bytes 780292
  18.7 149.2 %copy-start.2 = (f32[256]{0:T(256)S(1)}, f32[256]{0:T(256)}, u32[]{:S(2)}) copy-start(f32[256]{0:T(256)} %param.17) | copy-start | bytes 3076
  152.7 53.3 %all-to-all-start = ((f32[16,2,16,8,128]{4,3,2,1,0:T(8,128)}), f32[16,2,16,8,128]{4,3,2,1,0:T(8,128)}, u32[]{:S(2)}, u32[]{:S(2)}) async-start(f32[16,2,16,8,128]{4,3,2,1,0:T(8,128)} %turn_rest.1), calls=%async_computation | async-start | bytes 4194304 | tf_op jit(solution)/shard_map/all_to_all | solution.py:631
  161.0 33.9 %collective-permute-start = (f32[128,256]{1,0:T(8,128)S(1)}, f32[128,256]{1,0:T(8,128)S(1)}, u32[]{:S(2)}, u32[]{:S(2)}) collective-permute-start(f32[128,256]{1,0:T(8,128)S(1)} %slice.3), channel_id=1, source_target_pairs={{0,1},{1,2},{2,3},{3,4},{4,5},{5,6},{6,7},{7,8},{8,9},{9,10},{10,1... | collective-permute-start | bytes 393224 | tf_op jit(solution)/shard_map/ppermute | solution.py:637
  194.8 11.2 %copy-start.1 = (f32[128,256]{1,0:T(8,128)}, f32[128,256]{1,0:T(8,128)S(1)}, u32[]{:S(2)}) copy-start(f32[128,256]{1,0:T(8,128)S(1)} %collective-permute-done.rest_8_.halo_gate_ref) | copy-start | bytes 393220
  299.3 30.9 %all-to-all-start.2 = ((f32[32,8,8,128]{3,2,1,0:T(8,128)}), f32[32,8,8,128]{3,2,1,0:T(8,128)}, u32[]{:S(2)}, u32[]{:S(2)}) async-start(f32[32,8,8,128]{3,2,1,0:T(8,128)} %get-tuple-element.7), calls=%async_computation.2 | async-start | bytes 2097152 | tf_op jit(solution)/shard_map/all_to_all | solution.py:634

commit v9 on v7

--- a/solution.py
+++ b/solution.py
@@ -231,7 +231,7 @@
 
 def mix_scratch(block, width, hidden):
     reach = TAPS + 1
-    chunk = 256 if hidden % 256 == 0 else hidden
+    chunk = 512 if hidden % 512 == 0 else hidden
     return [
         pltpu.VMEM((block + reach, width), F32),
         pltpu.VMEM((block + reach, width), BF16),

time: 338 us -> 338 us (level)
  no operation moved by 1% of the time
where the time goes in v9:
time: 338 us; the launch traced here: 335 us
  blocking collectives  225 us (67%)
  Pallas kernels  78.1 us (23%)
  starting transfers between devices  16.6 us (5%)
  waiting for transfers between devices  13 us (4%)
    all_to_all x1, blocking collectives, enter(): return lax.all_to_all(array, 'tm', split_axis=0, concat_axis=0, tiled=True)  143 us
    all_to_all x1, blocking collectives, leave(): lax.all_to_all(array, ('tm', 'chan'), split_axis=0, concat_axis=0, tiled=...  81.6 us
    pallas_call x2, Pallas kernels, tail_part(): pl.pallas_call(early_kernel if first else late_kernel, grid=(count,), in_...  33.4 us
    pallas_call x1, Pallas kernels, filter_channels(): pl.pallas_call(first_channels_kernel, in_specs=in_specs, out_specs=pl.Blo...  26.3 us
    pallas_call x1, Pallas kernels, filter_channels(): pl.pallas_call(functools.partial(last_channels_kernel, late, len(ready)),...  11.8 us
    all_to_all x1, waiting for transfers between devices, enter(): return lax.all_to_all(array, 'tm', split_axis=0, concat_axis=0, tiled=True)  11.2 us
  transfers between devices with their start and end apart: 3, of which 2 were waited for; matrix products, arithmetic and copies ran while one was open for 1% of the time, Pallas kernels for 15%

profile of v9, /device:TPU:11, one launch (start us, length us, event | category | flops | bytes accessed | tf_op | source)
XLA Modules:
  0.0 335.3 jit_solution(2101050904692210)
XLA Ops:
  0.0 6.7 %turn.1 = (f32[16,6,16,8,128]{4,3,2,1,0:T(8,128)}, f32[16,2,16,8,128]{4,3,2,1,0:T(8,128)}) custom-call(f32[8192,128]{1,0:T(8,128)} %signal_ref.1, f32[8192,128]{1,0:T(8,128)} %kernel_ref.1), custom_call_target="tpu_custom_call" | custom-call | tf_op jit(solution)/shard_map/turn/pallas_call | solution.py:371
  6.7 143.0 %all_to_all.20 = f32[16,6,16,8,128]{4,3,2,1,0:T(8,128)} all-to-all(f32[16,6,16,8,128]{4,3,2,1,0:T(8,128)} %get-tuple-element.10), channel_id=1, replica_groups=mesh['grp'=1,'tm'=16,'chan'=2] {'tm'}, dimensions={0} | all-to-all | bytes 12582912 | tf_op jit(solution)/shard_map/all_to_all | solution.py:633
  149.7 0.0 copy-start
  149.7 0.0 copy-start.2
  149.7 5.7 %all-to-all-start = ((f32[16,2,16,8,128]{4,3,2,1,0:T(8,128)}), f32[16,2,16,8,128]{4,3,2,1,0:T(8,128)}, u32[]{:S(2)}, u32[]{:S(2)}) async-start(f32[16,2,16,8,128]{4,3,2,1,0:T(8,128)} %get-tuple-element.9), calls=%async_computation | async-start | bytes 4194304 | tf_op jit(solution)/shard_map/all_to_all | solution.py:633
  155.4 0.9 slice.3
  156.3 5.4 %collective-permute-start = (f32[128,256]{1,0:T(8,128)S(1)}, f32[128,256]{1,0:T(8,128)S(1)}, u32[]{:S(2)}, u32[]{:S(2)}) collective-permute-start(f32[128,256]{1,0:T(8,128)S(1)} %slice.3), channel_id=1, source_target_pairs={{0,1},{1,2},{2,3},{3,4},{4,5},{5,6},{6,7},{7,8},{8,9},{9,10},{10,1... | collective-permute-start | bytes 393224 | tf_op jit(solution)/shard_map/ppermute | solution.py:639
  161.7 0.0 copy-done
  161.7 0.2 reshape.28
  161.9 0.2 copy.19
  162.1 0.2 rev.3
  162.3 0.8 copy.20.rest_7_.rest_0_
  163.2 0.0 copy-done.2
  163.2 0.6 dynamic_slice.3.skip_ref
  163.8 26.3 %filter_first.1 = f32[8192,128]{1,0:T(8,128)} custom-call(f32[8]{0:T(128)} %dynamic_slice.3.skip_ref, f32[16,6,128,128]{3,2,1,0:T(8,128)} %bitcast.6, bf16[512,512]{1,0:T(8,128)(2,1)} %constant.30.clone.rest_0_, f32[256,512]{1,0:T(8,128)} %constant.31.clone.rest_1_, f32[256,512]{1,0:T(8,128)} %constant.32.clone.rest_2_, ...), custom_call_target="tpu_custom_call" | custom-call | flops 14495514624 | bytes 9437184 | tf_op jit(solution)/shard_map/filter_first/pallas_call | solution.py:493
  190.1 0.0 collective-permute-done.rest_8_.halo_gate_ref
  190.1 0.0 copy-start.1
  190.1 11.2 %all-to-all-done = f32[16,2,16,8,128]{4,3,2,1,0:T(8,128)} async-done(((f32[16,2,16,8,128]{4,3,2,1,0:T(8,128)}), f32[16,2,16,8,128]{4,3,2,1,0:T(8,128)}, u32[]{:S(2)}, u32[]{:S(2)}) %all-to-all-start) | async-done | bytes 2097184 | tf_op jit(solution)/shard_map/all_to_all | solution.py:633
  201.3 0.0 copy-done.1
  201.3 11.8 %filter_last.1 = (f32[32,25,8,128]{3,2,1,0:T(8,128)}, f32[32,8,8,128]{3,2,1,0:T(8,128)}) custom-call(f32[8]{0:T(128)} %dynamic_slice.3.skip_ref, f32[16,2,128,128]{3,2,1,0:T(8,128)} %bitcast.data_ref, bf16[512,512]{1,0:T(8,128)(2,1)} %constant.30.clone.rest_0_, f32[256,512]{1,0:T(8,128)} %constant.31.clone.rest_1_, f32[256,512]{1,0:T(8,128)} %constant.32.clone.rest_2_, ...), custom_call_target="tpu_custom_call" | custom-call | flops 4831838208 | bytes 3145728 | tf_op jit(solution)/shard_map/filter_last/pallas_call | solution.py:502
  213.1 81.6 %all_to_all.21.conv_ref.edge_ref = f32[32,25,8,128]{3,2,1,0:T(8,128)} all-to-all(f32[32,25,8,128]{3,2,1,0:T(8,128)} %get-tuple-element.12), channel_id=1, replica_groups=mesh['grp'=1,'tm'=16,'chan'=2] {'tm','chan'}, dimensions={0} | all-to-all | bytes 6553600 | tf_op jit(solution)/shard_map/all_to_all | solution.py:636
  294.7 5.5 %all-to-all-start.2 = ((f32[32,8,8,128]{3,2,1,0:T(8,128)}), f32[32,8,8,128]{3,2,1,0:T(8,128)}, u32[]{:S(2)}, u32[]{:S(2)}) async-start(f32[32,8,8,128]{3,2,1,0:T(8,128)} %get-tuple-element.11), calls=%async_computation.2 | async-start | bytes 2097152 | tf_op jit(solution)/shard_map/all_to_all | solution.py:636
  300.2 23.6 %mix_late.1.rest_5_ = f32[4096,256]{1,0:T(8,128)} custom-call(f32[32,25,8,128]{3,2,1,0:T(8,128)} %all_to_all.21.conv_ref.edge_ref, f32[32,25,8,128]{3,2,1,0:T(8,128)} %all_to_all.21.conv_ref.edge_ref, f32[4096,256]{1,0:T(8,128)} %gate_ref.3, f32[4096,256]{1,0:T(8,128)} %gate_ref.3, f32[256,256]{1,0:T(8,128)} %copy.20.rest_7_.rest_0_, f32[1,256]{1,0:T(1,128)} %bitcast.10, ...), custom_call_target="tpu_custom_call" | custom-call | flops 13287555072 | bytes 9437184 | tf_op jit(solution)/shard_map/mix_late/pallas_call | solution.py:608
  323.8 1.8 all-to-all-done.2.conv_ref.halo_ref
  325.5 9.8 %mix_early.1 = f32[4096,256]{1,0:T(8,128)} custom-call(f32[32,8,8,128]{3,2,1,0:T(8,128)} %all-to-all-done.2.conv_ref.halo_ref, f32[32,25,8,128]{3,2,1,0:T(8,128)} %all_to_all.21.conv_ref.edge_ref, f32[4096,256]{1,0:T(8,128)} %gate_ref.3, f32[32,8,8,128]{3,2,1,0:T(8,128)} %all-to-all-done.2.conv_ref.halo_ref, ...), custom_call_target="tpu_custom_call", output_to_operand_aliasing={{}: (10, {})} | custom-call | flops 4429185024 | bytes 3145728 | tf_op jit(solution)/shard_map/mix_early/pallas_call | solution.py:608
  (1 shorter events, 0.0 us)
Async XLA Ops:
  149.7 12.0 %copy-start = (f32[256,254]{1,0:T(8,128)S(1)}, f32[256,254]{1,0:T(8,128)}, u32[]{:S(2)}) copy-start(f32[256,254]{1,0:T(8,128)} %param.19) | copy-start | bytes 780292
  149.7 13.4 %copy-start.2 = (f32[256]{0:T(256)S(1)}, f32[256]{0:T(256)}, u32[]{:S(2)}) copy-start(f32[256]{0:T(256)} %param.17) | copy-start | bytes 3076
  149.7 51.6 %all-to-all-start = ((f32[16,2,16,8,128]{4,3,2,1,0:T(8,128)}), f32[16,2,16,8,128]{4,3,2,1,0:T(8,128)}, u32[]{:S(2)}, u32[]{:S(2)}) async-start(f32[16,2,16,8,128]{4,3,2,1,0:T(8,128)} %get-tuple-element.9), calls=%async_computation | async-start | bytes 4194304 | tf_op jit(solution)/shard_map/all_to_all | solution.py:633
  156.3 33.8 %collective-permute-start = (f32[128,256]{1,0:T(8,128)S(1)}, f32[128,256]{1,0:T(8,128)S(1)}, u32[]{:S(2)}, u32[]{:S(2)}) collective-permute-start(f32[128,256]{1,0:T(8,128)S(1)} %slice.3), channel_id=1, source_target_pairs={{0,1},{1,2},{2,3},{3,4},{4,5},{5,6},{6,7},{7,8},{8,9},{9,10},{10,1... | collective-permute-start | bytes 393224 | tf_op jit(solution)/shard_map/ppermute | solution.py:639
  190.1 11.2 %copy-start.1 = (f32[128,256]{1,0:T(8,128)}, f32[128,256]{1,0:T(8,128)S(1)}, u32[]{:S(2)}) copy-start(f32[128,256]{1,0:T(8,128)S(1)} %collective-permute-done.rest_8_.halo_gate_ref) | copy-start | bytes 393220
  294.7 30.9 %all-to-all-start.2 = ((f32[32,8,8,128]{3,2,1,0:T(8,128)}), f32[32,8,8,128]{3,2,1,0:T(8,128)}, u32[]{:S(2)}, u32[]{:S(2)}) async-start(f32[32,8,8,128]{3,2,1,0:T(8,128)} %get-tuple-element.11), calls=%async_computation.2 | async-start | bytes 2097152 | tf_op jit(solution)/shard_map/all_to_all | solution.py:636
